TPU v7x, 32 devices: a whole 2x2x4 slice. The times are simulated.
32 devices in a mesh: wide: 8 (over z, x), narrow: 4 (over y, core).
Axes of the slice: x: 2, y: 2, z: 4, core: 2. Of those that a mesh axis runs over, the one named last changes fastest.
Arguments:
- layer_input: bfloat16 [8, 1024, 2048], P('wide', 'narrow'), may hold values from -6 to 6
- out_grad: bfloat16 [8, 1024, 2048], P('wide', 'narrow'), may hold values from -6 to 6
- lengths: int32 [8], P('wide'), may hold values from 769 to 1024, as said below
- query_weight: float32 [2048, 2048], P('wide', 'narrow'), may hold values from -0.125 to 0.125
- query_mean: float32 [2048, 2048], P('wide', 'narrow'), may hold values from -256 to 256
- query_square: float32 [2048, 2048], P('wide', 'narrow'), may hold values from 2048 to 8192
- keyval_weight: float32 [2, 2048, 1024], P(None, 'wide', 'narrow'), may hold values from -0.125 to 0.125
- keyval_mean: float32 [2, 2048, 1024], P(None, 'wide', 'narrow'), may hold values from -256 to 256
- keyval_square: float32 [2, 2048, 1024], P(None, 'wide', 'narrow'), may hold values from 2048 to 8192
- output_weight: float32 [2048, 2048], P('narrow', 'wide'), may hold values from -1 to 1
- output_mean: float32 [2048, 2048], P('narrow', 'wide'), may hold values from -56 to 56
- output_square: float32 [2048, 2048], P('narrow', 'wide'), may hold values from 81.92 to 327.68
- gateup_weight: float32 [2, 2048, 6144], P(None, 'wide', 'narrow'), may hold values from -0.125 to 0.125
- gateup_mean: float32 [2, 2048, 6144], P(None, 'wide', 'narrow'), may hold values from -160 to 160
- gateup_square: float32 [2, 2048, 6144], P(None, 'wide', 'narrow'), may hold values from 737.28 to 2949.12
- down_weight: float32 [6144, 2048], P('narrow', 'wide'), may hold values from -0.078125 to 0.078125
- down_mean: float32 [6144, 2048], P('narrow', 'wide'), may hold values from -256 to 256
- down_square: float32 [6144, 2048], P('narrow', 'wide'), may hold values from 2048 to 8192
- norm_gains: float32 [2, 2048], P(None, 'wide'), may hold values from 0.5 to 1.5
- norm_mean: float32 [2, 2048], P(None, 'wide'), may hold values from -512 to 512
- norm_square: float32 [2, 2048], P(None, 'wide'), may hold values from 8192 to 32768
- head_gains: float32 [2, 128], P(None, 'wide'), may hold values from 0.5 to 1.5
- head_mean: float32 [2, 128], P(None, 'wide'), may hold values from -2048 to 2048
- head_square: float32 [2, 128], P(None, 'wide'), may hold values from 131072 to 524288
Outputs:
- layer_out: bfloat16 [8, 1024, 2048], P('wide', 'narrow')
- input_grad: float32 [8, 1024, 2048], P('wide', 'narrow')
- query_new: float32 [2048, 2048], P('wide', 'narrow')
- query_first: float32 [2048, 2048], P('wide', 'narrow')
- query_second: float32 [2048, 2048], P('wide', 'narrow')
- keyval_new: float32 [2, 2048, 1024], P(None, 'wide', 'narrow')
- keyval_first: float32 [2, 2048, 1024], P(None, 'wide', 'narrow')
- keyval_second: float32 [2, 2048, 1024], P(None, 'wide', 'narrow')
- output_new: float32 [2048, 2048], P('narrow', 'wide')
- output_first: float32 [2048, 2048], P('narrow', 'wide')
- output_second: float32 [2048, 2048], P('narrow', 'wide')
- gateup_new: float32 [2, 2048, 6144], P(None, 'wide', 'narrow')
- gateup_first: float32 [2, 2048, 6144], P(None, 'wide', 'narrow')
- gateup_second: float32 [2, 2048, 6144], P(None, 'wide', 'narrow')
- down_new: float32 [6144, 2048], P('narrow', 'wide')
- down_first: float32 [6144, 2048], P('narrow', 'wide')
- down_second: float32 [6144, 2048], P('narrow', 'wide')
- norm_new: float32 [2, 2048], P(None, 'wide')
- norm_first: float32 [2, 2048], P(None, 'wide')
- norm_second: float32 [2, 2048], P(None, 'wide')
- head_new: float32 [2, 128], P(None, 'wide')
- head_first: float32 [2, 128], P(None, 'wide')
- head_second: float32 [2, 128], P(None, 'wide')
Inputs may be any that keep to these rules, and one draw needn't show every extreme that they name: `lengths`: each row's count of valid tokens from its start; one row has exactly 1024 and one exactly 769.
All inputs are finite; a program needn't handle non-finite values.
Results may differ from a plain program's by a relative error of at most 0.015.
The roundings to bfloat16 on the way count: a program that leaves them out, or rounds other values in their place, can miss the bound.
Values may be sent and summed in bfloat16 or wider, within the bound.
A program may use at most 256 MiB of HBM per device.

v0:
```python
import jax
import jax.numpy as jnp
from jax import lax
from jax.sharding import PartitionSpec as P

HD = 128
STEP = 5


norm_eps = 1e-06
rope_base = 1000000.0
beta_first = 0.5
beta_second = 0.5
adam_eps = 1e-08
weight_decay = 0.1
masked_fill = -1e30


def row_scale(values):
    return lax.rsqrt(jnp.mean(values * values, axis=-1, keepdims=True) + norm_eps)


def rope_tables(length):
    half = HD // 2
    freqs = rope_base ** (-(jnp.arange(half, dtype=jnp.float32) * 2.0) / HD)
    angles = jnp.arange(length, dtype=jnp.float32)[:, None] * freqs[None, :]
    cosine = jnp.cos(angles)
    sine = jnp.sin(angles)
    return (
        jnp.concatenate([cosine, cosine], axis=-1)[:, None, :],
        jnp.concatenate([sine, sine], axis=-1)[:, None, :],
    )


def rotate(values, cosine, sine):
    half = values.shape[-1] // 2
    turned = jnp.concatenate([-values[..., half:], values[..., :half]], axis=-1)
    return values * cosine + turned * sine


def rotate_back(grads, cosine, sine):
    half = grads.shape[-1] // 2
    moved = grads * sine
    turned = jnp.concatenate([moved[..., half:], -moved[..., :half]], axis=-1)
    return grads * cosine + turned


def norm_back(grad, unit, scale, gain):
    scaled = grad * gain
    return scale * (scaled - unit * jnp.mean(scaled * unit, axis=-1, keepdims=True))


def masked_scores(query_block, keys, lengths, start):
    block_rows = query_block.shape[1]
    length = keys.shape[1]
    scores = jnp.einsum(
        "sqkgd,stkd->skgqt", query_block, keys, preferred_element_type=jnp.float32
    ) * HD ** (-0.5)
    rows = start + jnp.arange(block_rows)
    columns = jnp.arange(length)
    allowed = (columns[None, None, :] <= rows[None, :, None]) & (
        columns[None, None, :] < lengths[:, None, None]
    )
    return jnp.where(allowed[:, None, None], scores, masked_fill)


def adamw(weight, first, second, grad, rate):
    first_new = beta_first * first + (1.0 - beta_first) * grad
    second_new = beta_second * second + (1.0 - beta_second) * grad * grad
    first_hat = first_new / (1.0 - beta_first**STEP)
    second_hat = second_new / (1.0 - beta_second**STEP)
    weight_new = weight - rate * (
        first_hat / (jnp.sqrt(second_hat) + adam_eps) + weight_decay * weight
    )
    return (weight_new, first_new, second_new)


def per_device(
    layer_input,
    out_grad,
    lengths,
    query_weight,
    query_mean,
    query_square,
    keyval_weight,
    keyval_mean,
    keyval_square,
    output_weight,
    output_mean,
    output_square,
    gateup_weight,
    gateup_mean,
    gateup_square,
    down_weight,
    down_mean,
    down_square,
    norm_gains,
    norm_mean,
    norm_square,
    head_gains,
    head_mean,
    head_square,
):
    narrow_count = lax.axis_size("narrow")
    narrow_rank = lax.axis_index("narrow")
    sequences = layer_input.shape[0]
    local_rows = layer_input.shape[1]
    length = local_rows * narrow_count
    block_rows = min(512, length)
    block_count = length // block_rows
    attn_scale = HD ** (-0.5)
    copies = (
        lax.all_gather(query_weight.astype(jnp.bfloat16), "wide", axis=0, tiled=True),
        lax.all_gather(keyval_weight.astype(jnp.bfloat16), "wide", axis=1, tiled=True),
        lax.all_gather(output_weight.astype(jnp.bfloat16), "wide", axis=1, tiled=True),
        lax.all_gather(gateup_weight.astype(jnp.bfloat16), "wide", axis=1, tiled=True),
        lax.all_gather(down_weight.astype(jnp.bfloat16), "wide", axis=1, tiled=True),
        lax.all_gather(norm_gains.astype(jnp.bfloat16), "wide", axis=1, tiled=True),
        lax.all_gather(head_gains.astype(jnp.bfloat16), "wide", axis=1, tiled=True),
    )
    (
        query_matrix,
        key_value_matrix,
        output_matrix,
        gate_up_matrix,
        down_matrix,
        gain_norm,
        gain_head,
    ) = copies
    heads_local = query_matrix.shape[1] // HD
    pairs_local = key_value_matrix.shape[2] // HD
    groups = heads_local // pairs_local
    inputs = layer_input.astype(jnp.float32)
    scale_first = row_scale(inputs)
    unit_first = inputs * scale_first
    normed_rows = lax.all_gather(
        (unit_first * gain_norm[0]).astype(jnp.bfloat16), "narrow", axis=1, tiled=True
    )
    query_raw = jnp.einsum(
        "nxk,kc->nxc", normed_rows, query_matrix, preferred_element_type=jnp.float32
    ).reshape(sequences, length, heads_local, HD)
    key_raw = jnp.einsum(
        "nxk,kc->nxc", normed_rows, key_value_matrix[0], preferred_element_type=jnp.float32
    ).reshape(sequences, length, pairs_local, HD)
    value_raw = jnp.einsum(
        "nxk,kc->nxc", normed_rows, key_value_matrix[1], preferred_element_type=jnp.float32
    ).reshape(sequences, length, pairs_local, HD)
    cosine, sine = rope_tables(length)
    query_scale = row_scale(query_raw)
    query_unit = query_raw * query_scale
    key_scale = row_scale(key_raw)
    key_unit = key_raw * key_scale
    queries = rotate(query_unit * gain_head[0], cosine, sine).astype(jnp.bfloat16)
    keys = rotate(key_unit * gain_head[1], cosine, sine).astype(jnp.bfloat16)
    values = value_raw.astype(jnp.bfloat16)
    query_groups = queries.reshape(sequences, length, pairs_local, groups, HD)
    context_blocks = []
    total_logs = []
    for block in range(block_count):
        start = block * block_rows
        query_block = query_groups[:, start : start + block_rows]
        scores = masked_scores(query_block, keys, lengths, start)
        top = jnp.max(scores, axis=-1, keepdims=True)
        lifted = jnp.exp(scores - top)
        total = jnp.sum(lifted, axis=-1, keepdims=True)
        probs = (lifted / total).astype(jnp.bfloat16)
        context_blocks.append(
            jnp.einsum("skgqt,stkd->sqkgd", probs, values, preferred_element_type=jnp.float32)
        )
        total_logs.append(top + jnp.log(total))
    context_rows = (
        jnp.concatenate(context_blocks, axis=1)
        .reshape(sequences, length, heads_local * HD)
        .astype(jnp.bfloat16)
    )
    attention_share = jnp.einsum(
        "puy,yb->pub", context_rows, output_matrix, preferred_element_type=jnp.float32
    )
    resid = inputs + lax.psum_scatter(attention_share, "narrow", scatter_dimension=1, tiled=True)
    scale_second = row_scale(resid)
    unit_second = resid * scale_second
    mixed_rows = lax.all_gather(
        (unit_second * gain_norm[1]).astype(jnp.bfloat16), "narrow", axis=1, tiled=True
    )
    gate_rows = jnp.einsum(
        "ytm,mx->ytx", mixed_rows, gate_up_matrix[0], preferred_element_type=jnp.float32
    )
    up_rows = jnp.einsum(
        "ytm,mx->ytx", mixed_rows, gate_up_matrix[1], preferred_element_type=jnp.float32
    )
    sigma = jax.nn.sigmoid(gate_rows)
    activated = gate_rows * sigma
    hidden_rows = (activated * up_rows).astype(jnp.bfloat16)
    feedforward_share = jnp.einsum(
        "obt,tg->obg", hidden_rows, down_matrix, preferred_element_type=jnp.float32
    )
    result = resid + lax.psum_scatter(feedforward_share, "narrow", scatter_dimension=1, tiled=True)
    layer_out = result.astype(jnp.bfloat16)
    positions = narrow_rank * local_rows + jnp.arange(local_rows)
    valid = (positions[None, :] < lengths[:, None]).astype(jnp.float32)
    grad_result = out_grad.astype(jnp.float32) * valid[:, :, None]
    row_gradients = lax.all_gather(grad_result.astype(jnp.bfloat16), "narrow", axis=1, tiled=True)
    down_weight_grad = jnp.einsum(
        "tui,tue->ie", hidden_rows, row_gradients, preferred_element_type=jnp.float32
    )
    hidden_rows_grad = jnp.einsum(
        "yxt,ut->yxu", row_gradients, down_matrix, preferred_element_type=jnp.float32
    )
    gate_rows_grad = (
        hidden_rows_grad * up_rows * sigma * (1.0 + gate_rows * (1.0 - sigma))
    ).astype(jnp.bfloat16)
    up_rows_grad = (hidden_rows_grad * activated).astype(jnp.bfloat16)
    gateup_grad = jnp.stack(
        [
            jnp.einsum(
                "mjv,mjh->vh", mixed_rows, gate_rows_grad, preferred_element_type=jnp.float32
            ),
            jnp.einsum("mjv,mjh->vh", mixed_rows, up_rows_grad, preferred_element_type=jnp.float32),
        ]
    )
    mixed_part = jnp.einsum(
        "mao,go->mag", gate_rows_grad, gate_up_matrix[0], preferred_element_type=jnp.float32
    ) + jnp.einsum(
        "mao,go->mag", up_rows_grad, gate_up_matrix[1], preferred_element_type=jnp.float32
    )
    grad_mixed = lax.psum_scatter(mixed_part, "narrow", scatter_dimension=1, tiled=True)
    norm_second_grad = jnp.sum(grad_mixed * unit_second, axis=(0, 1))
    grad_resid = grad_result + norm_back(grad_mixed, unit_second, scale_second, gain_norm[1])
    residual_rows = lax.all_gather(grad_resid.astype(jnp.bfloat16), "narrow", axis=1, tiled=True)
    output_weight_grad = jnp.einsum(
        "wrm,wrn->mn", context_rows, residual_rows, preferred_element_type=jnp.float32
    )
    grad_context = (
        jnp.einsum("rbq,jq->rbj", residual_rows, output_matrix, preferred_element_type=jnp.float32)
        .astype(jnp.bfloat16)
        .reshape(sequences, length, pairs_local, groups, HD)
    )
    grad_keys = jnp.zeros((sequences, length, pairs_local, HD), jnp.float32)
    grad_values = jnp.zeros((sequences, length, pairs_local, HD), jnp.float32)
    query_grads = []
    for block in range(block_count):
        start = block * block_rows
        query_block = query_groups[:, start : start + block_rows]
        context_block = grad_context[:, start : start + block_rows]
        scores = masked_scores(query_block, keys, lengths, start)
        probs = jnp.exp(scores - total_logs[block])
        grad_probs = jnp.einsum(
            "sqkgd,stkd->skgqt", context_block, values, preferred_element_type=jnp.float32
        )
        grad_values = grad_values + jnp.einsum(
            "skgqt,sqkgd->stkd",
            probs.astype(jnp.bfloat16),
            context_block,
            preferred_element_type=jnp.float32,
        )
        delta = jnp.sum(probs * grad_probs, axis=-1, keepdims=True)
        grad_scores = (probs * (grad_probs - delta)).astype(jnp.bfloat16)
        query_grads.append(
            jnp.einsum("skgqt,stkd->sqkgd", grad_scores, keys, preferred_element_type=jnp.float32)
            * attn_scale
        )
        grad_keys = (
            grad_keys
            + jnp.einsum(
                "skgqt,sqkgd->stkd", grad_scores, query_block, preferred_element_type=jnp.float32
            )
            * attn_scale
        )
    grad_queries = jnp.concatenate(query_grads, axis=1).reshape(sequences, length, heads_local, HD)
    grad_qnorm = rotate_back(grad_queries, cosine, sine)
    grad_knorm = rotate_back(grad_keys, cosine, sine)
    head_grad = jnp.stack(
        [
            jnp.sum(grad_qnorm * query_unit, axis=(0, 1, 2)),
            jnp.sum(grad_knorm * key_unit, axis=(0, 1, 2)),
        ]
    )
    query_raw_grad = (
        norm_back(grad_qnorm, query_unit, query_scale, gain_head[0])
        .reshape(sequences, length, heads_local * HD)
        .astype(jnp.bfloat16)
    )
    key_raw_grad = (
        norm_back(grad_knorm, key_unit, key_scale, gain_head[1])
        .reshape(sequences, length, pairs_local * HD)
        .astype(jnp.bfloat16)
    )
    value_raw_grad = grad_values.reshape(sequences, length, pairs_local * HD).astype(jnp.bfloat16)
    query_weight_grad = jnp.einsum(
        "wfo,wfq->oq", normed_rows, query_raw_grad, preferred_element_type=jnp.float32
    )
    keyval_grad = jnp.stack(
        [
            jnp.einsum(
                "wfo,wfq->oq", normed_rows, key_raw_grad, preferred_element_type=jnp.float32
            ),
            jnp.einsum(
                "wfo,wfq->oq", normed_rows, value_raw_grad, preferred_element_type=jnp.float32
            ),
        ]
    )
    normed_share = jnp.einsum(
        "wta,qa->wtq", query_raw_grad, query_matrix, preferred_element_type=jnp.float32
    )
    normed_share = normed_share + jnp.einsum(
        "wta,qa->wtq", key_raw_grad, key_value_matrix[0], preferred_element_type=jnp.float32
    )
    normed_share = normed_share + jnp.einsum(
        "wta,qa->wtq", value_raw_grad, key_value_matrix[1], preferred_element_type=jnp.float32
    )
    grad_normed = lax.psum_scatter(normed_share, "narrow", scatter_dimension=1, tiled=True)
    norm_first_grad = jnp.sum(grad_normed * unit_first, axis=(0, 1))
    input_grad = grad_resid + norm_back(grad_normed, unit_first, scale_first, gain_norm[0])
    gain_sums = lax.psum((jnp.stack([norm_first_grad, norm_second_grad]), head_grad), "narrow")
    summed = (
        lax.psum_scatter(query_weight_grad, "wide", scatter_dimension=0, tiled=True),
        lax.psum_scatter(keyval_grad, "wide", scatter_dimension=1, tiled=True),
        lax.psum_scatter(output_weight_grad, "wide", scatter_dimension=1, tiled=True),
        lax.psum_scatter(gateup_grad, "wide", scatter_dimension=1, tiled=True),
        lax.psum_scatter(down_weight_grad, "wide", scatter_dimension=1, tiled=True),
        lax.psum_scatter(gain_sums[0], "wide", scatter_dimension=1, tiled=True),
        lax.psum_scatter(gain_sums[1], "wide", scatter_dimension=1, tiled=True),
    )
    query_new, query_first, query_second = adamw(
        query_weight, query_mean, query_square, summed[0], 0.04
    )
    keyval_new, keyval_first, keyval_second = adamw(
        keyval_weight, keyval_mean, keyval_square, summed[1], 0.04
    )
    output_new, output_first, output_second = adamw(
        output_weight, output_mean, output_square, summed[2], 0.3
    )
    gateup_new, gateup_first, gateup_second = adamw(
        gateup_weight, gateup_mean, gateup_square, summed[3], 0.04
    )
    down_new, down_first, down_second = adamw(down_weight, down_mean, down_square, summed[4], 0.025)
    norm_new, norm_first, norm_second = adamw(norm_gains, norm_mean, norm_square, summed[5], 0.4)
    head_new, head_first, head_second = adamw(head_gains, head_mean, head_square, summed[6], 0.4)
    return (
        layer_out,
        input_grad,
        query_new,
        query_first,
        query_second,
        keyval_new,
        keyval_first,
        keyval_second,
        output_new,
        output_first,
        output_second,
        gateup_new,
        gateup_first,
        gateup_second,
        down_new,
        down_first,
        down_second,
        norm_new,
        norm_first,
        norm_second,
        head_new,
        head_first,
        head_second,
    )


def solution(mesh):
    return jax.shard_map(
        per_device,
        mesh=mesh,
        in_specs=(
            P("wide", "narrow", None),
            P("wide", "narrow", None),
            P("wide"),
            P("wide", "narrow"),
            P("wide", "narrow"),
            P("wide", "narrow"),
            P(None, "wide", "narrow"),
            P(None, "wide", "narrow"),
            P(None, "wide", "narrow"),
            P("narrow", "wide"),
            P("narrow", "wide"),
            P("narrow", "wide"),
            P(None, "wide", "narrow"),
            P(None, "wide", "narrow"),
            P(None, "wide", "narrow"),
            P("narrow", "wide"),
            P("narrow", "wide"),
            P("narrow", "wide"),
            P(None, "wide"),
            P(None, "wide"),
            P(None, "wide"),
            P(None, "wide"),
            P(None, "wide"),
            P(None, "wide"),
        ),
        out_specs=(
            P("wide", "narrow", None),
            P("wide", "narrow", None),
            P("wide", "narrow"),
            P("wide", "narrow"),
            P("wide", "narrow"),
            P(None, "wide", "narrow"),
            P(None, "wide", "narrow"),
            P(None, "wide", "narrow"),
            P("narrow", "wide"),
            P("narrow", "wide"),
            P("narrow", "wide"),
            P(None, "wide", "narrow"),
            P(None, "wide", "narrow"),
            P(None, "wide", "narrow"),
            P("narrow", "wide"),
            P("narrow", "wide"),
            P("narrow", "wide"),
            P(None, "wide"),
            P(None, "wide"),
            P(None, "wide"),
            P(None, "wide"),
            P(None, "wide"),
            P(None, "wide"),
        ),
        check_vma=False,
    )
```

profile of v0, /device:TPU:1, one launch (start us, length us, event | category | flops | bytes accessed | tf_op | source)
XLA Modules:
  0.0 2058.6 jit_solution(12932799021813545560)
XLA Ops:
  9.9 17.9 all_gather.33
  34.8 12.7 all-gather
  66.2 31.8 %all-gather.11.cloned.1.call-done = bf16[1,1024,2048]{2,1,0:T(8,128)(2,1)} async-done(((bf16[1,256,2048]{2,1,0:T(8,128)(2,1)}), bf16[1,1024,2048]{2,1,0:T(8,128)(2,1)}) %all-gather.11.cloned.1.call-update) | async-done | bytes 4194320 | tf_op jit(solution)/shard_map/all_gather | solution.py:136
  102.9 45.6 %all-gather.15.cloned.1.call-done = bf16[2048,512]{1,0:T(8,128)(2,1)} async-done(((bf16[256,512]{1,0:T(8,128)(2,1)}), bf16[2048,512]{1,0:T(8,128)(2,1)}) %all-gather.15.cloned.1.call-update) | async-done | bytes 2097168 | tf_op jit(solution)/shard_map/all_gather | solution.py:113
  186.8 14.3 all-gather.17.cloned.1.call-done
  211.8 67.3 %reduce-scatter.16.cloned.1.call-done = f32[1,256,2048]{2,1,0:T(8,128)} async-done(((f32[1,1024,2048]{2,1,0:T(8,128)}), f32[1,256,2048]{2,1,0:T(8,128)}) %reduce-scatter.16.cloned.1.call-update) | async-done | bytes 2097168 | tf_op jit(solution)/shard_map/reduce_scatter | solution.py:179
  286.1 171.9 %all-gather.21.cloned.1.call-done = bf16[2,2048,1536]{2,1,0:T(8,128)(2,1)} async-done(((bf16[2,256,1536]{2,1,0:T(8,128)(2,1)}), bf16[2,2048,1536]{2,1,0:T(8,128)(2,1)}) %all-gather.21.cloned.1.call-update) | async-done | bytes 12582928 | tf_op jit(solution)/shard_map/all_gather | solution.py:116
  458.0 35.7 %all-gather.19.cloned.1.call-done = bf16[1,1024,2048]{2,1,0:T(8,128)(2,1)} async-done(((bf16[1,256,2048]{2,1,0:T(8,128)(2,1)}), bf16[1,1024,2048]{2,1,0:T(8,128)(2,1)}) %all-gather.19.cloned.1.call-update) | async-done | bytes 4194320 | tf_op jit(solution)/shard_map/all_gather | solution.py:182
  514.5 15.9 all-gather.25.cloned.1.call-done
  530.4 101.9 %all-gather.23.cloned.1.call-done = bf16[1536,2048]{1,0:T(8,128)(2,1)} async-done(((bf16[1536,256]{1,0:T(8,128)(2,1)}), bf16[1536,2048]{1,0:T(8,128)(2,1)}) %all-gather.23.cloned.1.call-update) | async-done | bytes 6291472 | tf_op jit(solution)/shard_map/all_gather | solution.py:117
  632.3 17.0 multiply_convert_fusion
  672.4 12.3 convolution_bitcast_fusion.3
  684.7 58.2 %reduce-scatter.20.cloned.1.call-done = f32[1,256,2048]{2,1,0:T(8,128)} async-done(((f32[1,1024,2048]{2,1,0:T(8,128)}), f32[1,256,2048]{2,1,0:T(8,128)}) %reduce-scatter.20.cloned.1.call-update) | async-done | bytes 2097168 | tf_op jit(solution)/shard_map/reduce_scatter | solution.py:226
  745.0 72.2 %reduce-scatter.18.cloned.1.call-done = f32[1,256,2048]{2,1,0:T(8,128)} async-done(((f32[1,1024,2048]{2,1,0:T(8,128)}), f32[1,256,2048]{2,1,0:T(8,128)}) %reduce-scatter.18.cloned.1.call-update) | async-done | bytes 2097168 | tf_op jit(solution)/shard_map/reduce_scatter | solution.py:197
  822.4 34.9 %all-gather.27.cloned.1.call-done = bf16[1,1024,2048]{2,1,0:T(8,128)(2,1)} async-done(((bf16[1,256,2048]{2,1,0:T(8,128)(2,1)}), bf16[1,1024,2048]{2,1,0:T(8,128)(2,1)}) %all-gather.27.cloned.1.call-update) | async-done | bytes 4194320 | tf_op jit(solution)/shard_map/all_gather | solution.py:229
  948.6 13.6 fusion.27
  1022.9 17.6 pad_maximum_fusion
  1040.5 41.9 %reduce-scatter.36.cloned.1.call-done = f32[16,2]{1,0:T(8,128)} async-done(((f32[128,2]{1,0:T(8,128)}), f32[16,2]{1,0:T(8,128)}) %reduce-scatter.36.cloned.1.call-update) | async-done | bytes 144
  1083.2 211.4 %reduce-scatter.32.cloned.1.call-done = f32[1536,256]{1,0:T(8,128)} async-done(((f32[1536,2048]{1,0:T(8,128)}), f32[1536,256]{1,0:T(8,128)}) %reduce-scatter.32.cloned.1.call-update) | async-done | bytes 1572880 | tf_op jit(solution)/shard_map/reduce_scatter | solution.py:320
  1299.9 85.7 %reduce-scatter.28.cloned.1.call-done = f32[512,256]{1,0:T(8,128)} async-done(((f32[512,2048]{1,0:T(8,128)}), f32[512,256]{1,0:T(8,128)}) %reduce-scatter.28.cloned.1.call-update) | async-done | bytes 524304 | tf_op jit(solution)/shard_map/reduce_scatter | solution.py:318
  1388.4 88.9 %reduce-scatter.24.cloned.1.call-done = f32[256,512]{1,0:T(8,128)} async-done(((f32[2048,512]{1,0:T(8,128)}), f32[256,512]{1,0:T(8,128)}) %reduce-scatter.24.cloned.1.call-update) | async-done | bytes 524304 | tf_op jit(solution)/shard_map/reduce_scatter | solution.py:316
  1480.2 88.3 %reduce-scatter.26.cloned.1.call-done = f32[2,256,256]{2,1,0:T(8,128)} async-done(((f32[2,2048,256]{2,1,0:T(8,128)}), f32[2,256,256]{2,1,0:T(8,128)}) %reduce-scatter.26.cloned.1.call-update) | async-done | bytes 524304 | tf_op jit(solution)/shard_map/reduce_scatter | solution.py:317
  1573.6 61.0 %reduce-scatter.34.cloned.1.call-done = f32[256,2]{1,0:T(8,128)} async-done(((f32[2048,2]{1,0:T(8,128)}), f32[256,2]{1,0:T(8,128)}) %reduce-scatter.34.cloned.1.call-update) | async-done | bytes 2064
  1643.9 399.4 %reduce-scatter.30.cloned.1.call-done = f32[2,256,1536]{2,1,0:T(8,128)} async-done(((f32[2,2048,1536]{2,1,0:T(8,128)}), f32[2,256,1536]{2,1,0:T(8,128)}) %reduce-scatter.30.cloned.1.call-update) | async-done | bytes 3145744 | tf_op jit(solution)/shard_map/reduce_scatter | solution.py:319
  (356 shorter events, 324.9 us)
Async XLA Ops:
  7.2 54.1 %all-gather.13.cloned.1.call-start = ((), (), s32[]{:S(2)}) async-start(), calls=%async_computation.12 | async-start | bytes 2359296 | tf_op jit(solution)/shard_map/all_gather | solution.py:114
  9.1 88.9 %all-gather.11.cloned.1.call-start = ((), (), s32[]{:S(2)}) async-start(), calls=%async_computation.11 | async-start | bytes 5242880 | tf_op jit(solution)/shard_map/all_gather | solution.py:136
  32.4 116.1 %all-gather.15.cloned.1.call-start = ((), (), s32[]{:S(2)}) async-start(), calls=%async_computation.13 | async-start | bytes 2359296 | tf_op jit(solution)/shard_map/all_gather | solution.py:113
  33.3 167.8 %all-gather.17.cloned.1.call-start = ((), (), s32[]{:S(2)}) async-start(), calls=%async_computation.14 | async-start | bytes 2359296 | tf_op jit(solution)/shard_map/all_gather | solution.py:115
  34.1 245.0 %reduce-scatter.16.cloned.1.call-start = ((), (), s32[]{:S(2)}) async-start(), calls=%async_computation.15 | async-start | bytes 10485760 | tf_op jit(solution)/shard_map/reduce_scatter | solution.py:179
  47.6 120.1 %copy-start.69 = (f32[128]{0:T(128)}, f32[128]{0:T(128)S(1)}, u32[]{:S(2)}) copy-start(f32[128]{0:T(128)S(1)} %get-tuple-element.78) | copy-start | bytes 1540
  208.4 249.6 %all-gather.21.cloned.1.call-start = ((), (), s32[]{:S(2)}) async-start(), calls=%async_computation.17 | async-start | bytes 14155776 | tf_op jit(solution)/shard_map/all_gather | solution.py:116
  211.8 281.9 %all-gather.19.cloned.1.call-start = ((), (), s32[]{:S(2)}) async-start(), calls=%async_computation.16 | async-start | bytes 5242880 | tf_op jit(solution)/shard_map/all_gather | solution.py:182
  282.3 248.1 %all-gather.25.cloned.1.call-start = ((), (), s32[]{:S(2)}) async-start(), calls=%async_computation.20 | async-start | bytes 5242880 | tf_op jit(solution)/shard_map/all_gather | solution.py:202
  283.6 348.8 %all-gather.23.cloned.1.call-start = ((), (), s32[]{:S(2)}) async-start(), calls=%async_computation.18 | async-start | bytes 7077888 | tf_op jit(solution)/shard_map/all_gather | solution.py:117
  286.0 456.8 %reduce-scatter.20.cloned.1.call-start = ((), (), s32[]{:S(2)}) async-start(), calls=%async_computation.21 | async-start | bytes 10485760 | tf_op jit(solution)/shard_map/reduce_scatter | solution.py:226
  672.3 144.9 %reduce-scatter.18.cloned.1.call-start = ((), (), s32[]{:S(2)}) async-start(), calls=%async_computation.19 | async-start | bytes 10485760 | tf_op jit(solution)/shard_map/reduce_scatter | solution.py:197
  684.7 172.7 %all-gather.27.cloned.1.call-start = ((), (), s32[]{:S(2)}) async-start(), calls=%async_computation.22 | async-start | bytes 5242880 | tf_op jit(solution)/shard_map/all_gather | solution.py:229
  822.3 196.9 %reduce-scatter.22.cloned.1.call-start = ((), (), s32[]{:S(2)}) async-start(), calls=%async_computation.23 | async-start | bytes 10485760 | tf_op jit(solution)/shard_map/reduce_scatter | solution.py:311
  947.7 134.6 %reduce-scatter.36.cloned.1.call-start = ((), (), s32[]{:S(2)}) async-start(), calls=%async_computation.30 | async-start | bytes 73728
  948.6 346.0 %reduce-scatter.32.cloned.1.call-start = ((), (), s32[]{:S(2)}) async-start(), calls=%async_computation.28 | async-start | bytes 14155776 | tf_op jit(solution)/shard_map/reduce_scatter | solution.py:320
  962.3 423.4 %reduce-scatter.28.cloned.1.call-start = ((), (), s32[]{:S(2)}) async-start(), calls=%async_computation.26 | async-start | bytes 4718592 | tf_op jit(solution)/shard_map/reduce_scatter | solution.py:318
  970.1 507.2 %reduce-scatter.24.cloned.1.call-start = ((), (), s32[]{:S(2)}) async-start(), calls=%async_computation.24 | async-start | bytes 4718592 | tf_op jit(solution)/shard_map/reduce_scatter | solution.py:316
  978.3 590.2 %reduce-scatter.26.cloned.1.call-start = ((), (), s32[]{:S(2)}) async-start(), calls=%async_computation.25 | async-start | bytes 4718592 | tf_op jit(solution)/shard_map/reduce_scatter | solution.py:317
  985.9 648.6 %reduce-scatter.34.cloned.1.call-start = ((), (), s32[]{:S(2)}) async-start(), calls=%async_computation.29 | async-start | bytes 1179648
  1022.8 1020.5 %reduce-scatter.30.cloned.1.call-start = ((), (), s32[]{:S(2)}) async-start(), calls=%async_computation.27 | async-start | bytes 28311552 | tf_op jit(solution)/shard_map/reduce_scatter | solution.py:319
  1040.5 254.1 %copy-start.28 = (f32[1536,256]{1,0:T(8,128)S(1)}, f32[1536,256]{1,0:T(8,128)}, u32[]{:S(2)}) copy-start(f32[1536,256]{1,0:T(8,128)} %param.39) | copy-start | bytes 4718596
  1083.2 302.5 %copy-start.46 = (f32[512,256]{1,0:T(8,128)S(1)}, f32[512,256]{1,0:T(8,128)}, u32[]{:S(2)}) copy-start(f32[512,256]{1,0:T(8,128)} %param.33) | copy-start | bytes 1572868
  1388.4 183.1 %copy-start.21 = (f32[1,256,2048]{2,1,0:T(8,128)S(1)}, f32[1,256,2048]{2,1,0:T(8,128)}, u32[]{:S(2)}) copy-start(f32[1,256,2048]{2,1,0:T(8,128)} %reduce-scatter.22.cloned.1.call-done) | copy-start | bytes 6291460
  (90 other events, 1221.5 us)
Sparse Core Ops, SparseCore 0:
  10.8 50.4 all-gather.12
  63.5 34.4 all-gather.10
  100.7 47.7 all-gather.14
  151.0 50.0 all-gather.16
  208.5 70.5 reduce-scatter.15
  281.9 175.9 all-gather.20
  460.2 33.4 all-gather.18
  495.9 34.4 all-gather.24
  533.2 99.0 all-gather.22
  672.4 70.3 reduce-scatter.19
  745.4 71.7 reduce-scatter.17
  822.4 34.8 all-gather.26
  947.9 71.2 reduce-scatter.21
  1023.0 59.3 reduce-scatter.35
  1085.8 208.6 reduce-scatter.31
  1298.1 87.5 reduce-scatter.27
  1389.6 87.6 reduce-scatter.23
  1480.8 87.6 reduce-scatter.25
  1572.9 61.6 reduce-scatter.33
  1638.2 405.0 reduce-scatter.29
where the time goes:
time: 2060 us
  waiting for transfers between devices  1640 us (80%)
  matrix products  196 us (10%)
  other arithmetic  112 us (5%)
  local copies, waits for them, and re-layouts  51.4 us (2%)
  blocking collectives  37.8 us (2%)
    reduce_scatter x1, waiting for transfers between devices, per_device(): lax.psum_scatter(gateup_grad, 'wide', scatter_dimension=1, tiled=True)  399 us
    reduce_scatter x1, waiting for transfers between devices, per_device(): lax.psum_scatter(down_weight_grad, 'wide', scatter_dimension=1, tiled=True)  211 us
    all_gather x1, waiting for transfers between devices, per_device(): lax.all_gather(gateup_weight.astype(jnp.bfloat16), 'wide', axis=1, tiled=...  172 us
    unnamed x22, waiting for transfers between devices  103 us
    all_gather x1, waiting for transfers between devices, per_device(): lax.all_gather(down_weight.astype(jnp.bfloat16), 'wide', axis=1, tiled=True)  102 us
    reduce_scatter x1, waiting for transfers between devices, per_device(): lax.psum_scatter(query_weight_grad, 'wide', scatter_dimension=0, tiled=True)  88.9 us
    reduce_scatter x1, waiting for transfers between devices, per_device(): lax.psum_scatter(keyval_grad, 'wide', scatter_dimension=1, tiled=True)  88.3 us
    reduce_scatter x1, waiting for transfers between devices, per_device(): lax.psum_scatter(output_weight_grad, 'wide', scatter_dimension=1, tiled=T...  85.7 us
  transfers between devices with their start and end apart: 20, of which 20 were waited for; matrix products, arithmetic and copies ran while one was open for 9% of the time, Pallas kernels for 0%

commit v1 on v0

v1 whole, which is shorter than its diff:
```python
import functools

import jax
import jax.numpy as jnp
from jax import lax
from jax.experimental import pallas as pl
from jax.experimental.pallas import tpu as pltpu
from jax.sharding import PartitionSpec as P

HD = 128
STEP = 5
MESH = pl.DeviceIdType.MESH
MIB = 2**20

norm_eps = 1e-06
rope_base = 1000000.0
beta_first = 0.5
beta_second = 0.5
adam_eps = 1e-08
weight_decay = 0.1
masked_fill = -1e30
f32 = jnp.float32
bf16 = jnp.bfloat16


def row_scale(values):
    return lax.rsqrt(jnp.mean(values * values, axis=-1, keepdims=True) + norm_eps)


def norm_back(grad, unit, scale, gain):
    scaled = grad * gain
    return scale * (scaled - unit * jnp.mean(scaled * unit, axis=-1, keepdims=True))


def adamw(weight, first, second, grad, rate):
    first_new = beta_first * first + (1.0 - beta_first) * grad
    second_new = beta_second * second + (1.0 - beta_second) * grad * grad
    first_hat = first_new / (1.0 - beta_first**STEP)
    second_hat = second_new / (1.0 - beta_second**STEP)
    weight_new = weight - rate * (
        first_hat / (jnp.sqrt(second_hat) + adam_eps) + weight_decay * weight
    )
    return (weight_new, first_new, second_new)


def rope_tables(length):
    half = HD // 2
    freqs = rope_base ** (-(jnp.arange(half, dtype=f32) * 2.0) / HD)
    angles = jnp.arange(length, dtype=f32)[:, None] * freqs[None, :]
    cosine = jnp.cos(angles)
    sine = jnp.sin(angles)
    return (
        jnp.concatenate([cosine, cosine], axis=-1),
        jnp.concatenate([-sine, sine], axis=-1),
    )


def dot_nn(left, right):
    return lax.dot_general(left, right, (((1,), (0,)), ((), ())), preferred_element_type=f32)


def dot_nt(left, right):
    return lax.dot_general(left, right, (((1,), (1,)), ((), ())), preferred_element_type=f32)


def dot_tn(left, right):
    return lax.dot_general(left, right, (((0,), (0,)), ((), ())), preferred_element_type=f32)


def loop(count, step):
    def body(index, carry):
        step(index)
        return carry

    lax.fori_loop(0, count, body, 0)


def rows(index, size):
    return pl.ds(pl.multiple_of(index * size, size), size)


class Place:
    def __init__(self, wide, narrow):
        self.depth = wide // 2
        w = lax.axis_index("wide")
        n = lax.axis_index("narrow")
        self.w, self.n = w, n
        self.z = w // 2
        self.x = w - 2 * self.z
        self.y = n // 2
        self.c = n - 2 * self.y

    def far(self, k, dx):
        x = self.x if dx == 0 else 1 - self.x
        return (lax.rem(self.z + k, self.depth) * 2 + x, self.n)

    def side(self, dy, dc):
        y = self.y if dy == 0 else 1 - self.y
        c = self.c if dc == 0 else 1 - self.c
        return (self.w, y * 2 + c)

    def slot(self, block):
        ay, ac = block // 2, block % 2
        dy = lax.rem(self.y + ay, 2)
        dc = lax.rem(self.c + ac, 2)
        return dc * 2 + dy


def remote(src, dst, send, recv, device):
    return pltpu.make_async_remote_copy(
        src_ref=src,
        dst_ref=dst,
        send_sem=send,
        recv_sem=recv,
        device_id=device,
        device_id_type=MESH,
    )


class Side:
    def __init__(self, place, send, recv):
        self.place, self.send, self.recv = place, send, recv
        self.used = 0
        self.sent = []

    def copy(self, src, dst, dy, dc):
        i = self.used
        self.used += 1
        made = remote(src, dst, self.send.at[i], self.recv.at[i], self.place.side(dy, dc))
        made.start()
        self.sent.append(made)
        return made

    def drain(self):
        for made in self.sent:
            made.wait_send()


class Gather:
    def __init__(self, side, own, buf, size):
        self.side, self.buf, self.size = side, buf, size
        self.across = side.copy(own, buf.at[pl.ds(size, size)], 1, 0)
        self.core = side.copy(own, buf.at[pl.ds(2 * size, size)], 0, 1)

    def forward(self):
        size = self.size
        self.across.wait_recv()
        self.last = self.side.copy(
            self.buf.at[pl.ds(size, size)], self.buf.at[pl.ds(3 * size, size)], 0, 1
        )

    def done(self):
        self.core.wait_recv()
        self.last.wait_recv()


class Wide:
    def __init__(self, place, block, chunks, own, full, zs, zr, xs, xr):
        self.place, self.block, self.chunks, self.own, self.full = place, block, chunks, own, full
        self.zs, self.zr, self.xs, self.xr = zs, zr, xs, xr
        self.near = place.depth == 4

    def slot(self, i, index):
        g, a, b = self.chunks[i]
        return self.full[g].at[pl.ds(index * self.block, self.block), pl.ds(a, b - a)]

    def mine(self, i):
        g, a, b = self.chunks[i]
        return self.own[g].at[:, pl.ds(a, b - a)]

    def along(self, i, k):
        depth = self.place.depth
        return remote(
            self.mine(i),
            self.slot(i, k),
            self.zs.at[i, k],
            self.zr.at[i, k],
            self.place.far(depth - k, 0),
        )

    def beyond(self, i, k):
        depth = self.place.depth
        return remote(
            self.slot(i, 2),
            self.slot(i, k),
            self.zs.at[i, depth + k],
            self.zr.at[i, k],
            self.place.far(1 if k == 1 else depth - 1, 0),
        )

    def across(self, i, k):
        depth = self.place.depth
        src = self.mine(i) if k == 0 else self.slot(i, k)
        return remote(
            src, self.slot(i, depth + k), self.xs.at[i, k], self.xr.at[i, k], self.place.far(0, 1)
        )

    def each(self, i, k, act):
        place = self.place
        if self.near and k in (1, 3):
            at_end = (place.z == 0) if k == 1 else (place.z == 3)

            @pl.when(jnp.logical_not(at_end))
            def _():
                act(self.along(i, k))
        else:
            act(self.along(i, k))

    def order(self):
        depth = self.place.depth
        return (2, 1, 3) if self.near else tuple(range(1, depth))

    def issue(self, i):
        if i >= len(self.chunks):
            return
        self.across(i, 0).start()
        for k in self.order():
            self.each(i, k, lambda made: made.start())

    def hand_on(self, i):
        z = self.place.z
        for k in self.order():
            self.along(i, k).wait_recv()
            if self.near and k == 2:

                @pl.when(z == 2)
                def _():
                    self.beyond(i, 1).start()

                @pl.when(z == 1)
                def _():
                    self.beyond(i, 3).start()

            self.across(i, k).start()

    def arrived(self, i):
        for k in range(self.place.depth):
            self.across(i, k).wait_recv()

    def drain(self):
        z = self.place.z
        for i in range(len(self.chunks)):
            for k in range(self.place.depth):
                if k:
                    self.each(i, k, lambda made: made.wait_send())
                if self.near and k in (1, 3):

                    @pl.when(z == (2 if k == 1 else 1))
                    def _():
                        self.beyond(i, k).wait_send()

                self.across(i, k).wait_send()


def greet(place):
    depth = place.depth
    peers = [place.far(k, dx) for dx in (0, 1) for k in range(depth) if k or dx]
    peers += [place.side(1, 0), place.side(0, 1)]
    barrier = pltpu.get_barrier_semaphore()
    for peer in peers:
        pl.semaphore_signal(barrier, inc=1, device_id=peer, device_id_type=MESH)
    pl.semaphore_wait(barrier, len(peers))


def turn(values):
    return pltpu.roll(values, HD // 2, 1)


def rope(values, cosine, sine):
    return values * cosine + turn(values) * sine


def rope_back(grads, cosine, sine):
    return grads * cosine - turn(grads) * sine


def softmax_block(query, keys, block, size, count, length):
    scores = dot_nt(query, keys) * HD ** (-0.5)
    shape = scores.shape
    at = block * size + lax.broadcasted_iota(jnp.int32, shape, 0)
    to = lax.broadcasted_iota(jnp.int32, shape, 1)
    scores = jnp.where((to <= at) & (to < length), scores, masked_fill)
    lifted = jnp.exp(scores - jnp.max(scores, axis=-1, keepdims=True))
    return lifted / jnp.sum(lifted, axis=-1, keepdims=True)


def chunks_of(widths):
    qkv, out, gate, up, down = widths
    return [
        (0, 0, qkv // 2),
        (0, qkv // 2, qkv),
        (1, 0, out),
        (2, 0, gate // 2),
        (3, 0, up // 2),
        (2, gate // 2, gate),
        (3, up // 2, up),
        (4, 0, down // 2),
        (4, down // 2, down),
    ]


def forward_kernel(
    wide,
    heads,
    pairs,
    length_ref,
    x_ref,
    gain_ref,
    cos_ref,
    sin_ref,
    dyb_ref,
    own_qkv,
    own_out,
    own_gate,
    own_up,
    own_down,
    full_qkv,
    full_out,
    full_gate,
    full_up,
    full_down,
    o_dyb,
    o_normed,
    o_qkv,
    o_ctx,
    o_resid,
    o_mixed,
    o_gate,
    o_up,
    o_hidden,
    gains,
    head_gain,
    slots,
    normed,
    qkv,
    ctx,
    resid,
    mixed,
    gate,
    up,
    hidden,
    weights,
    k_act,
    v_act,
    half_out,
    half_in,
    cross_out,
    cross_in,
    zs,
    zr,
    xs,
    xr,
    ns,
    nr,
    gs,
    gr,
    ls,
):
    place = Place(wide, 4)
    depth = place.depth
    size, width = x_ref.shape
    block = width // wide
    ff = gate.shape[1]
    groups = heads // pairs
    span = 4 * size
    own = [own_qkv, own_out, own_gate, own_up, own_down]
    full = [full_qkv, full_out, full_gate, full_up, full_down]
    chunks = chunks_of([ref.shape[1] for ref in full])
    greet(place)
    ag = Wide(place, block, chunks, own, full, zs, zr, xs, xr)
    side = Side(place, ns, nr)

    gain_copies = []
    for dx in (0, 1):
        for k in range(depth):
            if k or dx:
                at = dx * depth + (depth - k) % depth
                made = remote(
                    gain_ref, slots.at[at], gs.at[at], gr.at[at], place.far(k, dx)
                )
                made.start()
                gain_copies.append(made)
    for i in range(3):
        ag.issue(i)
    local = []

    def keep(src, dst):
        made = pltpu.make_async_copy(src, dst, ls.at[len(local)])
        made.start()
        local.append(made)
        return made

    for g in range(5):
        keep(own[g], full[g].at[pl.ds(0, block)])
    keep(dyb_ref, o_dyb.at[pl.ds(0, size)])
    slots[0] = gain_ref[...]
    for made in gain_copies:
        made.wait_recv()
    gains[...] = jnp.concatenate([slots[b][:, :block] for b in range(wide)], axis=1)
    total = slots[0][:, :HD]
    for b in range(1, wide):
        total = total + slots[b][:, :HD]
    head_gain[...] = total

    def first_norm(i):
        at = rows(i, size // 4)
        x = x_ref[at, :].astype(f32)
        normed[at, :] = (x * row_scale(x) * gains[0:1, :]).astype(bf16)

    loop(4, first_norm)
    take_normed = Gather(side, normed.at[pl.ds(0, size)], normed, size)
    take_dyb = Gather(side, dyb_ref, o_dyb, size)
    take_normed.forward()
    ag.hand_on(0)
    ag.issue(3)
    take_dyb.forward()
    take_normed.done()
    keep(normed, o_normed)
    ag.hand_on(1)
    ag.issue(4)
    ag.arrived(0)
    ag.arrived(1)
    qkv_width = full_qkv.shape[1]
    out_width = full_out.shape[1]
    w_qkv = weights.at[:, pl.ds(0, qkv_width)]
    w_out = weights.at[:, pl.ds(qkv_width, out_width)]
    local[0].wait()
    get = pltpu.make_async_copy(full_qkv, w_qkv, ls.at[20])
    get.start()
    get.wait()

    def project(m):
        for n in range(qkv_width // 512):
            qkv[rows(m, size), pl.ds(n * 512, 512)] = dot_nn(
                normed[rows(m, size), :], weights[:, pl.ds(n * 512, 512)]
            )

    loop(4, project)
    keep(qkv, o_qkv)
    ag.hand_on(2)
    ag.issue(5)

    length = length_ref[0]

    def pair(p):
        def keys(a):
            at = rows(place.slot(a), size)
            to = pl.ds(a * size, size)
            raw = qkv[at, pl.ds(pl.multiple_of((heads + p) * HD, HD), HD)]
            unit = raw * row_scale(raw) * head_gain[3:4, :]
            k_act[to, :] = rope(unit, cos_ref[to, :], sin_ref[to, :]).astype(bf16)
            v_act[to, :] = qkv[
                at, pl.ds(pl.multiple_of((heads + pairs + p) * HD, HD), HD)
            ].astype(bf16)

        for a in range(4):
            keys(a)

        def head(g):
            column = pl.ds(pl.multiple_of((p * groups + g) * HD, HD), HD)
            for a in range(4):
                at = rows(place.slot(a), size)
                to = pl.ds(a * size, size)
                raw = qkv[at, column]
                unit = raw * row_scale(raw) * head_gain[2:3, :]
                query = rope(unit, cos_ref[to, :], sin_ref[to, :]).astype(bf16)
                last = (a + 1) * size
                probs = softmax_block(query, k_act[0:last, :], a, size, last, length)
                ctx[at, column] = dot_nn(probs.astype(bf16), v_act[0:last, :]).astype(bf16)

        loop(groups, head)

    loop(pairs, pair)
    keep(ctx, o_ctx)
    ag.hand_on(3)
    ag.issue(6)
    ag.arrived(2)
    local[1].wait()
    get = pltpu.make_async_copy(full_out, w_out, ls.at[21])
    get.start()
    get.wait()

    step = 512

    def to_core(n):
        at = rows(n, step)
        half_out[:, at] = dot_nt(
            ctx[pl.ds(2 * size, 2 * size), :], weights[at, pl.ds(qkv_width, out_width)]
        ).astype(bf16)

    loop(width // step, to_core)
    core = side.copy(half_out, half_in, 0, 1)
    core.wait_recv()

    def to_other(n):
        at = rows(n, step)
        cross_out[:, at] = (
            dot_nt(ctx[pl.ds(size, size), :], weights[at, pl.ds(qkv_width, out_width)])
            + half_in[pl.ds(size, size), at].astype(f32)
        ).astype(bf16)

    loop(width // step, to_other)
    other = side.copy(cross_out, cross_in, 1, 0)

    def to_self(n):
        at = rows(n, step)
        resid[:, at] = (
            dot_nt(ctx[pl.ds(0, size), :], weights[at, pl.ds(qkv_width, out_width)])
            + half_in[pl.ds(0, size), at].astype(f32)
            + x_ref[:, at].astype(f32)
        )

    loop(width // step, to_self)
    other.wait_recv()

    def second_norm(i):
        at = rows(i, size // 4)
        value = resid[at, :] + cross_in[at, :].astype(f32)
        resid[at, :] = value
        mixed[at, :] = (value * row_scale(value) * gains[1:2, :]).astype(bf16)

    loop(4, second_norm)
    take_mixed = Gather(side, mixed.at[pl.ds(0, size)], mixed, size)
    keep(resid, o_resid)
    ag.hand_on(4)
    ag.issue(7)
    take_mixed.forward()
    take_mixed.done()
    take_dyb.done()
    keep(mixed, o_mixed)
    ag.hand_on(5)
    ag.issue(8)
    half = ff // 2

    def feed(part):
        a = part * half
        get_gate = pltpu.make_async_copy(
            full_gate.at[:, pl.ds(a, half)], weights.at[:, pl.ds(0, half)], ls.at[22]
        )
        get_up = pltpu.make_async_copy(
            full_up.at[:, pl.ds(a, half)], weights.at[:, pl.ds(half, half)], ls.at[23]
        )
        get_gate.start()
        get_up.start()
        get_gate.wait()
        get_up.wait()
        tile = 256

        def columns(n):
            def body(m):
                at = rows(m, size)
                left = mixed[at, :]
                gate_part = dot_nn(left, weights[:, rows(n, tile)])
                up_part = dot_nn(
                    left, weights[:, pl.ds(pl.multiple_of(half + n * tile, tile), tile)]
                )
                to = pl.ds(pl.multiple_of(a + n * tile, tile), tile)
                gate[at, to] = gate_part
                up[at, to] = up_part
                hidden[at, to] = (gate_part * jax.nn.sigmoid(gate_part) * up_part).astype(bf16)

            loop(4, body)

        loop(half // tile, columns)

    local[2].wait()
    local[3].wait()
    ag.arrived(3)
    ag.arrived(4)
    feed(0)
    ag.hand_on(6)
    ag.arrived(5)
    ag.arrived(6)
    feed(1)
    keep(gate, o_gate)
    keep(up, o_up)
    keep(hidden, o_hidden)
    ag.hand_on(7)
    ag.hand_on(8)
    ag.arrived(7)
    ag.arrived(8)
    for i, made in enumerate(local):
        if i > 3:
            made.wait()
    for made in gain_copies:
        made.wait_send()
    side.drain()
    ag.drain()


def forward_call(lengths, x, gain, cosine, sine, dyb, own, heads, pairs):
    wide = lax.axis_size("wide")
    size, width = x.shape
    span = 4 * size
    block = width // wide
    ff = own[2].shape[1]
    qkv_width = own[0].shape[1]
    out_width = own[1].shape[1]
    lanes = gain.shape[1]
    shape = jax.ShapeDtypeStruct
    anywhere = pl.BlockSpec(memory_space=pl.ANY)
    vmem = pl.BlockSpec(memory_space=pltpu.VMEM)
    count = len(chunks_of([w.shape[1] for w in own]))
    depth = wide // 2
    outs = [shape((width, w.shape[1]), bf16) for w in own] + [
        shape((span, width), bf16),
        shape((span, width), bf16),
        shape((span, qkv_width), f32),
        shape((span, out_width), bf16),
        shape((size, width), f32),
        shape((span, width), bf16),
        shape((span, ff), f32),
        shape((span, ff), f32),
        shape((span, ff), bf16),
        shape((8, width), f32),
        shape((8, HD), f32),
    ]
    return pl.pallas_call(
        functools.partial(forward_kernel, wide, heads, pairs),
        out_shape=outs,
        in_specs=[pl.BlockSpec(memory_space=pltpu.SMEM)] + [vmem] * 4 + [anywhere] * 6,
        out_specs=[anywhere] * 14 + [vmem] * 2,
        scratch_shapes=[
            pltpu.VMEM((wide, 8, lanes), f32),
            pltpu.VMEM((span, width), bf16),
            pltpu.VMEM((span, qkv_width), f32),
            pltpu.VMEM((span, out_width), bf16),
            pltpu.VMEM((size, width), f32),
            pltpu.VMEM((span, width), bf16),
            pltpu.VMEM((span, ff), f32),
            pltpu.VMEM((span, ff), f32),
            pltpu.VMEM((span, ff), bf16),
            pltpu.VMEM((width, max(qkv_width + out_width, ff)), bf16),
            pltpu.VMEM((span, HD), bf16),
            pltpu.VMEM((span, HD), bf16),
            pltpu.VMEM((2 * size, width), bf16),
            pltpu.VMEM((2 * size, width), bf16),
            pltpu.VMEM((size, width), bf16),
            pltpu.VMEM((size, width), bf16),
            pltpu.SemaphoreType.DMA((count, 2 * depth)),
            pltpu.SemaphoreType.DMA((count, depth)),
            pltpu.SemaphoreType.DMA((count, depth)),
            pltpu.SemaphoreType.DMA((count, depth)),
            pltpu.SemaphoreType.DMA((16,)),
            pltpu.SemaphoreType.DMA((16,)),
            pltpu.SemaphoreType.DMA((wide,)),
            pltpu.SemaphoreType.DMA((wide,)),
            pltpu.SemaphoreType.DMA((24,)),
        ],
        compiler_params=pltpu.CompilerParams(
            collective_id=0, has_side_effects=True, vmem_limit_bytes=62 * MIB
        ),
    )(lengths, x, gain, cosine, sine, dyb, *own)


def owners(wide):
    depth = wide // 2
    w = lax.axis_index("wide")
    z, x = w // 2, w % 2
    return [
        ((z + k) % depth) * 2 + (x if dx == 0 else 1 - x) for dx in (0, 1) for k in range(depth)
    ]


def places(wide):
    depth = wide // 2
    w = lax.axis_index("wide")
    z, x = w // 2, w % 2
    return [
        jnp.where(x == o % 2, 0, depth) + (o // 2 - z) % depth for o in range(wide)
    ]


def reorder(values, order):
    block = values.shape[-1] // len(order)
    return jnp.concatenate(
        [lax.dynamic_slice_in_dim(values, at * block, block, axis=-1) for at in order], axis=-1
    )


def along_z(values, k):
    wide = lax.axis_size("wide")
    depth = wide // 2
    return lax.ppermute(
        values, "wide", [(w, ((w // 2 + k) % depth) * 2 + w % 2) for w in range(wide)]
    )


def along_x(values):
    return lax.ppermute(values, "wide", [(w, w ^ 1) for w in range(lax.axis_size("wide"))])


def side(values, flip):
    return lax.ppermute(values, "narrow", [(n, n ^ flip) for n in range(4)])


def scatter_wide(left, right):
    wide = lax.axis_size("wide")
    depth = wide // 2
    half = left.shape[1] // 2
    block = left.shape[1] // wide
    away = dot_tn(left[:, half:], right).astype(bf16)
    got = along_x(away)
    home = (dot_tn(left[:, :half], right) + got.astype(f32)).astype(bf16)
    total = home[:block].astype(f32)
    for k in range(1, depth):
        total = total + along_z(home[k * block : (k + 1) * block], k).astype(f32)
    return total


def scatter_side(values):
    half = values.shape[0] // 2
    size = half // 2
    kept = values[:half] + side(values[half:].astype(bf16), 1).astype(f32)
    return kept[:size] + side(kept[size:].astype(bf16), 2).astype(f32)


def gather_side(values):
    other = side(values, 2)
    return jnp.concatenate([values, other, side(values, 1), side(other, 1)], axis=0)


def per_device(
    layer_input,
    out_grad,
    lengths,
    query_weight,
    query_mean,
    query_square,
    keyval_weight,
    keyval_mean,
    keyval_square,
    output_weight,
    output_mean,
    output_square,
    gateup_weight,
    gateup_mean,
    gateup_square,
    down_weight,
    down_mean,
    down_square,
    norm_gains,
    norm_mean,
    norm_square,
    head_gains,
    head_mean,
    head_square,
):
    wide = lax.axis_size("wide")
    depth = wide // 2
    w = lax.axis_index("wide")
    n = lax.axis_index("narrow")
    _, size, width = layer_input.shape
    block = width // wide
    span = 4 * size
    heads = query_weight.shape[1] // HD
    pairs = keyval_weight.shape[2] // HD
    groups = heads // pairs
    owner, place = owners(wide), places(wide)
    x = reorder(layer_input[0], owner)
    positions = n * size + jnp.arange(size)
    valid = positions < lengths[0]
    dyb = reorder(jnp.where(valid[:, None], out_grad[0], 0).astype(bf16), owner)
    own = [
        jnp.concatenate([query_weight, keyval_weight[0], keyval_weight[1]], axis=1).astype(bf16),
        output_weight.astype(bf16).T,
        gateup_weight[0].astype(bf16),
        gateup_weight[1].astype(bf16),
        down_weight.astype(bf16).T,
    ]
    lanes = max(HD, block)
    part = HD // wide
    gain = jnp.zeros((8, lanes), f32)
    gain = gain.at[0:2, 0:block].set(norm_gains.astype(bf16).astype(f32))
    gain = lax.dynamic_update_slice(gain, head_gains.astype(bf16).astype(f32), (2, w * part))
    cosine, sine = rope_tables(span)
    (
        full_qkv,
        full_out,
        full_gate,
        full_up,
        full_down,
        row_gradients,
        normed,
        qkv,
        context,
        resid,
        mixed,
        gate,
        up,
        hidden,
        gains,
        head_gain,
    ) = forward_call(lengths, x, gain, cosine, sine, dyb, own, heads, pairs)
    inputs = x.astype(f32)
    scale_first = row_scale(inputs)
    unit_first = inputs * scale_first
    scale_second = row_scale(resid)
    unit_second = resid * scale_second
    result = resid + scatter_side(dot_nt(hidden, full_down))
    layer_out = reorder(result.astype(bf16), place)[None]
    sigma = jax.nn.sigmoid(gate)
    hidden_grad = dot_nn(row_gradients, full_down)
    gate_grad = (hidden_grad * up * sigma * (1.0 + gate * (1.0 - sigma))).astype(bf16)
    up_grad = (hidden_grad * gate * sigma).astype(bf16)
    down_total = scatter_wide(row_gradients, hidden)
    gate_total = scatter_wide(mixed, gate_grad)
    up_total = scatter_wide(mixed, up_grad)
    grad_mixed = scatter_side(dot_nt(gate_grad, full_gate) + dot_nt(up_grad, full_up))
    norm_second_grad = jnp.sum(grad_mixed * unit_second, axis=0)
    grad_resid = dyb.astype(f32) + norm_back(grad_mixed, unit_second, scale_second, gains[1:2])
    residual_rows = gather_side(grad_resid.astype(bf16))
    output_total = scatter_wide(residual_rows, context)
    grad_context = dot_nn(residual_rows, full_out).astype(bf16)
    position_rows = jnp.concatenate(
        [(n ^ flip) * size + jnp.arange(size) for flip in (0, 2, 1, 3)]
    )
    cos_rows = jnp.take(cosine, position_rows, axis=0)[:, None]
    sin_rows = jnp.take(sine, position_rows, axis=0)[:, None]

    def turned(v):
        return jnp.roll(v, HD // 2, axis=-1)

    query_raw = qkv[:, : heads * HD].reshape(span, heads, HD)
    key_raw = qkv[:, heads * HD : (heads + pairs) * HD].reshape(span, pairs, HD)
    values = qkv[:, (heads + pairs) * HD :].reshape(span, pairs, HD).astype(bf16)
    query_scale = row_scale(query_raw)
    key_scale = row_scale(key_raw)
    query_unit = query_raw * query_scale
    key_unit = key_raw * key_scale
    gq, gk = head_gain[2], head_gain[3]
    queries = (query_unit * gq * cos_rows + turned(query_unit * gq) * sin_rows).astype(bf16)
    keys = (key_unit * gk * cos_rows + turned(key_unit * gk) * sin_rows).astype(bf16)
    queries = queries.reshape(span, pairs, groups, HD)
    scores = jnp.einsum("qkgd,tkd->kgqt", queries, keys, preferred_element_type=f32) * HD ** (-0.5)
    allowed = (position_rows[None, :] <= position_rows[:, None]) & (
        position_rows[None, :] < lengths[0]
    )
    scores = jnp.where(allowed[None, None], scores, masked_fill)
    probs = jax.nn.softmax(scores, axis=-1)
    gctx = grad_context.reshape(span, pairs, groups, HD)
    grad_probs = jnp.einsum("qkgd,tkd->kgqt", gctx, values, preferred_element_type=f32)
    grad_values = jnp.einsum(
        "kgqt,qkgd->tkd", probs.astype(bf16), gctx, preferred_element_type=f32
    )
    delta = jnp.sum(probs * grad_probs, axis=-1, keepdims=True)
    grad_scores = (probs * (grad_probs - delta)).astype(bf16)
    grad_queries = jnp.einsum(
        "kgqt,tkd->qkgd", grad_scores, keys, preferred_element_type=f32
    ).reshape(span, heads, HD) * HD ** (-0.5)
    grad_keys = jnp.einsum(
        "kgqt,qkgd->tkd", grad_scores, queries, preferred_element_type=f32
    ) * HD ** (-0.5)
    grad_qnorm = grad_queries * cos_rows - turned(grad_queries) * sin_rows
    grad_knorm = grad_keys * cos_rows - turned(grad_keys) * sin_rows
    head_grad = jnp.stack(
        [
            jnp.sum(grad_qnorm * query_unit, axis=(0, 1)),
            jnp.sum(grad_knorm * key_unit, axis=(0, 1)),
        ]
    )
    qkv_grad = jnp.concatenate(
        [
            norm_back(grad_qnorm, query_unit, query_scale, gq).reshape(span, heads * HD),
            norm_back(grad_knorm, key_unit, key_scale, gk).reshape(span, pairs * HD),
            grad_values.reshape(span, pairs * HD),
        ],
        axis=1,
    ).astype(bf16)
    qkv_total = scatter_wide(normed, qkv_grad)
    grad_normed = scatter_side(dot_nt(qkv_grad, full_qkv))
    norm_first_grad = jnp.sum(grad_normed * unit_first, axis=0)
    input_grad = grad_resid + norm_back(grad_normed, unit_first, scale_first, gains[0:1])
    input_grad = reorder(input_grad, place)[None]
    norm_grads = reorder(jnp.stack([norm_first_grad, norm_second_grad]), place)
    norm_grads, head_grad = lax.psum((norm_grads, head_grad), ("wide", "narrow"))
    norm_total = lax.dynamic_slice_in_dim(norm_grads, w * block, block, axis=1)
    head_total = lax.dynamic_slice_in_dim(head_grad, w * part, part, axis=1)
    split = heads * HD
    key_split = split + pairs * HD
    query = adamw(query_weight, query_mean, query_square, qkv_total[:, :split], 0.04)
    keyval = adamw(
        keyval_weight,
        keyval_mean,
        keyval_square,
        jnp.stack([qkv_total[:, split:key_split], qkv_total[:, key_split:]]),
        0.04,
    )
    output = adamw(output_weight, output_mean, output_square, output_total.T, 0.3)
    gateup = adamw(
        gateup_weight, gateup_mean, gateup_square, jnp.stack([gate_total, up_total]), 0.04
    )
    down = adamw(down_weight, down_mean, down_square, down_total.T, 0.025)
    norm = adamw(norm_gains, norm_mean, norm_square, norm_total, 0.4)
    head = adamw(head_gains, head_mean, head_square, head_total, 0.4)
    return (layer_out, input_grad, *query, *keyval, *output, *gateup, *down, *norm, *head)


def solution(mesh):
    tokens = P("wide", "narrow", None)
    down = [P("wide", "narrow")] * 3
    pair = [P(None, "wide", "narrow")] * 3
    across = [P("narrow", "wide")] * 3
    gain = [P(None, "wide")] * 3
    weights = down + pair + across + pair + across + gain + gain
    return jax.shard_map(
        per_device,
        mesh=mesh,
        in_specs=(tokens, tokens, P("wide"), *weights),
        out_specs=(tokens, tokens, *weights),
        check_vma=False,
    )
```

time: 2060 us -> 948 us (0.46)
  waiting for transfers between devices: 1640 us -> 210 us
  Pallas kernels: 0 us -> 310 us
  local copies, waits for them, and re-layouts: 51.4 us -> 122 us
  matrix products: 196 us -> 137 us
  starting transfers between devices: 0.83 us -> 29.5 us
  other arithmetic: 112 us -> 89.4 us
    reduce_scatter x9 -> x0, waiting for transfers between devices: 1080 us -> none  [the longest x1 399 us: per_device(): lax.psum_scatter(gateup_grad, 'wide', scatter_dimension=1, tiled=True)]
    all_gather x9 -> x0, waiting for transfers between devices: 460 us -> none  [the longest x1 172 us: per_device(): lax.all_gather(gateup_weight.astype(jnp.bfloat16), 'wide', axis=1, tiled=...]
    pallas_call x0 -> x1, Pallas kernels: none -> 310 us  [forward_call(): pl.pallas_call(functools.partial(forward_kernel, wide, heads, pairs), out...]
    ppermute x0 -> x29, waiting for transfers between devices: none -> 210 us  [the longest x15 122 us: along_z(): lax.ppermute(values, 'wide', [(w, (w // 2 + k) % depth * 2 + w % 2) for w...]
    unnamed x22 -> x0, waiting for transfers between devices: 103 us -> none
    dot_general x33 -> x20, matrix products: 196 us -> 125 us  [the longest x10 43.8 us: dot_tn(): lax.dot_general(left, right, (((0,), (0,)), ((), ())), preferred_element_...]
    unnamed x193 -> x242, local copies, waits for them, and re-layouts: 20 us -> 56.2 us
    all_gather x2 -> x0, blocking collectives: 30.6 us -> none  [the longest x1 17.9 us: per_device(): lax.all_gather(norm_gains.astype(jnp.bfloat16), 'wide', axis=1, tiled=True)]
  transfers between devices with their start and end apart: 20 -> 29, of which waited for: 20 -> 11; matrix products, arithmetic and copies ran while one was open for 9% -> 27% of each run, Pallas kernels for 0% -> 0%
where the time goes in v1:
time: 948 us; the launch traced here: 938 us
  Pallas kernels  310 us (33%)
  waiting for transfers between devices  210 us (22%)
  matrix products  137 us (14%)
  local copies, waits for them, and re-layouts  122 us (13%)
  other arithmetic  89.4 us (9%)
  blocking collectives  37.1 us (4%)
  starting transfers between devices  29.5 us (3%)
    pallas_call x1, Pallas kernels, forward_call(): pl.pallas_call(functools.partial(forward_kernel, wide, heads, pairs), out...  310 us
    ppermute x15, waiting for transfers between devices, along_z(): lax.ppermute(values, 'wide', [(w, (w // 2 + k) % depth * 2 + w % 2) for w...  122 us
    ppermute x5, waiting for transfers between devices, along_x(): lax.ppermute(values, 'wide', [(w, w ^ 1) for w in range(lax.axis_size('wi...  69 us
    unnamed x242, local copies, waits for them, and re-layouts  56.2 us
    dot_general x10, matrix products, dot_tn(): lax.dot_general(left, right, (((0,), (0,)), ((), ())), preferred_element_...  43.8 us
    psum x1, blocking collectives, per_device(): lax.psum((norm_grads, head_grad), ('wide', 'narrow'))  37.1 us
    dot_general x4, matrix products, dot_nt(): lax.dot_general(left, right, (((1,), (1,)), ((), ())), preferred_element_...  32.2 us
    ppermute x15, starting transfers between devices, along_z(): lax.ppermute(values, 'wide', [(w, (w // 2 + k) % depth * 2 + w % 2) for w...  22 us
  transfers between devices with their start and end apart: 29, of which 11 were waited for; matrix products, arithmetic and copies ran while one was open for 27% of the time, Pallas kernels for 0%

profile of v1, /device:TPU:1, one launch (start us, length us, event | category | flops | bytes accessed | tf_op | source)
XLA Modules:
  0.0 937.7 jit_solution(15717801143825969506)
XLA Ops:
  34.7 310.1 %shard_map.407 = (bf16[2048,1024]{1,0:T(8,128)(2,1)}, bf16[2048,512]{1,0:T(8,128)(2,1)}, bf16[2048,1536]{1,0:T(8,128)(2,1)}, bf16[2048,1536]{1,0:T(8,128)(2,1)},...) custom-call(s32[1]{0:T(128)} %copy.374.length_ref, ...), custom_call_target="tpu_custom_call" | custom-call | tf_op jit(solution)/shard_map/pallas_call | solution.py:618
  344.9 15.9 %multiply_convert_fusion = (bf16[1024,1536]{1,0:T(8,128)(2,1)S(1)}, bf16[1024,1536]{1,0:T(8,128)(2,1)}) fusion(f32[1024,1536]{1,0:T(8,128)} %get-tuple-element.57, f32[1024,1536]{1,0:T(8,128)} %get-tuple-element.56, bf16[1024,2048]{1,0:T(8,128)(2,1)} %get-tuple-element.55, bf16[2048,1536]{1,0:T(8,128)(2,1)} %get-tuple-element.54), kind=kOutput, calls=%fused_computation.20 | convolution fusion | flops 6462898176 | bytes 29360128 | tf_op jit(solution)/shard_map/dot_general | solution.py:59
  360.8 11.6 %fusion.118 = f32[1024,2048]{1,0:T(8,128)} fusion(bf16[1024,1536]{1,0:T(8,128)(2,1)} %get-tuple-element.243, bf16[2048,1536]{1,0:T(8,128)(2,1)S(1)} %copy-done.81), kind=kOutput, calls=%fused_computation.281 | convolution fusion | flops 6442450944 | bytes 17825792 | tf_op jit(solution)/shard_map/dot_general | solution.py:63
  372.4 9.4 %convolution_add_fusion = f32[1024,2048]{1,0:T(8,128)S(1)} fusion(f32[1024,2048]{1,0:T(8,128)} %fusion.118, bf16[1024,1536]{1,0:T(8,128)(2,1)S(1)} %get-tuple-element.242, bf16[2048,1536]{1,0:T(8,128)(2,1)S(1)} %copy-done.80), kind=kOutput, calls=%fused_computation.34 | convolution fusion | flops 6444548096 | bytes 26214400 | tf_op jit(solution)/shard_map/dot_general | solution.py:63
  386.4 6.7 fusion.117
  459.8 11.9 %fusion.116 = (f32[2,2,1024]{2,1,0:T(2,128)S(1)}, f32[2,2,1024,1024]{2,3,1,0:T(8,128)}) fusion(pred[1024,1024]{0,1:T(8,128)(4,1)} %compare_and_fusion, bf16[1024,2,128,1]{0,2,3,1:T(8,128)(2,1)} %fusion.77, bf16[1024,2,2,128]{0,3,2,1:T(8,128)(2,1)} %fusion.31), kind=kOutput, calls=%fused_computation.279 | convolution fusion | flops 1090520064 | bytes 19415040 | tf_op jit(solution)/shard_map/sub | solution.py:840
  505.9 18.0 %collective-permute-done.1 = bf16[256,2048]{1,0:T(8,128)(2,1)} collective-permute-done((bf16[256,2048]{1,0:T(8,128)(2,1)}, bf16[256,2048]{1,0:T(8,128)(2,1)}, u32[]{:S(2)}, u32[]{:S(2)}) %collective-permute-start.1) | collective-permute-done | bytes 1048608 | tf_op jit(solution)/shard_map/ppermute | solution.py:694
  523.9 5.6 fusion.105
  529.8 11.5 %collective-permute-done.17 = bf16[1024,1536]{1,0:T(8,128)(2,1)} collective-permute-done((bf16[1024,1536]{1,0:T(8,128)(2,1)}, bf16[1024,1536]{1,0:T(8,128)(2,1)}, u32[]{:S(2)}, u32[]{:S(2)}) %collective-permute-start.17) | collective-permute-done | bytes 3145760 | tf_op jit(solution)/shard_map/ppermute | solution.py:690
  550.0 57.4 %collective-permute-done.21 = bf16[1024,1536]{1,0:T(8,128)(2,1)} collective-permute-done((bf16[1024,1536]{1,0:T(8,128)(2,1)}, bf16[1024,1536]{1,0:T(8,128)(2,1)}, u32[]{:S(2)}, u32[]{:S(2)}) %collective-permute-start.21) | collective-permute-done | bytes 3145760 | tf_op jit(solution)/shard_map/ppermute | solution.py:690
  607.5 5.3 add_convert_fusion.1
  624.6 9.5 %collective-permute-done.22 = bf16[256,1536]{1,0:T(8,128)(2,1)S(1)} collective-permute-done((bf16[256,1536]{1,0:T(8,128)(2,1)S(1)}, bf16[256,1536]{1,0:T(8,128)(2,1)S(1)}, u32[]{:S(2)}, u32[]{:S(2)}) %collective-permute-start.22) | collective-permute-done | bytes 786464 | tf_op jit(solution)/shard_map/ppermute | solution.py:684
  634.1 16.4 %collective-permute-done.24 = bf16[256,1536]{1,0:T(8,128)(2,1)S(1)} collective-permute-done((bf16[256,1536]{1,0:T(8,128)(2,1)S(1)}, bf16[256,1536]{1,0:T(8,128)(2,1)S(1)}, u32[]{:S(2)}, u32[]{:S(2)}) %collective-permute-start.24) | collective-permute-done | bytes 786464 | tf_op jit(solution)/shard_map/ppermute | solution.py:684
  650.5 7.2 collective-permute-start.28
  657.7 43.1 %collective-permute-done.23 = bf16[256,1536]{1,0:T(8,128)(2,1)S(1)} collective-permute-done((bf16[256,1536]{1,0:T(8,128)(2,1)S(1)}, bf16[256,1536]{1,0:T(8,128)(2,1)S(1)}, u32[]{:S(2)}, u32[]{:S(2)}) %collective-permute-start.23) | collective-permute-done | bytes 786464 | tf_op jit(solution)/shard_map/ppermute | solution.py:684
  707.7 5.4 convolution_convert_fusion.3
  713.1 9.6 %fusion.68 = bf16[2,128,1024]{2,1,0:T(8,128)(2,1)} fusion(bf16[1024,2,2,128]{0,3,2,1:T(8,128)(2,1)S(1)} %bitcast.226, f32[2,2,1024,1024]{2,3,1,0:T(8,128)} %get-tuple-element.287, f32[2,2,1024]{2,1,0:T(2,128)S(1)} %get-tuple-element.286), kind=kOutput, calls=%fused_computation.116 | convolution fusion | flops 1082392576 | bytes 18366464 | tf_op jit(solution)/shard_map/kgqt,qkgd->tkd/dot_general | solution.py:843
  722.7 10.6 %fusion.1 = (f32[2,2,1024]{2,1,0:T(2,128)S(1)}, f32[2,1024,1024,2]{2,1,3,0:T(8,128)}) fusion(f32[2,2,1024,1024]{2,3,1,0:T(8,128)} %get-tuple-element.287, f32[2,2,1024]{2,1,0:T(2,128)S(1)} %get-tuple-element.286, bf16[1024,2,2,128]{0,3,2,1:T(8,128)(2,1)S(1)} %bitcast.227, bf16[1024,2,128,1]{2,1,0,3:T(2,128)(2,1)S(1)} %bitcast.214), kind=kOutput, calls=%fused_computation.5 | convolution fusion | flops 1086320640 | bytes 35160064 | tf_op jit(solution)/shard_map/qkgd,tkd->kgqt/dot_general | solution.py:842
  733.3 12.1 %fusion.3 = bf16[2,2,1024,1024]{2,3,1,0:T(8,128)(2,1)S(1)} fusion(f32[2,1024,1024,2]{2,1,3,0:T(8,128)} %get-tuple-element.289, f32[2,2,1024]{2,1,0:T(2,128)S(1)} %get-tuple-element.288, f32[2,2,1024,1024]{2,3,1,0:T(8,128)} %get-tuple-element.287, f32[2,2,1024]{2,1,0:T(2,128)S(1)} %get-tuple-element.286), kind=kLoop, calls=%fused_computation.7 | loop fusion | flops 16777216 | bytes 41975808 | tf_op jit(solution)/shard_map/convert_element_type | solution.py:847
  821.7 12.2 %collective-permute-done.15 = bf16[256,512]{1,0:T(8,128)(2,1)} collective-permute-done((bf16[256,512]{1,0:T(8,128)(2,1)}, bf16[256,512]{1,0:T(8,128)(2,1)}, u32[]{:S(2)}, u32[]{:S(2)}) %collective-permute-start.15) | collective-permute-done | bytes 262176 | tf_op jit(solution)/shard_map/ppermute | solution.py:684
  851.7 5.3 collective-permute-done.10
  857.0 13.3 %collective-permute-done.12 = bf16[256,1024]{1,0:T(8,128)(2,1)S(1)} collective-permute-done((bf16[256,1024]{1,0:T(8,128)(2,1)S(1)}, bf16[256,1024]{1,0:T(8,128)(2,1)S(1)}, u32[]{:S(2)}, u32[]{:S(2)}) %collective-permute-start.12) | collective-permute-done | bytes 524320 | tf_op jit(solution)/shard_map/ppermute | solution.py:684
  870.2 22.5 %collective-permute-done.11 = bf16[256,1024]{1,0:T(8,128)(2,1)S(1)} collective-permute-done((bf16[256,1024]{1,0:T(8,128)(2,1)S(1)}, bf16[256,1024]{1,0:T(8,128)(2,1)S(1)}, u32[]{:S(2)}, u32[]{:S(2)}) %collective-permute-start.11) | collective-permute-done | bytes 524320 | tf_op jit(solution)/shard_map/ppermute | solution.py:684
  899.1 37.1 %all-reduce.1 = (f32[2,2048]{1,0:T(2,128)S(1)}, f32[2,128]{1,0:T(2,128)S(1)}) all-reduce(f32[2,2048]{1,0:T(2,128)S(1)} %constant_dynamic-update-slice_fusion, f32[2,128]{1,0:T(2,128)S(1)} %pad_maximum_fusion.7), channel_id=1, replica_groups=mesh['wide'=8,'narrow'=4] {'wide','narrow'}, use_global_device_ids=true, to_apply=%region_13.15 | all-reduce | flops 4352 | bytes 34816 | tf_op jit(solution)/shard_map/psum | solution.py:876
  (420 shorter events, 266.8 us)
Async XLA Ops:
  383.5 88.2 %collective-permute-start.2 = (bf16[512,2048]{1,0:T(8,128)(2,1)}, bf16[512,2048]{1,0:T(8,128)(2,1)}, u32[]{:S(2)}, u32[]{:S(2)}) collective-permute-start(bf16[512,2048]{1,0:T(8,128)(2,1)} %slice.423), channel_id=1, source_target_pairs={{0,1},{1,0},{2,3},{3,2},{4,5},{5,4},{6,7},{7,6},{8,9},{9,8},{10,11... | collective-permute-start | bytes 6291464 | tf_op jit(solution)/shard_map/ppermute | solution.py:694
  394.8 82.4 %collective-permute-start = (bf16[512,2048]{1,0:T(8,128)(2,1)}, bf16[512,2048]{1,0:T(8,128)(2,1)}, u32[]{:S(2)}, u32[]{:S(2)}) collective-permute-start(bf16[512,2048]{1,0:T(8,128)(2,1)} %slice.424), channel_id=1, source_target_pairs={{0,1},{1,0},{2,3},{3,2},{4,5},{5,4},{6,7},{7,6},{8,9},{9,8},{10,11... | collective-permute-start | bytes 6291464 | tf_op jit(solution)/shard_map/ppermute | solution.py:694
  403.5 209.5 %collective-permute-start.25 = (bf16[1024,1536]{1,0:T(8,128)(2,1)}, bf16[1024,1536]{1,0:T(8,128)(2,1)}, u32[]{:S(2)}, u32[]{:S(2)}) collective-permute-start(bf16[1024,1536]{1,0:T(8,128)(2,1)} %convolution_convert_fusion), channel_id=1, source_target_pairs={{0,4},{4,0},{8,12},{12,8},{16,20},{20,16},{24,28},{28,24},{1,5},{5... | collective-permute-start | bytes 9437192 | tf_op jit(solution)/shard_map/ppermute | solution.py:690
  409.0 132.4 %collective-permute-start.17 = (bf16[1024,1536]{1,0:T(8,128)(2,1)}, bf16[1024,1536]{1,0:T(8,128)(2,1)}, u32[]{:S(2)}, u32[]{:S(2)}) collective-permute-start(bf16[1024,1536]{1,0:T(8,128)(2,1)} %convolution_convert_fusion.2), channel_id=1, source_target_pairs={{0,4},{4,0},{8,12},{12,8},{16,20},{20,16},{24,28},{28,24},{1,5},{5... | collective-permute-start | bytes 9437192 | tf_op jit(solution)/shard_map/ppermute | solution.py:690
  414.6 192.9 %collective-permute-start.21 = (bf16[1024,1536]{1,0:T(8,128)(2,1)}, bf16[1024,1536]{1,0:T(8,128)(2,1)}, u32[]{:S(2)}, u32[]{:S(2)}) collective-permute-start(bf16[1024,1536]{1,0:T(8,128)(2,1)} %convolution_convert_fusion.1), channel_id=1, source_target_pairs={{0,4},{4,0},{8,12},{12,8},{16,20},{20,16},{24,28},{28,24},{1,5},{5... | collective-permute-start | bytes 9437192 | tf_op jit(solution)/shard_map/ppermute | solution.py:690
  476.4 25.4 %collective-permute-start.3 = (bf16[256,2048]{1,0:T(8,128)(2,1)}, bf16[256,2048]{1,0:T(8,128)(2,1)}, u32[]{:S(2)}, u32[]{:S(2)}) collective-permute-start(bf16[256,2048]{1,0:T(8,128)(2,1)} %slice.426), channel_id=1, source_target_pairs={{0,2},{1,3},{2,0},{3,1},{4,6},{5,7},{6,4},{7,5},{8,10},{9,11},{10,... | collective-permute-start | bytes 3145736 | tf_op jit(solution)/shard_map/ppermute | solution.py:694
  482.9 40.9 %collective-permute-start.1 = (bf16[256,2048]{1,0:T(8,128)(2,1)}, bf16[256,2048]{1,0:T(8,128)(2,1)}, u32[]{:S(2)}, u32[]{:S(2)}) collective-permute-start(bf16[256,2048]{1,0:T(8,128)(2,1)} %slice.427), channel_id=1, source_target_pairs={{0,2},{1,3},{2,0},{3,1},{4,6},{5,7},{6,4},{7,5},{8,10},{9,11},{10,... | collective-permute-start | bytes 3145736 | tf_op jit(solution)/shard_map/ppermute | solution.py:694
  546.7 74.8 %collective-permute-start.18 = (bf16[256,1536]{1,0:T(8,128)(2,1)S(1)}, bf16[256,1536]{1,0:T(8,128)(2,1)S(1)}, u32[]{:S(2)}, u32[]{:S(2)}) collective-permute-start(bf16[256,1536]{1,0:T(8,128)(2,1)S(1)} %get-tuple-element.247), channel_id=1, source_target_pairs={{0,8},{4,12},{8,16},{12,20},{16,24},{20,28},{24,0},{28,4},{1,9},{5... | collective-permute-start | bytes 2359304 | tf_op jit(solution)/shard_map/ppermute | solution.py:684
  546.8 77.1 %collective-permute-start.20 = (bf16[256,1536]{1,0:T(8,128)(2,1)S(1)}, bf16[256,1536]{1,0:T(8,128)(2,1)S(1)}, u32[]{:S(2)}, u32[]{:S(2)}) collective-permute-start(bf16[256,1536]{1,0:T(8,128)(2,1)S(1)} %get-tuple-element.248), channel_id=1, source_target_pairs={{0,24},{4,28},{8,0},{12,4},{16,8},{20,12},{24,16},{28,20},{1,25},{... | collective-permute-start | bytes 2359304 | tf_op jit(solution)/shard_map/ppermute | solution.py:684
  550.0 73.9 %collective-permute-start.19 = (bf16[256,1536]{1,0:T(8,128)(2,1)S(1)}, bf16[256,1536]{1,0:T(8,128)(2,1)S(1)}, u32[]{:S(2)}, u32[]{:S(2)}) collective-permute-start(bf16[256,1536]{1,0:T(8,128)(2,1)S(1)} %get-tuple-element.249), channel_id=1, source_target_pairs={{0,16},{4,20},{8,24},{12,28},{16,0},{20,4},{24,8},{28,12},{1,17},{... | collective-permute-start | bytes 2359304 | tf_op jit(solution)/shard_map/ppermute | solution.py:684
  613.0 37.5 %collective-permute-start.24 = (bf16[256,1536]{1,0:T(8,128)(2,1)S(1)}, bf16[256,1536]{1,0:T(8,128)(2,1)S(1)}, u32[]{:S(2)}, u32[]{:S(2)}) collective-permute-start(bf16[256,1536]{1,0:T(8,128)(2,1)S(1)} %get-tuple-element.251), channel_id=1, source_target_pairs={{0,24},{4,28},{8,0},{12,4},{16,8},{20,12},{24,16},{28,20},{1,25},{... | collective-permute-start | bytes 2359304 | tf_op jit(solution)/shard_map/ppermute | solution.py:684
  621.5 79.3 %collective-permute-start.23 = (bf16[256,1536]{1,0:T(8,128)(2,1)S(1)}, bf16[256,1536]{1,0:T(8,128)(2,1)S(1)}, u32[]{:S(2)}, u32[]{:S(2)}) collective-permute-start(bf16[256,1536]{1,0:T(8,128)(2,1)S(1)} %get-tuple-element.252), channel_id=1, source_target_pairs={{0,16},{4,20},{8,24},{12,28},{16,0},{20,4},{24,8},{28,12},{1,17},{... | collective-permute-start | bytes 2359304 | tf_op jit(solution)/shard_map/ppermute | solution.py:684
  623.9 83.8 %collective-permute-start.5 = (bf16[256,2048]{1,0:T(8,128)(2,1)S(1)}, bf16[256,2048]{1,0:T(8,128)(2,1)S(1)}, u32[]{:S(2)}, u32[]{:S(2)}) collective-permute-start(bf16[256,2048]{1,0:T(8,128)(2,1)S(1)} %get-tuple-element.240), channel_id=1, source_target_pairs={{0,1},{1,0},{2,3},{3,2},{4,5},{5,4},{6,7},{7,6},{8,9},{9,8},{10,11... | collective-permute-start | bytes 3145736 | tf_op jit(solution)/shard_map/ppermute | solution.py:694
  623.9 77.3 %collective-permute-start.4 = (bf16[256,2048]{1,0:T(8,128)(2,1)S(1)}, bf16[256,2048]{1,0:T(8,128)(2,1)S(1)}, u32[]{:S(2)}, u32[]{:S(2)}) collective-permute-start(bf16[256,2048]{1,0:T(8,128)(2,1)S(1)} %get-tuple-element.240), channel_id=1, source_target_pairs={{0,2},{1,3},{2,0},{3,1},{4,6},{5,7},{6,4},{7,5},{8,10},{9,11},{10,... | collective-permute-start | bytes 3145736 | tf_op jit(solution)/shard_map/ppermute | solution.py:694
  634.1 173.4 %collective-permute-start.26 = (bf16[256,1536]{1,0:T(8,128)(2,1)}, bf16[256,1536]{1,0:T(8,128)(2,1)}, u32[]{:S(2)}, u32[]{:S(2)}) collective-permute-start(bf16[256,1536]{1,0:T(8,128)(2,1)} %get-tuple-element.244), channel_id=1, source_target_pairs={{0,8},{4,12},{8,16},{12,20},{16,24},{20,28},{24,0},{28,4},{1,9},{5... | collective-permute-start | bytes 2359304 | tf_op jit(solution)/shard_map/ppermute | solution.py:684
  650.5 157.0 %collective-permute-start.28 = (bf16[256,1536]{1,0:T(8,128)(2,1)}, bf16[256,1536]{1,0:T(8,128)(2,1)}, u32[]{:S(2)}, u32[]{:S(2)}) collective-permute-start(bf16[256,1536]{1,0:T(8,128)(2,1)} %get-tuple-element.245), channel_id=1, source_target_pairs={{0,24},{4,28},{8,0},{12,4},{16,8},{20,12},{24,16},{28,20},{1,25},{... | collective-permute-start | bytes 2359304 | tf_op jit(solution)/shard_map/ppermute | solution.py:684
  700.8 110.0 %collective-permute-start.27 = (bf16[256,1536]{1,0:T(8,128)(2,1)}, bf16[256,1536]{1,0:T(8,128)(2,1)}, u32[]{:S(2)}, u32[]{:S(2)}) collective-permute-start(bf16[256,1536]{1,0:T(8,128)(2,1)} %get-tuple-element.246), channel_id=1, source_target_pairs={{0,16},{4,20},{8,24},{12,28},{16,0},{20,4},{24,8},{28,12},{1,17},{... | collective-permute-start | bytes 2359304 | tf_op jit(solution)/shard_map/ppermute | solution.py:684
  756.5 42.8 %collective-permute-start.13 = (bf16[1024,512]{1,0:T(8,128)(2,1)}, bf16[1024,512]{1,0:T(8,128)(2,1)}, u32[]{:S(2)}, u32[]{:S(2)}) collective-permute-start(bf16[1024,512]{1,0:T(8,128)(2,1)} %fusion.62), channel_id=1, source_target_pairs={{0,4},{4,0},{8,12},{12,8},{16,20},{20,16},{24,28},{28,24},{1,5},{5... | collective-permute-start | bytes 3145736 | tf_op jit(solution)/shard_map/ppermute | solution.py:690
  791.8 46.7 %collective-permute-start.9 = (bf16[1024,1024]{1,0:T(8,128)(2,1)}, bf16[1024,1024]{1,0:T(8,128)(2,1)}, u32[]{:S(2)}, u32[]{:S(2)}) collective-permute-start(bf16[1024,1024]{1,0:T(8,128)(2,1)} %fusion.42), channel_id=1, source_target_pairs={{0,4},{4,0},{8,12},{12,8},{16,20},{20,16},{24,28},{28,24},{1,5},{5... | collective-permute-start | bytes 6291464 | tf_op jit(solution)/shard_map/ppermute | solution.py:690
  802.6 45.4 %collective-permute-start.7 = (bf16[512,2048]{1,0:T(8,128)(2,1)}, bf16[512,2048]{1,0:T(8,128)(2,1)}, u32[]{:S(2)}, u32[]{:S(2)}) collective-permute-start(bf16[512,2048]{1,0:T(8,128)(2,1)} %slice.422), channel_id=1, source_target_pairs={{0,1},{1,0},{2,3},{3,2},{4,5},{5,4},{6,7},{7,6},{8,9},{9,8},{10,11... | collective-permute-start | bytes 6291464 | tf_op jit(solution)/shard_map/ppermute | solution.py:694
  810.9 23.0 %collective-permute-start.15 = (bf16[256,512]{1,0:T(8,128)(2,1)}, bf16[256,512]{1,0:T(8,128)(2,1)}, u32[]{:S(2)}, u32[]{:S(2)}) collective-permute-start(bf16[256,512]{1,0:T(8,128)(2,1)} %get-tuple-element.265), channel_id=1, source_target_pairs={{0,16},{4,20},{8,24},{12,28},{16,0},{20,4},{24,8},{28,12},{1,17},{... | collective-permute-start | bytes 786440 | tf_op jit(solution)/shard_map/ppermute | solution.py:684
  843.4 26.9 %collective-permute-start.12 = (bf16[256,1024]{1,0:T(8,128)(2,1)S(1)}, bf16[256,1024]{1,0:T(8,128)(2,1)S(1)}, u32[]{:S(2)}, u32[]{:S(2)}) collective-permute-start(bf16[256,1024]{1,0:T(8,128)(2,1)S(1)} %get-tuple-element.254), channel_id=1, source_target_pairs={{0,24},{4,28},{8,0},{12,4},{16,8},{20,12},{24,16},{28,20},{1,25},{... | collective-permute-start | bytes 1572872 | tf_op jit(solution)/shard_map/ppermute | solution.py:684
  846.6 46.1 %collective-permute-start.11 = (bf16[256,1024]{1,0:T(8,128)(2,1)S(1)}, bf16[256,1024]{1,0:T(8,128)(2,1)S(1)}, u32[]{:S(2)}, u32[]{:S(2)}) collective-permute-start(bf16[256,1024]{1,0:T(8,128)(2,1)S(1)} %get-tuple-element.255), channel_id=1, source_target_pairs={{0,16},{4,20},{8,24},{12,28},{16,0},{20,4},{24,8},{28,12},{1,17},{... | collective-permute-start | bytes 1572872 | tf_op jit(solution)/shard_map/ppermute | solution.py:684
  851.6 44.8 %collective-permute-start.8 = (bf16[256,2048]{1,0:T(8,128)(2,1)S(1)}, bf16[256,2048]{1,0:T(8,128)(2,1)S(1)}, u32[]{:S(2)}, u32[]{:S(2)}) collective-permute-start(bf16[256,2048]{1,0:T(8,128)(2,1)S(1)} %slice.425), channel_id=1, source_target_pairs={{0,2},{1,3},{2,0},{3,1},{4,6},{5,7},{6,4},{7,5},{8,10},{9,11},{10,... | collective-permute-start | bytes 3145736 | tf_op jit(solution)/shard_map/ppermute | solution.py:694
  (105 other events, 1191.5 us)

commit v2 on v1

v2 whole, which is shorter than its diff:
```python
import functools

import jax
import jax.numpy as jnp
from jax import lax
from jax.experimental import pallas as pl
from jax.experimental.pallas import tpu as pltpu
from jax.sharding import PartitionSpec as P

HD = 128
STEP = 5
MESH = pl.DeviceIdType.MESH
MIB = 2**20

norm_eps = 1e-06
rope_base = 1000000.0
beta_first = 0.5
beta_second = 0.5
adam_eps = 1e-08
weight_decay = 0.1
masked_fill = -1e30
f32 = jnp.float32
bf16 = jnp.bfloat16


def row_scale(values):
    return lax.rsqrt(jnp.mean(values * values, axis=-1, keepdims=True) + norm_eps)


def norm_back(grad, unit, scale, gain):
    scaled = grad * gain
    return scale * (scaled - unit * jnp.mean(scaled * unit, axis=-1, keepdims=True))


def adamw(weight, first, second, grad, rate):
    first_new = beta_first * first + (1.0 - beta_first) * grad
    second_new = beta_second * second + (1.0 - beta_second) * grad * grad
    first_hat = first_new / (1.0 - beta_first**STEP)
    second_hat = second_new / (1.0 - beta_second**STEP)
    weight_new = weight - rate * (
        first_hat / (jnp.sqrt(second_hat) + adam_eps) + weight_decay * weight
    )
    return (weight_new, first_new, second_new)


def rope_tables(length):
    half = HD // 2
    freqs = rope_base ** (-(jnp.arange(half, dtype=f32) * 2.0) / HD)
    angles = jnp.arange(length, dtype=f32)[:, None] * freqs[None, :]
    cosine = jnp.cos(angles)
    sine = jnp.sin(angles)
    return (
        jnp.concatenate([cosine, cosine], axis=-1),
        jnp.concatenate([-sine, sine], axis=-1),
    )


def dot_nn(left, right):
    return lax.dot_general(left, right, (((1,), (0,)), ((), ())), preferred_element_type=f32)


def dot_nt(left, right):
    return lax.dot_general(left, right, (((1,), (1,)), ((), ())), preferred_element_type=f32)


def dot_tn(left, right):
    return lax.dot_general(left, right, (((0,), (0,)), ((), ())), preferred_element_type=f32)


def loop(count, step):
    def body(index, carry):
        step(index)
        return carry

    lax.fori_loop(0, count, body, 0)


def rows(index, size):
    return pl.ds(pl.multiple_of(index * size, size), size)


class Place:
    def __init__(self, wide, narrow):
        self.depth = wide // 2
        w = lax.axis_index("wide")
        n = lax.axis_index("narrow")
        self.w, self.n = w, n
        self.z = w // 2
        self.x = w - 2 * self.z
        self.y = n // 2
        self.c = n - 2 * self.y
        self.known = {(k, dx): self.reach(k, dx) for k in range(self.depth) for dx in (0, 1)}
        self.sides = {}
        for dy in (0, 1):
            for dc in (0, 1):
                y = self.y if dy == 0 else 1 - self.y
                c = self.c if dc == 0 else 1 - self.c
                self.sides[dy, dc] = (w, y * 2 + c)

    def reach(self, k, dx):
        x = self.x if dx == 0 else 1 - self.x
        return (lax.rem(self.z + k, self.depth) * 2 + x, self.n)

    def far(self, k, dx):
        return self.known[k, dx] if isinstance(k, int) else self.reach(k, dx)

    def side(self, dy, dc):
        return self.sides[dy, dc]

    def slot(self, block):
        ay, ac = block // 2, block % 2
        dy = lax.rem(self.y + ay, 2)
        dc = lax.rem(self.c + ac, 2)
        return dc * 2 + dy


def remote(src, dst, send, recv, device):
    return pltpu.make_async_remote_copy(
        src_ref=src,
        dst_ref=dst,
        send_sem=send,
        recv_sem=recv,
        device_id=device,
        device_id_type=MESH,
    )


class Side:
    def __init__(self, place, send, recv):
        self.place = place
        self.send = [send.at[i] for i in range(send.shape[0])]
        self.recv = [recv.at[i] for i in range(recv.shape[0])]
        self.used = 0
        self.sent = []

    def copy(self, src, dst, dy, dc):
        i = self.used
        self.used += 1
        made = remote(src, dst, self.send[i], self.recv[i], self.place.side(dy, dc))
        made.start()
        self.sent.append(made)
        return made

    def drain(self):
        for made in self.sent:
            made.wait_send()
        self.sent = []


class Gather:
    def __init__(self, side, own, buf, size):
        self.side, self.buf, self.size = side, buf, size
        self.across = side.copy(own, buf.at[pl.ds(size, size)], 1, 0)
        self.core = side.copy(own, buf.at[pl.ds(2 * size, size)], 0, 1)

    def forward(self):
        size = self.size
        self.across.wait_recv()
        self.last = self.side.copy(
            self.buf.at[pl.ds(size, size)], self.buf.at[pl.ds(3 * size, size)], 0, 1
        )

    def done(self):
        self.core.wait_recv()
        self.last.wait_recv()


class Wide:
    def __init__(self, place, block, chunks, own, full, zs, zr, xs, xr):
        self.place, self.block, self.chunks, self.own, self.full = place, block, chunks, own, full
        self.zs, self.zr, self.xs, self.xr = zs, zr, xs, xr
        self.near = place.depth == 4

    def slot(self, i, index):
        g, a, b = self.chunks[i]
        return self.full[g].at[pl.ds(index * self.block, self.block), pl.ds(a, b - a)]

    def mine(self, i):
        g, a, b = self.chunks[i]
        return self.own[g].at[:, pl.ds(a, b - a)]

    def along(self, i, k):
        depth = self.place.depth
        return remote(
            self.mine(i),
            self.slot(i, k),
            self.zs.at[i, k],
            self.zr.at[i, k],
            self.place.far(depth - k, 0),
        )

    def beyond(self, i, k):
        depth = self.place.depth
        return remote(
            self.slot(i, 2),
            self.slot(i, k),
            self.zs.at[i, depth + k],
            self.zr.at[i, k],
            self.place.far(1 if k == 1 else depth - 1, 0),
        )

    def across(self, i, k):
        depth = self.place.depth
        src = self.mine(i) if k == 0 else self.slot(i, k)
        return remote(
            src, self.slot(i, depth + k), self.xs.at[i, k], self.xr.at[i, k], self.place.far(0, 1)
        )

    def each(self, i, k, act):
        place = self.place
        if self.near and k in (1, 3):
            at_end = (place.z == 0) if k == 1 else (place.z == 3)

            @pl.when(jnp.logical_not(at_end))
            def _():
                act(self.along(i, k))
        else:
            act(self.along(i, k))

    def order(self):
        depth = self.place.depth
        return (2, 1, 3) if self.near else tuple(range(1, depth))

    def issue(self, i):
        if i >= len(self.chunks):
            return
        self.across(i, 0).start()
        for k in self.order():
            self.each(i, k, lambda made: made.start())

    def hand_on(self, i):
        z = self.place.z
        for k in self.order():
            self.along(i, k).wait_recv()
            if self.near and k == 2:

                @pl.when(z == 2)
                def _():
                    self.beyond(i, 1).start()

                @pl.when(z == 1)
                def _():
                    self.beyond(i, 3).start()

            self.across(i, k).start()

    def arrived(self, i):
        for k in range(self.place.depth):
            self.across(i, k).wait_recv()

    def drain(self):
        z = self.place.z
        for i in range(len(self.chunks)):
            for k in range(self.place.depth):
                if k:
                    self.each(i, k, lambda made: made.wait_send())
                if self.near and k in (1, 3):

                    @pl.when(z == (2 if k == 1 else 1))
                    def _():
                        self.beyond(i, k).wait_send()

                self.across(i, k).wait_send()


def greet(place):
    depth = place.depth
    peers = [place.far(k, dx) for dx in (0, 1) for k in range(depth) if k or dx]
    peers += [place.side(1, 0), place.side(0, 1)]
    barrier = pltpu.get_barrier_semaphore()
    for peer in peers:
        pl.semaphore_signal(barrier, inc=1, device_id=peer, device_id_type=MESH)
    pl.semaphore_wait(barrier, len(peers))


def turn(values):
    return pltpu.roll(values, HD // 2, 1)


def rope(values, cosine, sine):
    return values * cosine + turn(values) * sine


def rope_back(grads, cosine, sine):
    return grads * cosine - turn(grads) * sine


def softmax_block(query, keys, block, size, count, length):
    scores = dot_nt(query, keys) * HD ** (-0.5)
    shape = scores.shape
    at = block * size + lax.broadcasted_iota(jnp.int32, shape, 0)
    to = lax.broadcasted_iota(jnp.int32, shape, 1)
    scores = jnp.where((to <= at) & (to < length), scores, masked_fill)
    lifted = jnp.exp(scores - jnp.max(scores, axis=-1, keepdims=True))
    return lifted / jnp.sum(lifted, axis=-1, keepdims=True)


def chunks_of(widths):
    qkv, out, gate, up, down = widths
    return [
        (0, 0, qkv // 2),
        (0, qkv // 2, qkv),
        (1, 0, out),
        (2, 0, gate // 2),
        (3, 0, up // 2),
        (2, gate // 2, gate),
        (3, up // 2, up),
        (4, 0, down // 2),
        (4, down // 2, down),
    ]


def layer_kernel(
    wide,
    heads,
    pairs,
    length_ref,
    x_ref,
    gain_ref,
    cos_ref,
    sin_ref,
    dyb_ref,
    own_qkv,
    own_out,
    own_gate,
    own_up,
    own_down,
    o_out,
    o_grad,
    o_norm,
    o_head,
    home_qkv,
    home_out,
    home_gate,
    home_up,
    home_down,
    come_qkv,
    come_out,
    come_gate,
    come_up,
    come_down,
    full_qkv,
    full_out,
    full_gate,
    full_up,
    full_down,
    away_qkv,
    away_out,
    away_gate,
    away_up,
    away_down,
    got_qkv,
    got_out,
    got_gate,
    got_up,
    got_down,
    all_dyb,
    all_normed,
    all_qkv,
    all_dresb,
    slots,
    gains,
    head_gain,
    ctx,
    resid,
    total,
    mixed,
    hidden,
    weights,
    tokens,
    feed_grad,
    stage,
    arrived_tile,
    half_out,
    half_in,
    cross_out,
    cross_in,
    sums,
    sums_in,
    head_sums,
    head_sums_in,
    last_norm,
    last_head,
    zs,
    zr,
    xs,
    xr,
    ns,
    nr,
    gs,
    gr,
    ls,
    rxs,
    rxr,
    rzs,
    rzr,
    stage_sem,
    tile_sem,
    free_core,
    free_other,
):
    place = Place(wide, 4)
    depth = place.depth
    size, width = x_ref.shape
    block = width // wide
    ff = hidden.shape[1]
    groups = heads // pairs
    span = 4 * size
    own = [own_qkv, own_out, own_gate, own_up, own_down]
    full = [full_qkv, full_out, full_gate, full_up, full_down]
    away = [away_qkv, away_out, away_gate, away_up, away_down]
    got = [got_qkv, got_out, got_gate, got_up, got_down]
    home = [home_qkv, home_out, home_gate, home_up, home_down]
    come = [come_qkv, come_out, come_gate, come_up, come_down]
    qkv_width = full_qkv.shape[1]
    out_width = full_out.shape[1]
    chunks = chunks_of([ref.shape[1] for ref in full])
    greet(place)
    ag = Wide(place, block, chunks, own, full, zs, zr, xs, xr)
    side = Side(place, ns, nr)
    copies = []
    quarter = size // 4

    def keep(src, dst):
        made = pltpu.make_async_copy(src, dst, ls.at[len(copies)])
        made.start()
        copies.append(made)
        return made

    def fetch(*pairs_of):
        made = [keep(src, dst) for src, dst in pairs_of]
        for one in made:
            one.wait()

    gain_copies = []
    for dx in (0, 1):
        for k in range(depth):
            if k or dx:
                at = dx * depth + (depth - k) % depth
                made = remote(gain_ref, slots.at[at], gs.at[at], gr.at[at], place.far(k, dx))
                made.start()
                gain_copies.append(made)
    for i in range(3):
        ag.issue(i)
    own_copies = [keep(own[g], full[g].at[pl.ds(0, block)]) for g in range(5)]
    dyb_copy = keep(dyb_ref, all_dyb.at[pl.ds(0, size)])
    slots[0] = gain_ref[...]
    for made in gain_copies:
        made.wait_recv()
    gains[...] = jnp.concatenate([slots[b][:, :block] for b in range(wide)], axis=1)
    heads_row = slots[0][:, :HD]
    for b in range(1, wide):
        heads_row = heads_row + slots[b][:, :HD]
    head_gain[...] = heads_row

    def first_norm(i):
        at = rows(i, quarter)
        x = x_ref[at, :].astype(f32)
        cross_out[at, :] = (x * row_scale(x) * gains[0:1, :]).astype(bf16)

    loop(4, first_norm)
    take_normed = Gather(side, cross_out, all_normed, size)
    normed_copy = keep(cross_out, all_normed.at[pl.ds(0, size)])
    take_dyb = Gather(side, dyb_ref, all_dyb, size)
    take_normed.forward()
    ag.hand_on(0)
    ag.issue(3)
    take_dyb.forward()
    take_normed.done()
    normed_copy.wait()
    ag.hand_on(1)
    ag.issue(4)
    ag.arrived(0)
    ag.arrived(1)
    own_copies[0].wait()
    length = length_ref[0]

    def keys_of(p, qkv, k_act, v_act):
        for a in range(4):
            at = rows(place.slot(a), size)
            to = pl.ds(a * size, size)
            raw = qkv[at, pl.ds(pl.multiple_of((heads + p) * HD, HD), HD)]
            unit = raw * row_scale(raw) * head_gain[3:4, :]
            k_act[to, :] = rope(unit, cos_ref[to, :], sin_ref[to, :]).astype(bf16)
            v_act[to, :] = qkv[
                at, pl.ds(pl.multiple_of((heads + pairs + p) * HD, HD), HD)
            ].astype(bf16)

    def attention(normed, qkv, k_act, v_act):
        fetch((all_normed, normed), (full_qkv, weights.at[:, pl.ds(0, qkv_width)]))

        def project(m):
            for n in range(qkv_width // 512):
                qkv[rows(m, size), pl.ds(n * 512, 512)] = dot_nn(
                    normed[rows(m, size), :], weights[:, pl.ds(n * 512, 512)]
                )

        loop(4, project)
        qkv_copy = keep(qkv, all_qkv)
        ag.hand_on(2)
        ag.issue(5)

        def pair(p):
            keys_of(p, qkv, k_act, v_act)

            def head(g):
                column = pl.ds(pl.multiple_of((p * groups + g) * HD, HD), HD)
                for a in range(4):
                    at = rows(place.slot(a), size)
                    to = pl.ds(a * size, size)
                    raw = qkv[at, column]
                    unit = raw * row_scale(raw) * head_gain[2:3, :]
                    query = rope(unit, cos_ref[to, :], sin_ref[to, :]).astype(bf16)
                    last = (a + 1) * size
                    probs = softmax_block(query, k_act[0:last, :], a, size, last, length)
                    ctx[at, column] = dot_nn(probs.astype(bf16), v_act[0:last, :]).astype(bf16)

            loop(groups, head)

        loop(pairs, pair)
        qkv_copy.wait()

    pl.run_scoped(
        attention,
        pltpu.VMEM((span, width), bf16),
        pltpu.VMEM((span, qkv_width), f32),
        pltpu.VMEM((span, HD), bf16),
        pltpu.VMEM((span, HD), bf16),
    )
    ag.hand_on(3)
    ag.issue(6)
    ag.arrived(2)
    own_copies[1].wait()
    fetch((full_out, weights.at[:, pl.ds(0, out_width)]))
    step = 512

    def scatter(tile):
        def to_core(n):
            half_out[:, rows(n, step)] = tile(2 * size, 2 * size, n).astype(bf16)

        loop(width // step, to_core)
        core = side.copy(half_out, half_in, 0, 1)

        def to_self(n):
            total[:, rows(n, step)] = tile(0, size, n)

        loop(width // step, to_self)
        core.wait_recv()

        def to_other(n):
            at = rows(n, step)
            part = tile(size, size, n) + half_in[pl.ds(size, size), at].astype(f32)
            cross_out[:, at] = part.astype(bf16)

        loop(width // step, to_other)
        other = side.copy(cross_out, cross_in, 1, 0)
        total[...] += half_in[pl.ds(0, size), :].astype(f32)
        return other

    def out_tile(start, count, n):
        return dot_nt(ctx[pl.ds(start, count), :], weights[rows(n, step), pl.ds(0, out_width)])

    side.drain()
    other = scatter(out_tile)
    other.wait_recv()

    def second_norm(i):
        at = rows(i, quarter)
        value = x_ref[at, :].astype(f32) + total[at, :] + cross_in[at, :].astype(f32)
        resid[at, :] = value
        mixed[at, :] = (value * row_scale(value) * gains[1:2, :]).astype(bf16)

    loop(4, second_norm)
    take_mixed = Gather(side, mixed.at[pl.ds(0, size)], mixed, size)
    ag.hand_on(4)
    ag.issue(7)
    take_mixed.forward()
    take_mixed.done()
    take_dyb.done()
    dyb_copy.wait()
    fetch((all_dyb, tokens))
    ag.hand_on(5)
    ag.issue(8)
    half = ff // 2
    tile = 256

    piece = max(block, HD)
    steps = depth * block // piece
    held = piece // block

    def staged(g, slot, to):
        return pltpu.make_async_copy(
            stage.at[slot, :, pl.ds(0, full[g].shape[1])], to, stage_sem.at[slot]
        )

    def part_of(ref, t):
        return ref.at[rows(t, piece)]

    def cross(g, t):
        return remote(
            part_of(away[g], t), part_of(got[g], t), rxs.at[g, t], rxr.at[g, t], place.far(0, 1)
        )

    def hand_over(g, k):
        return remote(
            home[g].at[rows(k, block)],
            come[g].at[rows(k - 1, block)],
            rzs.at[g, k],
            rzr.at[g, k],
            place.far(k, 0),
        )

    def send_away(g, left, right):
        wide_g = full[g].shape[1]

        def finish(t):
            staged(g, lax.rem(t, 2), part_of(away[g], t)).wait()
            cross(g, t).start()

        def one(t):
            made = dot_tn(left[:, rows(steps + t, piece)], right())
            stage[lax.rem(t, 2), :, pl.ds(0, wide_g)] = made.astype(bf16)

            @pl.when(t > 0)
            def _():
                finish(t - 1)

            staged(g, lax.rem(t, 2), part_of(away[g], t)).start()

        loop(steps, one)
        finish(steps - 1)

    def send_home(g, left, right):
        wide_g = full[g].shape[1]

        def finish(j):
            t = lax.rem(j + 1, steps)
            staged(g, lax.rem(j, 2), part_of(home[g], t)).wait()
            for r in range(held):
                k = t * held + r

                @pl.when(k > 0)
                def _(k=k):
                    hand_over(g, k).start()

        def one(j):
            t = lax.rem(j + 1, steps)
            cross(g, t).wait_recv()
            get = pltpu.make_async_copy(
                part_of(got[g], t), arrived_tile.at[:, pl.ds(0, wide_g)], tile_sem
            )
            get.start()
            made = dot_tn(left[:, rows(t, piece)], right())
            get.wait()
            made = made + arrived_tile[:, pl.ds(0, wide_g)].astype(f32)
            stage[lax.rem(j, 2), :, pl.ds(0, wide_g)] = made.astype(bf16)

            @pl.when(j > 0)
            def _():
                finish(j - 1)

            staged(g, lax.rem(j, 2), part_of(home[g], t)).start()

        loop(steps, one)
        finish(steps - 1)

    def feed_forward(gate, up):
        def feed(part):
            a = part * half
            fetch(
                (full_gate.at[:, pl.ds(a, half)], weights.at[:, pl.ds(0, half)]),
                (full_up.at[:, pl.ds(a, half)], weights.at[:, pl.ds(half, half)]),
            )

            def columns(n):
                def body(m):
                    at = rows(m, size)
                    left = mixed[at, :]
                    gate_part = dot_nn(left, weights[:, rows(n, tile)])
                    up_part = dot_nn(
                        left, weights[:, pl.ds(pl.multiple_of(half + n * tile, tile), tile)]
                    )
                    to = pl.ds(pl.multiple_of(a + n * tile, tile), tile)
                    gate[at, to] = gate_part
                    up[at, to] = up_part
                    hidden[at, to] = (gate_part * jax.nn.sigmoid(gate_part) * up_part).astype(bf16)

                loop(4, body)

            loop(half // tile, columns)

        own_copies[2].wait()
        own_copies[3].wait()
        ag.arrived(3)
        ag.arrived(4)
        feed(0)
        ag.hand_on(6)
        ag.arrived(5)
        ag.arrived(6)
        feed(1)
        send_away(4, tokens, lambda: hidden[...])
        ag.hand_on(7)
        ag.hand_on(8)
        ag.arrived(7)
        ag.arrived(8)
        own_copies[4].wait()
        fetch((full_down, weights))

        def columns(n):
            def body(m):
                at = rows(m, size)
                to = rows(n, tile)
                grad = dot_nn(tokens[at, :], weights[:, to])
                gate_part = gate[at, to]
                up_part = up[at, to]
                sigma = jax.nn.sigmoid(gate_part)
                feed_grad[at, to] = (
                    grad * up_part * sigma * (1.0 + gate_part * (1.0 - sigma))
                ).astype(bf16)
                feed_grad[at, pl.ds(pl.multiple_of(ff + n * tile, tile), tile)] = (
                    grad * gate_part * sigma
                ).astype(bf16)

            loop(4, body)

        loop(ff // tile, columns)

    pl.run_scoped(feed_forward, pltpu.VMEM((span, ff), f32), pltpu.VMEM((span, ff), f32))

    def mixed_grad(both):
        fetch(
            (full_gate, both.at[:, pl.ds(0, ff)]),
            (full_up, both.at[:, pl.ds(ff, ff)]),
        )

        def mixed_tile(start, count, n):
            return dot_nt(feed_grad[pl.ds(start, count), :], both[rows(n, step), :])

        side.drain()
        scattered.append(scatter(mixed_tile))

    scattered = []
    pl.run_scoped(mixed_grad, pltpu.VMEM((width, 2 * ff), bf16))
    other = scattered[0]
    send_away(2, mixed, lambda: feed_grad[:, pl.ds(0, ff)])
    other.wait_recv()
    sums[...] = jnp.zeros_like(sums)
    head_sums[...] = jnp.zeros_like(head_sums)

    def second_back(i):
        at = rows(i, quarter)
        value = resid[at, :]
        scale = row_scale(value)
        unit = value * scale
        grad = total[at, :] + cross_in[at, :].astype(f32)
        sums[1:2, :] += jnp.sum(grad * unit, axis=0, keepdims=True)
        back = norm_back(grad, unit, scale, gains[1:2, :])
        result = dyb_ref[at, :].astype(f32) + back
        o_grad[at, :] = result
        cross_out[at, :] = result.astype(bf16)

    side.drain()
    loop(4, second_back)
    take_dresb = Gather(side, cross_out, all_dresb, size)
    dresb_copy = keep(cross_out, all_dresb.at[pl.ds(0, size)])
    send_away(3, mixed, lambda: feed_grad[:, pl.ds(ff, ff)])
    take_dresb.forward()
    send_home(4, tokens, lambda: hidden[...])
    take_dresb.done()
    dresb_copy.wait()

    def down_tile(start, count, n):
        return dot_nt(hidden[pl.ds(start, count), :], weights[rows(n, step), :])

    side.drain()
    other = scatter(down_tile)
    other.wait_recv()
    o_out[...] = (resid[...] + total[...] + cross_in[...].astype(f32)).astype(bf16)
    pl.semaphore_signal(free_core, inc=1, device_id=place.side(0, 1), device_id_type=MESH)
    pl.semaphore_signal(free_other, inc=1, device_id=place.side(1, 0), device_id_type=MESH)

    def attention_back(qkv, k_act, v_act, ctx_grad, qkv_grad, k_grad, v_grad):
        fetch(
            (all_dresb, tokens),
            (all_qkv, qkv),
            (full_out, weights.at[:, pl.ds(0, out_width)]),
        )
        send_away(1, tokens, lambda: ctx[...])

        def context_grad(m):
            ctx_grad[rows(m, size), :] = dot_nn(
                tokens[rows(m, size), :], weights[:, pl.ds(0, out_width)]
            ).astype(bf16)

        loop(4, context_grad)

        def head_back(raw, grad, gain, a):
            to = pl.ds(a * size, size)
            scale = row_scale(raw)
            unit = raw * scale
            turned = rope_back(grad, cos_ref[to, :], sin_ref[to, :])
            gain_part = jnp.sum(turned * unit, axis=0, keepdims=True)
            return norm_back(turned, unit, scale, gain).astype(bf16), gain_part

        def pair(p):
            keys_of(p, qkv, k_act, v_act)
            k_grad[...] = jnp.zeros_like(k_grad)
            v_grad[...] = jnp.zeros_like(v_grad)

            def head(g):
                column = pl.ds(pl.multiple_of((p * groups + g) * HD, HD), HD)
                for a in range(4):
                    at = rows(place.slot(a), size)
                    to = pl.ds(a * size, size)
                    last = (a + 1) * size
                    raw = qkv[at, column]
                    unit = raw * row_scale(raw) * head_gain[2:3, :]
                    query = rope(unit, cos_ref[to, :], sin_ref[to, :]).astype(bf16)
                    probs = softmax_block(query, k_act[0:last, :], a, size, last, length)
                    grad = ctx_grad[at, column]
                    probs_grad = dot_nt(grad, v_act[0:last, :])
                    v_grad[0:last, :] += dot_tn(probs.astype(bf16), grad)
                    delta = jnp.sum(probs * probs_grad, axis=-1, keepdims=True)
                    scores_grad = (probs * (probs_grad - delta)).astype(bf16)
                    query_grad = dot_nn(scores_grad, k_act[0:last, :]) * HD ** (-0.5)
                    k_grad[0:last, :] += dot_tn(scores_grad, query) * HD ** (-0.5)
                    made, gain_part = head_back(raw, query_grad, head_gain[2:3, :], a)
                    qkv_grad[at, column] = made
                    head_sums[0:1, :] += gain_part

            loop(groups, head)
            for a in range(4):
                at = rows(place.slot(a), size)
                to = pl.ds(a * size, size)
                column = pl.ds(pl.multiple_of((heads + p) * HD, HD), HD)
                made, gain_part = head_back(
                    qkv[at, column], k_grad[to, :], head_gain[3:4, :], a
                )
                qkv_grad[at, column] = made
                head_sums[1:2, :] += gain_part
                column = pl.ds(pl.multiple_of((heads + pairs + p) * HD, HD), HD)
                qkv_grad[at, column] = v_grad[to, :].astype(bf16)

        loop(pairs, pair)
        send_home(1, tokens, lambda: ctx[...])
        fetch((all_normed, tokens), (full_qkv, weights.at[:, pl.ds(0, qkv_width)]))
        send_away(0, tokens, lambda: qkv_grad[...])

        def normed_tile(start, count, n):
            return dot_nt(
                qkv_grad[pl.ds(start, count), :], weights[rows(n, step), pl.ds(0, qkv_width)]
            )

        side.drain()
        pl.semaphore_wait(free_core, 1)
        pl.semaphore_wait(free_other, 1)
        other = scatter(normed_tile)
        send_home(2, mixed, lambda: feed_grad[:, pl.ds(0, ff)])
        other.wait_recv()

        def first_back(i):
            at = rows(i, quarter)
            value = x_ref[at, :].astype(f32)
            scale = row_scale(value)
            unit = value * scale
            grad = total[at, :] + cross_in[at, :].astype(f32)
            sums[0:1, :] += jnp.sum(grad * unit, axis=0, keepdims=True)
            o_grad[at, :] += norm_back(grad, unit, scale, gains[0:1, :])

        loop(4, first_back)

        for flip, (dy, dc) in enumerate(((0, 1), (1, 0))):
            norm_made = side.copy(sums, sums_in.at[flip], dy, dc)
            head_made = side.copy(head_sums, head_sums_in.at[flip], dy, dc)
            norm_made.wait_recv()
            head_made.wait_recv()
            side.drain()
            sums[...] += sums_in[flip]
            head_sums[...] += head_sums_in[flip]
        for made in gain_copies:
            made.wait_send()
        for b in range(wide):
            slots[b, :, 0:block] = sums[:, b * block : (b + 1) * block]
        last = []
        for dx in (0, 1):
            for k in range(depth):
                if k or dx:
                    to = dx * depth + k
                    at = dx * depth + (depth - k) % depth
                    made = remote(
                        slots.at[to], last_norm.at[at], gs.at[at], gr.at[at], place.far(k, dx)
                    )
                    made.start()
                    last.append(made)
                    made = remote(
                        head_sums,
                        last_head.at[at],
                        gs.at[wide + at],
                        gr.at[wide + at],
                        place.far(k, dx),
                    )
                    made.start()
                    last.append(made)
        send_home(3, mixed, lambda: feed_grad[:, pl.ds(ff, ff)])
        send_home(0, tokens, lambda: qkv_grad[...])
        for made in last:
            made.wait_recv()
        norm_total = slots[0]
        head_total = head_sums[...]
        for b in range(1, wide):
            norm_total = norm_total + last_norm[b]
            head_total = head_total + last_head[b]
        o_norm[...] = norm_total
        o_head[...] = head_total
        for made in last:
            made.wait_send()

    pl.run_scoped(
        attention_back,
        pltpu.VMEM((span, qkv_width), f32),
        pltpu.VMEM((span, HD), bf16),
        pltpu.VMEM((span, HD), bf16),
        pltpu.VMEM((span, out_width), bf16),
        pltpu.VMEM((span, qkv_width), bf16),
        pltpu.VMEM((span, HD), f32),
        pltpu.VMEM((span, HD), f32),
    )
    for g in range(5):
        for t in range(steps):
            cross(g, t).wait_send()
        for k in range(1, depth):
            hand_over(g, k).wait()
    side.drain()
    ag.drain()


def layer_call(lengths, x, gain, cosine, sine, dyb, own, heads, pairs):
    wide = lax.axis_size("wide")
    depth = wide // 2
    size, width = x.shape
    span = 4 * size
    block = width // wide
    ff = own[2].shape[1]
    widths = [w.shape[1] for w in own]
    lanes = gain.shape[1]
    shape = jax.ShapeDtypeStruct
    anywhere = pl.BlockSpec(memory_space=pl.ANY)
    vmem = pl.BlockSpec(memory_space=pltpu.VMEM)
    count = len(chunks_of(widths))
    outs = [
        shape((size, width), bf16),
        shape((size, width), f32),
        shape((8, lanes), f32),
        shape((8, HD), f32),
    ]
    outs += [shape((width // 2, w), bf16) for w in widths]
    outs += [shape(((depth - 1) * block, w), bf16) for w in widths]
    outs += [shape((width, w), bf16) for w in widths]
    outs += [shape((width // 2, w), bf16) for w in widths] * 2
    outs += [
        shape((span, width), bf16),
        shape((span, width), bf16),
        shape((span, widths[0]), f32),
        shape((span, width), bf16),
    ]
    dma = pltpu.SemaphoreType.DMA
    return pl.pallas_call(
        functools.partial(layer_kernel, wide, heads, pairs),
        out_shape=outs,
        in_specs=[pl.BlockSpec(memory_space=pltpu.SMEM)] + [vmem] * 5 + [anywhere] * 5,
        out_specs=[vmem] * 4 + [anywhere] * (len(outs) - 4),
        scratch_shapes=[
            pltpu.VMEM((wide, 8, lanes), f32),
            pltpu.VMEM((8, width), f32),
            pltpu.VMEM((8, HD), f32),
            pltpu.VMEM((span, widths[1]), bf16),
            pltpu.VMEM((size, width), f32),
            pltpu.VMEM((size, width), f32),
            pltpu.VMEM((span, width), bf16),
            pltpu.VMEM((span, ff), bf16),
            pltpu.VMEM((width, ff), bf16),
            pltpu.VMEM((span, width), bf16),
            pltpu.VMEM((span, 2 * ff), bf16),
            pltpu.VMEM((2, max(block, HD), max(widths)), bf16),
            pltpu.VMEM((max(block, HD), max(widths)), bf16),
            pltpu.VMEM((2 * size, width), bf16),
            pltpu.VMEM((2 * size, width), bf16),
            pltpu.VMEM((size, width), bf16),
            pltpu.VMEM((size, width), bf16),
            pltpu.VMEM((8, width), f32),
            pltpu.VMEM((2, 8, width), f32),
            pltpu.VMEM((8, HD), f32),
            pltpu.VMEM((2, 8, HD), f32),
            pltpu.VMEM((wide, 8, lanes), f32),
            pltpu.VMEM((wide, 8, HD), f32),
            dma((count, 2 * depth)),
            dma((count, depth)),
            dma((count, depth)),
            dma((count, depth)),
            dma((40,)),
            dma((40,)),
            dma((2 * wide,)),
            dma((2 * wide,)),
            dma((40,)),
            dma((5, depth)),
            dma((5, depth)),
            dma((5, depth)),
            dma((5, depth)),
            dma((2,)),
            dma,
            pltpu.SemaphoreType.REGULAR,
            pltpu.SemaphoreType.REGULAR,
        ],
        compiler_params=pltpu.CompilerParams(
            collective_id=0, has_side_effects=True, vmem_limit_bytes=63 * MIB
        ),
    )(lengths, x, gain, cosine, sine, dyb, *own)


def owners(wide):
    depth = wide // 2
    w = lax.axis_index("wide")
    z, x = w // 2, w % 2
    return [
        ((z + k) % depth) * 2 + (x if dx == 0 else 1 - x) for dx in (0, 1) for k in range(depth)
    ]


def places(wide):
    depth = wide // 2
    w = lax.axis_index("wide")
    z, x = w // 2, w % 2
    return [
        jnp.where(x == o % 2, 0, depth) + (o // 2 - z) % depth for o in range(wide)
    ]


def reorder(values, order):
    block = values.shape[-1] // len(order)
    return jnp.concatenate(
        [lax.dynamic_slice_in_dim(values, at * block, block, axis=-1) for at in order], axis=-1
    )


def per_device(
    layer_input,
    out_grad,
    lengths,
    query_weight,
    query_mean,
    query_square,
    keyval_weight,
    keyval_mean,
    keyval_square,
    output_weight,
    output_mean,
    output_square,
    gateup_weight,
    gateup_mean,
    gateup_square,
    down_weight,
    down_mean,
    down_square,
    norm_gains,
    norm_mean,
    norm_square,
    head_gains,
    head_mean,
    head_square,
):
    wide = lax.axis_size("wide")
    depth = wide // 2
    w = lax.axis_index("wide")
    n = lax.axis_index("narrow")
    _, size, width = layer_input.shape
    block = width // wide
    span = 4 * size
    heads = query_weight.shape[1] // HD
    pairs = keyval_weight.shape[2] // HD
    groups = heads // pairs
    owner, place = owners(wide), places(wide)
    x = reorder(layer_input[0], owner)
    positions = n * size + jnp.arange(size)
    valid = positions < lengths[0]
    dyb = reorder(jnp.where(valid[:, None], out_grad[0], 0).astype(bf16), owner)
    own = [
        jnp.concatenate([query_weight, keyval_weight[0], keyval_weight[1]], axis=1).astype(bf16),
        output_weight.astype(bf16).T,
        gateup_weight[0].astype(bf16),
        gateup_weight[1].astype(bf16),
        down_weight.astype(bf16).T,
    ]
    lanes = max(HD, block)
    part = HD // wide
    gain = jnp.zeros((8, lanes), f32)
    gain = gain.at[0:2, 0:block].set(norm_gains.astype(bf16).astype(f32))
    gain = lax.dynamic_update_slice(gain, head_gains.astype(bf16).astype(f32), (2, w * part))
    cosine, sine = rope_tables(span)
    outs = layer_call(lengths, x, gain, cosine, sine, dyb, own, heads, pairs)
    layer_out = reorder(outs[0], place)[None]
    input_grad = reorder(outs[1], place)[None]
    norm_total = outs[2][0:2, 0:block]
    head_total = lax.dynamic_slice(outs[3], (0, w * part), (2, part))

    def total(g):
        result = outs[4 + g][0:block].astype(f32)
        for k in range(depth - 1):
            result = result + outs[9 + g][k * block : (k + 1) * block].astype(f32)
        return result

    qkv_total, output_total, gate_total, up_total, down_total = [total(g) for g in range(5)]
    split = heads * HD
    key_split = split + pairs * HD
    query = adamw(query_weight, query_mean, query_square, qkv_total[:, :split], 0.04)
    keyval = adamw(
        keyval_weight,
        keyval_mean,
        keyval_square,
        jnp.stack([qkv_total[:, split:key_split], qkv_total[:, key_split:]]),
        0.04,
    )
    output = adamw(output_weight, output_mean, output_square, output_total.T, 0.3)
    gateup = adamw(
        gateup_weight, gateup_mean, gateup_square, jnp.stack([gate_total, up_total]), 0.04
    )
    down = adamw(down_weight, down_mean, down_square, down_total.T, 0.025)
    norm = adamw(norm_gains, norm_mean, norm_square, norm_total, 0.4)
    head = adamw(head_gains, head_mean, head_square, head_total, 0.4)
    return (layer_out, input_grad, *query, *keyval, *output, *gateup, *down, *norm, *head)


def solution(mesh):
    tokens = P("wide", "narrow", None)
    down = [P("wide", "narrow")] * 3
    pair = [P(None, "wide", "narrow")] * 3
    across = [P("narrow", "wide")] * 3
    gain = [P(None, "wide")] * 3
    weights = down + pair + across + pair + across + gain + gain
    return jax.shard_map(
        per_device,
        mesh=mesh,
        in_specs=(tokens, tokens, P("wide"), *weights),
        out_specs=(tokens, tokens, *weights),
        check_vma=False,
    )
```

time: 948 us -> 866 us (0.914)
  the two profiles are of different devices: /device:TPU:1 before, /device:TPU:29 now
where the time goes in v2:
time: 866 us; the launch traced here: 856 us
  Pallas kernels  784 us (91%)
  local copies, waits for them, and re-layouts  36.7 us (4%)
  other arithmetic  32.3 us (4%)
    pallas_call x1, Pallas kernels, layer_call(): pl.pallas_call(functools.partial(layer_kernel, wide, heads, pairs), out_s...  784 us
    unnamed x107, local copies, waits for them, and re-layouts  33.1 us
    sub x7, other arithmetic, adamw(): weight - rate * (first_hat / (jnp.sqrt(second_hat) + adam_eps) + weight_d...  17.9 us

profile of v2, /device:TPU:29, one launch (start us, length us, event | category | flops | bytes accessed | tf_op | source)
XLA Modules:
  0.0 855.6 jit_solution(17102727702815357982)
XLA Ops:
  1.4 1.4 bitcast_select_fusion
  4.1 1.1 bitcast_dynamic-update-slice_fusion.6
  11.4 2.0 fusion.7
  13.4 1.3 pad_maximum_fusion.1
  15.7 1.1 copy-done.2
  17.0 1.2 slice_bitcast_fusion
  19.4 1.1 copy-done
  23.5 784.1 %shard_map.407 = (bf16[256,2048]{1,0:T(8,128)(2,1)}, f32[256,2048]{1,0:T(8,128)}, f32[8,256]{1,0:T(8,128)}, f32[8,128]{1,0:T(8,128)}, bf16[1024,1024]{1,0:T(8,12...) custom-call(s32[1]{0:T(128)} %copy.92.length_ref, ...), custom_call_target="tpu_custom_call" | custom-call | tf_op jit(solution)/shard_map/pallas_call | solution.py:967
  807.6 3.1 copy.53
  810.7 1.6 copy.54
  812.3 6.0 multiply_subtract_fusion.1
  818.3 3.1 copy.60
  821.4 1.6 copy.61
  823.1 1.6 copy.62
  824.7 2.4 add_bitcast_fusion.1
  827.1 2.6 add_bitcast_fusion
  830.5 4.8 multiply_subtract_fusion
  836.4 1.7 multiply_subtract_fusion.2
  838.1 1.0 copy.57
  841.1 2.0 convert_add_fusion.1
  843.1 1.4 multiply_subtract_fusion.3
  845.0 1.4 multiply_subtract_fusion.4
  852.5 1.3 multiply_subtract_fusion.6
  853.8 1.3 multiply_subtract_fusion.5
  (116 shorter events, 22.8 us)
Async XLA Ops:
  2.7 8.0 copy-start.28
  2.7 8.0 copy-start.29
  4.1 10.6 %copy-start.17 = (bf16[256,2048]{1,0:T(8,128)(2,1)}, bf16[256,2048]{1,0:T(8,128)(2,1)S(1)}, u32[]{:S(2)}) copy-start(bf16[256,2048]{1,0:T(8,128)(2,1)S(1)} %dynamic-slice_dynamic-update-slice_fusion.16.dyb_ref) | copy-start | bytes 3145732
  10.7 4.0 copy-start.16
  11.3 3.3 copy-start.26
  11.4 3.3 copy-start.10
  14.7 2.1 copy-start.2
  16.9 2.0 copy-start.14
  807.6 3.2 copy-start.15
  818.3 3.1 copy-start.4
  824.7 5.0 copy-start.7
  824.7 5.0 copy-start.8
  827.0 3.5 copy-start.3
  830.5 4.8 copy-start.24
  830.5 5.0 copy-start.25
  841.0 2.1 copy-start.11
  841.1 2.1 copy-start.19
  841.1 2.1 copy-start.20
  846.4 5.8 copy-start.18
  849.3 3.2 copy-start.32
  849.3 3.2 copy-start.33
  849.3 4.5 copy-start.30
  849.3 4.5 copy-start.31
  852.4 2.7 copy-start.27
  (10 other events, 13.9 us)

commit v3 on v2

--- a/solution.py
+++ b/solution.py
@@ -2,6 +2,7 @@
 
 import jax
 import jax.numpy as jnp
+import numpy as np
 from jax import lax
 from jax.experimental import pallas as pl
 from jax.experimental.pallas import tpu as pltpu
@@ -45,13 +46,13 @@
 
 def rope_tables(length):
     half = HD // 2
-    freqs = rope_base ** (-(jnp.arange(half, dtype=f32) * 2.0) / HD)
-    angles = jnp.arange(length, dtype=f32)[:, None] * freqs[None, :]
-    cosine = jnp.cos(angles)
-    sine = jnp.sin(angles)
+    freqs = rope_base ** (-(np.arange(half, dtype=np.float32) * np.float32(2.0)) / np.float32(HD))
+    angles = np.arange(length, dtype=np.float32)[:, None] * freqs.astype(np.float32)[None, :]
+    cosine = np.cos(angles.astype(np.float64)).astype(np.float32)
+    sine = np.sin(angles.astype(np.float64)).astype(np.float32)
     return (
-        jnp.concatenate([cosine, cosine], axis=-1),
-        jnp.concatenate([-sine, sine], axis=-1),
+        jnp.asarray(np.concatenate([cosine, cosine], axis=-1)),
+        jnp.asarray(np.concatenate([-sine, sine], axis=-1)),
     )
 
 
@@ -166,23 +167,34 @@
 
 
 class Wide:
-    def __init__(self, place, block, chunks, own, full, zs, zr, xs, xr):
-        self.place, self.block, self.chunks, self.own, self.full = place, block, chunks, own, full
+    def __init__(self, place, block, chunks, full, zs, zr, xs, xr):
+        self.place, self.block, self.chunks, self.full = place, block, chunks, full
         self.zs, self.zr, self.xs, self.xr = zs, zr, xs, xr
         self.near = place.depth == 4
+        self.odd = place.z - 2 * (place.z // 2)
+
+    def shared(self, i):
+        return self.near and i in (3, 5, 7)
+
+    def beside(self, i):
+        g, a, b = self.chunks[i]
+        at = (self.place.depth + 3 - 2 * self.odd) * self.block
+        return remote(
+            self.slot(i, self.place.depth),
+            self.full[g].at[pl.ds(pl.multiple_of(at, self.block), self.block), pl.ds(a, b - a)],
+            self.xs.at[i, 1 + 2 * self.odd],
+            self.xr.at[i, 3 - 2 * self.odd],
+            self.place.far(1 + 2 * self.odd, 0),
+        )
 
     def slot(self, i, index):
         g, a, b = self.chunks[i]
         return self.full[g].at[pl.ds(index * self.block, self.block), pl.ds(a, b - a)]
 
-    def mine(self, i):
-        g, a, b = self.chunks[i]
-        return self.own[g].at[:, pl.ds(a, b - a)]
-
     def along(self, i, k):
         depth = self.place.depth
         return remote(
-            self.mine(i),
+            self.slot(i, 0),
             self.slot(i, k),
             self.zs.at[i, k],
             self.zr.at[i, k],
@@ -201,9 +213,12 @@
 
     def across(self, i, k):
         depth = self.place.depth
-        src = self.mine(i) if k == 0 else self.slot(i, k)
         return remote(
-            src, self.slot(i, depth + k), self.xs.at[i, k], self.xr.at[i, k], self.place.far(0, 1)
+            self.slot(i, k),
+            self.slot(i, depth + k),
+            self.xs.at[i, k],
+            self.xr.at[i, k],
+            self.place.far(0, 1),
         )
 
     def each(self, i, k, act):
@@ -242,11 +257,21 @@
                 def _():
                     self.beyond(i, 3).start()
 
-            self.across(i, k).start()
+            if self.shared(i) and k in (1, 3):
+
+                @pl.when(self.odd == (1 if k == 1 else 0))
+                def _():
+                    self.across(i, k).start()
+            else:
+                self.across(i, k).start()
+        if self.shared(i):
+            self.across(i, 0).wait_recv()
+            self.beside(i).start()
 
     def arrived(self, i):
         for k in range(self.place.depth):
-            self.across(i, k).wait_recv()
+            if k or not self.shared(i):
+                self.across(i, k).wait_recv()
 
     def drain(self):
         z = self.place.z
@@ -310,25 +335,56 @@
     ]
 
 
+def owners(wide):
+    depth = wide // 2
+    w = lax.axis_index("wide")
+    z, x = w // 2, w % 2
+    return [
+        ((z + k) % depth) * 2 + (x if dx == 0 else 1 - x) for dx in (0, 1) for k in range(depth)
+    ]
+
+
+def places(wide):
+    depth = wide // 2
+    w = lax.axis_index("wide")
+    z, x = w // 2, w % 2
+    return [
+        jnp.where(x == o % 2, 0, depth) + (o // 2 - z) % depth for o in range(wide)
+    ]
+
+
+def reorder(values, order):
+    block = values.shape[-1] // len(order)
+    return jnp.concatenate(
+        [lax.dynamic_slice_in_dim(values, at * block, block, axis=-1) for at in order], axis=-1
+    )
+
+
 def layer_kernel(
     wide,
     heads,
     pairs,
     length_ref,
-    x_ref,
-    gain_ref,
+    norm_ref,
+    head_ref,
     cos_ref,
     sin_ref,
-    dyb_ref,
-    own_qkv,
-    own_out,
-    own_gate,
-    own_up,
-    own_down,
+    x_in,
+    dy_in,
+    w_query,
+    w_keyval,
+    w_output,
+    w_gateup,
+    w_down,
+    o_norm,
+    o_head,
     o_out,
     o_grad,
-    o_norm,
-    o_head,
+    o_query,
+    o_keyval,
+    o_output,
+    o_gateup,
+    o_down,
     home_qkv,
     home_out,
     home_gate,
@@ -354,10 +410,19 @@
     got_gate,
     got_up,
     got_down,
+    relay_qkv,
+    relay_out,
+    relay_gate,
+    relay_up,
+    relay_down,
     all_dyb,
     all_normed,
     all_qkv,
     all_dresb,
+    x_ref,
+    dyb_ref,
+    grad_own,
+    gain_ref,
     slots,
     gains,
     head_gain,
@@ -403,20 +468,20 @@
     depth = place.depth
     size, width = x_ref.shape
     block = width // wide
+    inside = block % HD == 0
     ff = hidden.shape[1]
     groups = heads // pairs
     span = 4 * size
-    own = [own_qkv, own_out, own_gate, own_up, own_down]
     full = [full_qkv, full_out, full_gate, full_up, full_down]
     away = [away_qkv, away_out, away_gate, away_up, away_down]
     got = [got_qkv, got_out, got_gate, got_up, got_down]
     home = [home_qkv, home_out, home_gate, home_up, home_down]
     come = [come_qkv, come_out, come_gate, come_up, come_down]
-    qkv_width = full_qkv.shape[1]
-    out_width = full_out.shape[1]
-    chunks = chunks_of([ref.shape[1] for ref in full])
-    greet(place)
-    ag = Wide(place, block, chunks, own, full, zs, zr, xs, xr)
+    relay = [relay_qkv, relay_out, relay_gate, relay_up, relay_down]
+    widths = [ref.shape[1] for ref in full]
+    qkv_width, out_width = widths[0], widths[1]
+    chunks = chunks_of(widths)
+    ag = Wide(place, block, chunks, full, zs, zr, xs, xr)
     side = Side(place, ns, nr)
     copies = []
     quarter = size // 4
@@ -431,6 +496,67 @@
         made = [keep(src, dst) for src, dst in pairs_of]
         for one in made:
             one.wait()
+
+    def in_order(ref, buf, out=False):
+        if not inside:
+            return [keep(buf, ref) if out else keep(ref, buf)]
+        made = []
+        for b in range(wide):
+            w, _ = place.far(b % depth, b // depth)
+            there = ref.at[:, pl.ds(pl.multiple_of(w * block, block), block)]
+            here = buf.at[:, pl.ds(b * block, block)]
+            made.append(keep(here, there) if out else keep(there, here))
+        return made
+
+    def land(g, buf):
+        if not inside:
+            return [keep([w_query, w_keyval, w_output, w_gateup, w_down][g], full[g].at[0:block])]
+        if g == 0:
+            at, made = 0, []
+            for ref in (w_query, w_keyval.at[0], w_keyval.at[1]):
+                made.append(keep(ref, buf.at[:, pl.ds(at, ref.shape[1])]))
+                at += ref.shape[1]
+            return made
+        if g in (2, 3):
+            return [keep(w_gateup.at[g - 2], buf.at[:, pl.ds(0, widths[g])])]
+        ref = w_output if g == 1 else w_down
+        return [
+            keep(ref.at[pl.ds(i * block, block)], buf.at[:, pl.ds(i * block, block)])
+            for i in range(widths[g] // block)
+        ]
+
+    def settle(g, buf, made):
+        for one in made:
+            one.wait()
+        if not inside:
+            return
+        slot = g % 2
+        if g in (1, 4):
+            for i in range(widths[g] // block):
+                at = pl.ds(i * block, block)
+                stage[slot, :, at] = buf[:, at].T.astype(bf16)
+        else:
+
+            def cast(i):
+                at = rows(i, block // 4)
+                stage[slot, at, pl.ds(0, widths[g])] = buf[at, 0 : widths[g]].astype(bf16)
+
+            loop(4, cast)
+        fetch((stage.at[slot, :, pl.ds(0, widths[g])], full[g].at[pl.ds(0, block)]))
+
+    landing = land(0, total)
+    x_copies = in_order(x_in, x_ref)
+    landing_out = land(1, resid)
+    dy_copies = in_order(dy_in, dyb_ref)
+
+    part = head_ref.shape[1]
+    gain_ref[...] = jnp.zeros_like(gain_ref)
+    gain_ref[0:2, 0:part] = head_ref[...]
+    spread = pltpu.roll(gain_ref[:, 0:HD], place.w * part, 1)
+    gain_ref[:, 0:HD] = pltpu.roll(spread, 2, 0)
+    gain_ref[0:2, 0:block] = norm_ref[...]
+    gain_ref[...] = gain_ref[...].astype(bf16).astype(f32)
+    greet(place)
 
     gain_copies = []
     for dx in (0, 1):
@@ -440,10 +566,13 @@
                 made = remote(gain_ref, slots.at[at], gs.at[at], gr.at[at], place.far(k, dx))
                 made.start()
                 gain_copies.append(made)
-    for i in range(3):
-        ag.issue(i)
-    own_copies = [keep(own[g], full[g].at[pl.ds(0, block)]) for g in range(5)]
-    dyb_copy = keep(dyb_ref, all_dyb.at[pl.ds(0, size)])
+    settle(0, total, landing)
+    landing = land(2, total)
+    ag.issue(0)
+    ag.issue(1)
+    settle(1, resid, landing_out)
+    landing_up = land(3, resid)
+    ag.issue(2)
     slots[0] = gain_ref[...]
     for made in gain_copies:
         made.wait_recv()
@@ -452,6 +581,8 @@
     for b in range(1, wide):
         heads_row = heads_row + slots[b][:, :HD]
     head_gain[...] = heads_row
+    for made in x_copies:
+        made.wait()
 
     def first_norm(i):
         at = rows(i, quarter)
@@ -461,19 +592,35 @@
     loop(4, first_norm)
     take_normed = Gather(side, cross_out, all_normed, size)
     normed_copy = keep(cross_out, all_normed.at[pl.ds(0, size)])
+    length = length_ref[0]
+    for made in dy_copies:
+        made.wait()
+
+    def mask(i):
+        at = rows(i, quarter)
+        value = dyb_ref[at, :].astype(f32)
+        where = place.n * size + i * quarter + lax.broadcasted_iota(jnp.int32, value.shape, 0)
+        dyb_ref[at, :] = jnp.where(where < length, value, 0.0).astype(bf16)
+
+    loop(4, mask)
     take_dyb = Gather(side, dyb_ref, all_dyb, size)
+    dyb_copy = keep(dyb_ref, all_dyb.at[pl.ds(0, size)])
+    settle(2, total, landing)
+    landing = land(4, total)
+    ag.hand_on(0)
+    settle(3, resid, landing_up)
+    ag.issue(3)
     take_normed.forward()
-    ag.hand_on(0)
-    ag.issue(3)
+    ag.hand_on(1)
+    ag.issue(4)
+    settle(4, total, landing)
+    ag.hand_on(2)
+    ag.issue(5)
     take_dyb.forward()
     take_normed.done()
     normed_copy.wait()
-    ag.hand_on(1)
-    ag.issue(4)
     ag.arrived(0)
     ag.arrived(1)
-    own_copies[0].wait()
-    length = length_ref[0]
 
     def keys_of(p, qkv, k_act, v_act):
         for a in range(4):
@@ -497,8 +644,6 @@
 
         loop(4, project)
         qkv_copy = keep(qkv, all_qkv)
-        ag.hand_on(2)
-        ag.issue(5)
 
         def pair(p):
             keys_of(p, qkv, k_act, v_act)
@@ -530,7 +675,6 @@
     ag.hand_on(3)
     ag.issue(6)
     ag.arrived(2)
-    own_copies[1].wait()
     fetch((full_out, weights.at[:, pl.ds(0, out_width)]))
     step = 512
 
@@ -575,12 +719,9 @@
     ag.hand_on(4)
     ag.issue(7)
     take_mixed.forward()
-    take_mixed.done()
-    take_dyb.done()
-    dyb_copy.wait()
-    fetch((all_dyb, tokens))
     ag.hand_on(5)
     ag.issue(8)
+    take_mixed.done()
     half = ff // 2
     tile = 256
 
@@ -610,59 +751,90 @@
             place.far(k, 0),
         )
 
+    order = (1, 3, 2, 0) if ag.near else tuple(range(1, steps)) + (0,)
+    waiting = []
+    turns = [0]
+
+    def flush():
+        while waiting:
+            waiting.pop(0)()
+
     def send_away(g, left, right):
+        wide_g = widths[g]
+        for t in order:
+            flush()
+            slot = turns[0] % 2
+            turns[0] += 1
+            at = (steps + t) * piece
+            stage[slot, :, 0:wide_g] = dot_tn(left[:, at : at + piece], right()).astype(bf16)
+            staged(g, slot, part_of(away[g], t)).start()
+
+            def finish(t=t, slot=slot):
+                staged(g, slot, part_of(away[g], t)).wait()
+                cross(g, t).start()
+
+            waiting.append(finish)
+
+    def add_to_stage(g, slot, src, made):
         wide_g = full[g].shape[1]
-
-        def finish(t):
-            staged(g, lax.rem(t, 2), part_of(away[g], t)).wait()
-            cross(g, t).start()
-
-        def one(t):
-            made = dot_tn(left[:, rows(steps + t, piece)], right())
-            stage[lax.rem(t, 2), :, pl.ds(0, wide_g)] = made.astype(bf16)
-
-            @pl.when(t > 0)
-            def _():
-                finish(t - 1)
-
-            staged(g, lax.rem(t, 2), part_of(away[g], t)).start()
-
-        loop(steps, one)
-        finish(steps - 1)
-
-    def send_home(g, left, right):
+        made.wait_recv()
+        more = pltpu.make_async_copy(src, arrived_tile.at[:, pl.ds(0, wide_g)], tile_sem)
+        more.start()
+        more.wait()
+        stage[slot, :, 0:wide_g] = (
+            stage[slot, :, 0:wide_g].astype(f32) + arrived_tile[:, 0:wide_g].astype(f32)
+        ).astype(bf16)
+
+    def relay_over(g, k):
+        return remote(
+            part_of(home[g], k),
+            relay[g],
+            rzs.at[g, k],
+            rzr.at[g, 0],
+            place.far(depth - 1 if k == 1 else 1, 0),
+        )
+
+    def send_home(g, left, right, which=None):
         wide_g = full[g].shape[1]
-
-        def finish(j):
-            t = lax.rem(j + 1, steps)
-            staged(g, lax.rem(j, 2), part_of(home[g], t)).wait()
-            for r in range(held):
-                k = t * held + r
-
-                @pl.when(k > 0)
-                def _(k=k):
-                    hand_over(g, k).start()
-
-        def one(j):
-            t = lax.rem(j + 1, steps)
+        for t in order if which is None else which:
+            flush()
+            slot = turns[0] % 2
+            turns[0] += 1
             cross(g, t).wait_recv()
             get = pltpu.make_async_copy(
                 part_of(got[g], t), arrived_tile.at[:, pl.ds(0, wide_g)], tile_sem
             )
             get.start()
-            made = dot_tn(left[:, rows(t, piece)], right())
+            made = dot_tn(left[:, t * piece : (t + 1) * piece], right())
             get.wait()
-            made = made + arrived_tile[:, pl.ds(0, wide_g)].astype(f32)
-            stage[lax.rem(j, 2), :, pl.ds(0, wide_g)] = made.astype(bf16)
-
-            @pl.when(j > 0)
-            def _():
-                finish(j - 1)
-
-            staged(g, lax.rem(j, 2), part_of(home[g], t)).start()
-
-        loop(steps, one)
-        finish(steps - 1)
+            made = made + arrived_tile[:, 0:wide_g].astype(f32)
+            stage[slot, :, 0:wide_g] = made.astype(bf16)
+            if ag.near and t == 2:
+
+                @pl.when((place.z == 1) | (place.z == 2))
+                def _():
+                    add_to_stage(g, slot, relay[g], relay_over(g, 1))
+
+            staged(g, slot, part_of(home[g], t)).start()
+
+            def finish(t=t, slot=slot):
+                staged(g, slot, part_of(home[g], t)).wait()
+                for r in range(held):
+                    k = t * held + r
+                    if ag.near and k in (1, 3):
+                        at_end = place.z == (3 if k == 1 else 0)
+
+                        @pl.when(at_end)
+                        def _():
+                            relay_over(g, k).start()
+
+                        @pl.when(jnp.logical_not(at_end))
+                        def _():
+                            hand_over(g, k).start()
+                    elif k:
+                        hand_over(g, k).start()
+
+            waiting.append(finish)
 
     def feed_forward(gate, up):
         def feed(part):
@@ -689,21 +861,23 @@
 
             loop(half // tile, columns)
 
-        own_copies[2].wait()
-        own_copies[3].wait()
         ag.arrived(3)
         ag.arrived(4)
         feed(0)
+        take_dyb.done()
+        dyb_copy.wait()
+        tokens_copy = keep(all_dyb, tokens)
         ag.hand_on(6)
+        ag.hand_on(7)
         ag.arrived(5)
         ag.arrived(6)
         feed(1)
+        ag.hand_on(8)
+        tokens_copy.wait()
         send_away(4, tokens, lambda: hidden[...])
-        ag.hand_on(7)
-        ag.hand_on(8)
+        flush()
         ag.arrived(7)
         ag.arrived(8)
-        own_copies[4].wait()
         fetch((full_down, weights))
 
         def columns(n):
@@ -743,6 +917,9 @@
     pl.run_scoped(mixed_grad, pltpu.VMEM((width, 2 * ff), bf16))
     other = scattered[0]
     send_away(2, mixed, lambda: feed_grad[:, pl.ds(0, ff)])
+    flush()
+    down_home = functools.partial(send_home, 4, tokens, lambda: hidden[...])
+    down_home(order[:1])
     other.wait_recv()
     sums[...] = jnp.zeros_like(sums)
     head_sums[...] = jnp.zeros_like(head_sums)
@@ -756,7 +933,7 @@
         sums[1:2, :] += jnp.sum(grad * unit, axis=0, keepdims=True)
         back = norm_back(grad, unit, scale, gains[1:2, :])
         result = dyb_ref[at, :].astype(f32) + back
-        o_grad[at, :] = result
+        grad_own[at, :] = result
         cross_out[at, :] = result.astype(bf16)
 
     side.drain()
@@ -764,28 +941,20 @@
     take_dresb = Gather(side, cross_out, all_dresb, size)
     dresb_copy = keep(cross_out, all_dresb.at[pl.ds(0, size)])
     send_away(3, mixed, lambda: feed_grad[:, pl.ds(ff, ff)])
+    flush()
+    down_home(order[1:2])
     take_dresb.forward()
-    send_home(4, tokens, lambda: hidden[...])
+    down_home(order[2:])
+    flush()
     take_dresb.done()
     dresb_copy.wait()
 
-    def down_tile(start, count, n):
-        return dot_nt(hidden[pl.ds(start, count), :], weights[rows(n, step), :])
-
-    side.drain()
-    other = scatter(down_tile)
-    other.wait_recv()
-    o_out[...] = (resid[...] + total[...] + cross_in[...].astype(f32)).astype(bf16)
-    pl.semaphore_signal(free_core, inc=1, device_id=place.side(0, 1), device_id_type=MESH)
-    pl.semaphore_signal(free_other, inc=1, device_id=place.side(1, 0), device_id_type=MESH)
-
-    def attention_back(qkv, k_act, v_act, ctx_grad, qkv_grad, k_grad, v_grad):
+    def attention_back(qkv_grad, qkv, k_act, v_act, ctx_grad, k_grad, v_grad):
         fetch(
             (all_dresb, tokens),
             (all_qkv, qkv),
             (full_out, weights.at[:, pl.ds(0, out_width)]),
         )
-        send_away(1, tokens, lambda: ctx[...])
 
         def context_grad(m):
             ctx_grad[rows(m, size), :] = dot_nn(
@@ -842,9 +1011,76 @@
                 qkv_grad[at, column] = v_grad[to, :].astype(bf16)
 
         loop(pairs, pair)
-        send_home(1, tokens, lambda: ctx[...])
-        fetch((all_normed, tokens), (full_qkv, weights.at[:, pl.ds(0, qkv_width)]))
-        send_away(0, tokens, lambda: qkv_grad[...])
+
+    def finish_back(qkv_grad, normed, come_v, home_v, sum_v, sum_t):
+        normed_copy = keep(all_normed, normed)
+        qkv_copy = keep(full_qkv, weights.at[:, pl.ds(0, qkv_width)])
+        send_away(1, tokens, lambda: ctx[...])
+        normed_copy.wait()
+        send_away(0, normed, lambda: qkv_grad[...])
+        flush()
+        gate_home = functools.partial(send_home, 2, mixed, lambda: feed_grad[:, pl.ds(0, ff)])
+        up_home = functools.partial(send_home, 3, mixed, lambda: feed_grad[:, pl.ds(ff, ff)])
+        out_home = functools.partial(send_home, 1, tokens, lambda: ctx[...])
+        qkv_home = functools.partial(send_home, 0, normed, lambda: qkv_grad[...])
+        gate_home(order[:-1])
+        flush()
+        qkv_copy.wait()
+        written = []
+
+        def finals(g):
+            flush()
+            wide_g = widths[g]
+            mine = keep(home[g].at[pl.ds(0, block)], home_v.at[:, pl.ds(0, wide_g)])
+            for k in range(1, depth):
+                at = pl.ds((k - 1) * block, block)
+
+                def bring(g=g, k=k, at=at):
+                    hand_over(g, k).wait_recv()
+                    made = pltpu.make_async_copy(
+                        come[g].at[at], come_v.at[at, pl.ds(0, wide_g)], tile_sem
+                    )
+                    made.start()
+                    made.wait()
+
+                if ag.near and k in (1, 3):
+                    here = place.z != (0 if k == 1 else 3)
+                    pl.when(here)(bring)
+
+                    @pl.when(jnp.logical_not(here))
+                    def _(at=at):
+                        come_v[at, 0:wide_g] = jnp.zeros((block, wide_g), bf16)
+                else:
+                    bring()
+            mine.wait()
+            while written:
+                written.pop().wait()
+
+            def add(i):
+                at = rows(i, block // 4)
+                value = home_v[at, 0:wide_g].astype(f32)
+                for k in range(1, depth):
+                    more = pl.ds(
+                        pl.multiple_of((k - 1) * block + i * (block // 4), block // 4), block // 4
+                    )
+                    value = value + come_v[more, 0:wide_g].astype(f32)
+                sum_v[at, 0:wide_g] = value
+
+            loop(4, add)
+            if g in (1, 4):
+                for i in range(wide_g // HD):
+                    sum_t[pl.ds(i * HD, HD), :] = sum_v[:, i * HD : (i + 1) * HD].T
+                ref = o_output if g == 1 else o_down
+                written.append(keep(sum_t.at[pl.ds(0, wide_g)], ref))
+            elif g == 0:
+                ends = (o_query, o_keyval.at[0], o_keyval.at[1])
+                columns = (heads * HD, pairs * HD, pairs * HD)
+                at = 0
+                for ref, count in zip(ends, columns, strict=True):
+                    written.append(keep(sum_v.at[:, pl.ds(at, count)], ref))
+                    at += count
+            else:
+                written.append(keep(sum_v.at[:, pl.ds(0, wide_g)], o_gateup.at[g - 2]))
 
         def normed_tile(start, count, n):
             return dot_nt(
@@ -852,10 +1088,11 @@
             )
 
         side.drain()
-        pl.semaphore_wait(free_core, 1)
-        pl.semaphore_wait(free_other, 1)
         other = scatter(normed_tile)
-        send_home(2, mixed, lambda: feed_grad[:, pl.ds(0, ff)])
+        finals(4)
+        gate_home(order[-1:])
+        up_home(order[:1])
+        flush()
         other.wait_recv()
 
         def first_back(i):
@@ -865,9 +1102,11 @@
             unit = value * scale
             grad = total[at, :] + cross_in[at, :].astype(f32)
             sums[0:1, :] += jnp.sum(grad * unit, axis=0, keepdims=True)
-            o_grad[at, :] += norm_back(grad, unit, scale, gains[0:1, :])
+            grad_own[at, :] += norm_back(grad, unit, scale, gains[0:1, :])
 
         loop(4, first_back)
+        pl.semaphore_signal(free_core, inc=1, device_id=place.side(0, 1), device_id_type=MESH)
+        pl.semaphore_signal(free_other, inc=1, device_id=place.side(1, 0), device_id_type=MESH)
 
         for flip, (dy, dc) in enumerate(((0, 1), (1, 0))):
             norm_made = side.copy(sums, sums_in.at[flip], dy, dc)
@@ -901,8 +1140,31 @@
                     )
                     made.start()
                     last.append(made)
-        send_home(3, mixed, lambda: feed_grad[:, pl.ds(ff, ff)])
-        send_home(0, tokens, lambda: qkv_grad[...])
+        up_home(order[1:-1])
+        fetch((full_down, weights))
+
+        def down_tile(start, count, n):
+            return dot_nt(hidden[pl.ds(start, count), :], weights[rows(n, step), :])
+
+        pl.semaphore_wait(free_core, 1)
+        pl.semaphore_wait(free_other, 1)
+        other = scatter(down_tile)
+        grads = in_order(o_grad, grad_own, out=True)
+        finals(2)
+        up_home(order[-1:])
+        flush()
+        other.wait_recv()
+        side.drain()
+        cross_out[...] = (resid[...] + total[...] + cross_in[...].astype(f32)).astype(bf16)
+        results = in_order(o_out, cross_out, out=True)
+        out_home(None)
+        qkv_home(order[:-1])
+        finals(3)
+        finals(1)
+        qkv_home(order[-1:])
+        finals(0)
+        for made in grads + results + written:
+            made.wait()
         for made in last:
             made.wait_recv()
         norm_total = slots[0]
@@ -915,48 +1177,67 @@
         for made in last:
             made.wait_send()
 
-    pl.run_scoped(
-        attention_back,
-        pltpu.VMEM((span, qkv_width), f32),
-        pltpu.VMEM((span, HD), bf16),
-        pltpu.VMEM((span, HD), bf16),
-        pltpu.VMEM((span, out_width), bf16),
-        pltpu.VMEM((span, qkv_width), bf16),
-        pltpu.VMEM((span, HD), f32),
-        pltpu.VMEM((span, HD), f32),
-    )
+    def back(qkv_grad):
+        pl.run_scoped(
+            functools.partial(attention_back, qkv_grad),
+            pltpu.VMEM((span, qkv_width), f32),
+            pltpu.VMEM((span, HD), bf16),
+            pltpu.VMEM((span, HD), bf16),
+            pltpu.VMEM((span, out_width), bf16),
+            pltpu.VMEM((span, HD), f32),
+            pltpu.VMEM((span, HD), f32),
+        )
+        pl.run_scoped(
+            functools.partial(finish_back, qkv_grad),
+            pltpu.VMEM((span, width), bf16),
+            pltpu.VMEM(((depth - 1) * block, max(widths)), bf16),
+            pltpu.VMEM((block, max(widths)), bf16),
+            pltpu.VMEM((block, max(widths)), f32),
+            pltpu.VMEM((max(widths), block), f32),
+        )
+
+    pl.run_scoped(back, pltpu.VMEM((span, qkv_width), bf16))
     for g in range(5):
         for t in range(steps):
             cross(g, t).wait_send()
         for k in range(1, depth):
-            hand_over(g, k).wait()
+            hand_over(g, k).wait_send()
     side.drain()
     ag.drain()
 
 
-def layer_call(lengths, x, gain, cosine, sine, dyb, own, heads, pairs):
+def layer_call(lengths, norm_gains, head_gains, x, dy, weights, heads, pairs):
     wide = lax.axis_size("wide")
     depth = wide // 2
     size, width = x.shape
     span = 4 * size
     block = width // wide
-    ff = own[2].shape[1]
-    widths = [w.shape[1] for w in own]
-    lanes = gain.shape[1]
+    inside = block % HD == 0
+    ff = weights[3].shape[-1]
+    widths = [(heads + 2 * pairs) * HD, heads * HD, ff, ff, ff]
+    lanes = max(HD, block)
     shape = jax.ShapeDtypeStruct
     anywhere = pl.BlockSpec(memory_space=pl.ANY)
     vmem = pl.BlockSpec(memory_space=pltpu.VMEM)
+    smem = pl.BlockSpec(memory_space=pltpu.SMEM)
     count = len(chunks_of(widths))
+    cosine, sine = rope_tables(span)
     outs = [
+        shape((8, lanes), f32),
+        shape((8, HD), f32),
         shape((size, width), bf16),
         shape((size, width), f32),
-        shape((8, lanes), f32),
-        shape((8, HD), f32),
+        shape((block, heads * HD), f32),
+        shape((2, block, pairs * HD), f32),
+        shape((heads * HD, block), f32),
+        shape((2, block, ff), f32),
+        shape((ff, block), f32),
     ]
     outs += [shape((width // 2, w), bf16) for w in widths]
     outs += [shape(((depth - 1) * block, w), bf16) for w in widths]
     outs += [shape((width, w), bf16) for w in widths]
     outs += [shape((width // 2, w), bf16) for w in widths] * 2
+    outs += [shape((block, w), bf16) for w in widths]
     outs += [
         shape((span, width), bf16),
         shape((span, width), bf16),
@@ -964,12 +1245,27 @@
         shape((span, width), bf16),
     ]
     dma = pltpu.SemaphoreType.DMA
-    return pl.pallas_call(
+    if not inside:
+        query, keyval, output, gateup, down = [w.astype(bf16) for w in weights]
+        weights = [
+            jnp.concatenate([query, keyval[0], keyval[1]], axis=1),
+            output.T,
+            gateup[0],
+            gateup[1],
+            down.T,
+        ]
+        owner, place = owners(wide), places(wide)
+        x, dy = reorder(x, owner), reorder(dy, owner)
+    results = pl.pallas_call(
         functools.partial(layer_kernel, wide, heads, pairs),
         out_shape=outs,
-        in_specs=[pl.BlockSpec(memory_space=pltpu.SMEM)] + [vmem] * 5 + [anywhere] * 5,
-        out_specs=[vmem] * 4 + [anywhere] * (len(outs) - 4),
+        in_specs=[smem] + [vmem] * 4 + [anywhere] * 7,
+        out_specs=[vmem] * 2 + [anywhere] * (len(outs) - 2),
         scratch_shapes=[
+            pltpu.VMEM((size, width), bf16),
+            pltpu.VMEM((size, width), bf16),
+            pltpu.VMEM((size, width), f32),
+            pltpu.VMEM((8, lanes), f32),
             pltpu.VMEM((wide, 8, lanes), f32),
             pltpu.VMEM((8, width), f32),
             pltpu.VMEM((8, HD), f32),
@@ -1001,7 +1297,7 @@
             dma((40,)),
             dma((2 * wide,)),
             dma((2 * wide,)),
-            dma((40,)),
+            dma((160,)),
             dma((5, depth)),
             dma((5, depth)),
             dma((5, depth)),
@@ -1014,32 +1310,12 @@
         compiler_params=pltpu.CompilerParams(
             collective_id=0, has_side_effects=True, vmem_limit_bytes=63 * MIB
         ),
-    )(lengths, x, gain, cosine, sine, dyb, *own)
-
-
-def owners(wide):
-    depth = wide // 2
-    w = lax.axis_index("wide")
-    z, x = w // 2, w % 2
-    return [
-        ((z + k) % depth) * 2 + (x if dx == 0 else 1 - x) for dx in (0, 1) for k in range(depth)
-    ]
-
-
-def places(wide):
-    depth = wide // 2
-    w = lax.axis_index("wide")
-    z, x = w // 2, w % 2
-    return [
-        jnp.where(x == o % 2, 0, depth) + (o // 2 - z) % depth for o in range(wide)
-    ]
-
-
-def reorder(values, order):
-    block = values.shape[-1] // len(order)
-    return jnp.concatenate(
-        [lax.dynamic_slice_in_dim(values, at * block, block, axis=-1) for at in order], axis=-1
-    )
+    )(lengths, norm_gains, head_gains, cosine, sine, x, dy, *weights)
+    results = list(results[:9])
+    if not inside:
+        results[2] = reorder(results[2], place)
+        results[3] = reorder(results[3], place)
+    return results
 
 
 def per_device(
@@ -1069,61 +1345,24 @@
     head_square,
 ):
     wide = lax.axis_size("wide")
-    depth = wide // 2
     w = lax.axis_index("wide")
-    n = lax.axis_index("narrow")
-    _, size, width = layer_input.shape
-    block = width // wide
-    span = 4 * size
+    block = layer_input.shape[2] // wide
     heads = query_weight.shape[1] // HD
     pairs = keyval_weight.shape[2] // HD
-    groups = heads // pairs
-    owner, place = owners(wide), places(wide)
-    x = reorder(layer_input[0], owner)
-    positions = n * size + jnp.arange(size)
-    valid = positions < lengths[0]
-    dyb = reorder(jnp.where(valid[:, None], out_grad[0], 0).astype(bf16), owner)
-    own = [
-        jnp.concatenate([query_weight, keyval_weight[0], keyval_weight[1]], axis=1).astype(bf16),
-        output_weight.astype(bf16).T,
-        gateup_weight[0].astype(bf16),
-        gateup_weight[1].astype(bf16),
-        down_weight.astype(bf16).T,
-    ]
-    lanes = max(HD, block)
+    weights = [query_weight, keyval_weight, output_weight, gateup_weight, down_weight]
+    results = layer_call(
+        lengths, norm_gains, head_gains, layer_input[0], out_grad[0], weights, heads, pairs
+    )
+    norm_total = results[0][0:2, 0:block]
     part = HD // wide
-    gain = jnp.zeros((8, lanes), f32)
-    gain = gain.at[0:2, 0:block].set(norm_gains.astype(bf16).astype(f32))
-    gain = lax.dynamic_update_slice(gain, head_gains.astype(bf16).astype(f32), (2, w * part))
-    cosine, sine = rope_tables(span)
-    outs = layer_call(lengths, x, gain, cosine, sine, dyb, own, heads, pairs)
-    layer_out = reorder(outs[0], place)[None]
-    input_grad = reorder(outs[1], place)[None]
-    norm_total = outs[2][0:2, 0:block]
-    head_total = lax.dynamic_slice(outs[3], (0, w * part), (2, part))
-
-    def total(g):
-        result = outs[4 + g][0:block].astype(f32)
-        for k in range(depth - 1):
-            result = result + outs[9 + g][k * block : (k + 1) * block].astype(f32)
-        return result
-
-    qkv_total, output_total, gate_total, up_total, down_total = [total(g) for g in range(5)]
-    split = heads * HD
-    key_split = split + pairs * HD
-    query = adamw(query_weight, query_mean, query_square, qkv_total[:, :split], 0.04)
-    keyval = adamw(
-        keyval_weight,
-        keyval_mean,
-        keyval_square,
-        jnp.stack([qkv_total[:, split:key_split], qkv_total[:, key_split:]]),
-        0.04,
-    )
-    output = adamw(output_weight, output_mean, output_square, output_total.T, 0.3)
-    gateup = adamw(
-        gateup_weight, gateup_mean, gateup_square, jnp.stack([gate_total, up_total]), 0.04
-    )
-    down = adamw(down_weight, down_mean, down_square, down_total.T, 0.025)
+    head_total = lax.dynamic_slice(results[1], (0, w * part), (2, part))
+    layer_out, input_grad = results[2][None], results[3][None]
+    query_total, keyval_total, output_total, gateup_total, down_total = results[4:]
+    query = adamw(query_weight, query_mean, query_square, query_total, 0.04)
+    keyval = adamw(keyval_weight, keyval_mean, keyval_square, keyval_total, 0.04)
+    output = adamw(output_weight, output_mean, output_square, output_total, 0.3)
+    gateup = adamw(gateup_weight, gateup_mean, gateup_square, gateup_total, 0.04)
+    down = adamw(down_weight, down_mean, down_square, down_total, 0.025)
     norm = adamw(norm_gains, norm_mean, norm_square, norm_total, 0.4)
     head = adamw(head_gains, head_mean, head_square, head_total, 0.4)
     return (layer_out, input_grad, *query, *keyval, *output, *gateup, *down, *norm, *head)

time: 866 us -> 626 us (0.72)
  the two profiles are of different devices: /device:TPU:29 before, /device:TPU:1 now
where the time goes in v3:
time: 626 us; the launch traced here: 616 us
  Pallas kernels  591 us (94%)
  other arithmetic  18.3 us (3%)
    pallas_call x1, Pallas kernels, layer_call(): pl.pallas_call(functools.partial(layer_kernel, wide, heads, pairs), out_s...  591 us
    sub x7, other arithmetic, adamw(): weight - rate * (first_hat / (jnp.sqrt(second_hat) + adam_eps) + weight_d...  18.3 us

profile of v3, /device:TPU:1, one launch (start us, length us, event | category | flops | bytes accessed | tf_op | source)
XLA Modules:
  0.0 615.9 jit_solution(4783528537626353413)
XLA Ops:
  1.3 591.4 %shard_map.425 = (f32[8,256]{1,0:T(8,128)}, f32[8,128]{1,0:T(8,128)}, bf16[256,2048]{1,0:T(8,128)(2,1)}, f32[256,2048]{1,0:T(8,128)}, f32[256,512]{1,0:T(8,128)}...) custom-call(s32[1]{0:T(128)S(6)} %copy.51.length_ref, ...), custom_call_target="tpu_custom_call" | custom-call | tf_op jit(solution)/shard_map/pallas_call | solution.py:1259
  592.7 1.3 multiply_subtract_fusion.6
  594.1 8.4 %multiply_subtract_fusion = (f32[2,256,1536]{2,1,0:T(8,128)}, f32[2,256,1536]{2,1,0:T(8,128)}, f32[2,256,1536]{2,1,0:T(8,128)}) fusion(f32[2,256,1536]{2,1,0:T(8,128)} %w_gateup.1, f32[2,256,1536]{2,1,0:T(8,128)} %get-tuple-element.37, f32[2,256,1536]{2,1,0:T(8,128)} %param.39, f32[2,256,1536]{2,1,0:T(8,128)} %param.40), kind=kLoop, calls=%fused_computation.3 | loop fusion | flops 11010048 | bytes 22020096 | tf_op jit(solution)/shard_map/sub | solution.py:41
  602.5 0.0 copy-done.5
  602.5 0.9 copy-done.6
  603.4 0.5 copy-done.7
  603.9 3.0 multiply_subtract_fusion.1
  606.9 0.0 copy-done.1
  606.9 0.0 copy-done.9
  606.9 0.0 copy-done.10
  606.9 0.0 copy-done.17
  606.9 0.0 copy-start.3
  607.0 0.0 copy-start.13
  607.0 0.0 copy-start.14
  607.0 0.0 copy-start.15
  607.0 1.4 multiply_subtract_fusion.4
  608.4 0.2 copy-done.12
  608.7 0.3 copy-done.16
  609.0 1.4 multiply_subtract_fusion.3
  610.4 0.0 copy-done.3
  610.4 1.4 multiply_subtract_fusion.2
  611.9 1.3 multiply_subtract_fusion.5
  613.2 1.0 copy.52
  614.1 1.3 copy.53
  (34 shorter events, 0.1 us)
Async XLA Ops:
  1.3 591.4 %copy-start.19 = (f32[2,16]{1,0:T(2,128)S(1)}, f32[2,16]{1,0:T(2,128)}, u32[]{:S(2)}) copy-start(f32[2,16]{1,0:T(2,128)} %head_ref.1) | copy-start | bytes 388
  1.3 591.4 %copy-start.22 = (f32[2,16]{1,0:T(2,128)S(1)}, f32[2,16]{1,0:T(2,128)}, u32[]{:S(2)}) copy-start(f32[2,16]{1,0:T(2,128)} %param.48) | copy-start | bytes 388
  1.3 591.4 %copy-start.23 = (f32[2,16]{1,0:T(2,128)S(1)}, f32[2,16]{1,0:T(2,128)}, u32[]{:S(2)}) copy-start(f32[2,16]{1,0:T(2,128)} %param.49) | copy-start | bytes 388
  594.1 8.4 %copy-start = (f32[1536,256]{1,0:T(8,128)S(1)}, f32[1536,256]{1,0:T(8,128)}, u32[]{:S(2)}) copy-start(f32[1536,256]{1,0:T(8,128)} %w_down.1) | copy-start | bytes 4718596
  594.1 8.4 %copy-start.5 = (f32[1536,256]{1,0:T(8,128)S(1)}, f32[1536,256]{1,0:T(8,128)}, u32[]{:S(2)}) copy-start(f32[1536,256]{1,0:T(8,128)} %param.42) | copy-start | bytes 4718596
  594.1 9.3 %copy-start.6 = (f32[1536,256]{1,0:T(8,128)S(1)}, f32[1536,256]{1,0:T(8,128)}, u32[]{:S(2)}) copy-start(f32[1536,256]{1,0:T(8,128)} %param.43) | copy-start | bytes 4718596
  594.1 9.8 %copy-start.7 = (f32[1536,256]{1,0:T(8,128)S(1)}, f32[1536,256]{1,0:T(8,128)}, u32[]{:S(2)}) copy-start(f32[1536,256]{1,0:T(8,128)} %get-tuple-element.38) | copy-start | bytes 4718596
  603.8 3.1 copy-start.1
  603.8 3.1 copy-start.9
  603.8 3.1 copy-start.10
  603.9 3.1 copy-start.17
  606.9 1.5 copy-start.2
  606.9 1.5 copy-start.11
  606.9 1.8 copy-start.12
  606.9 2.1 copy-start.16
  606.9 3.5 copy-start.3
  607.0 3.5 copy-start.13
  607.0 3.4 copy-start.14
  607.0 3.4 copy-start.15
  609.0 2.9 copy-start.18
  609.0 2.9 copy-start.20
  609.0 2.9 copy-start.21
  609.0 4.2 copy-start.8
  610.4 3.7 copy-start.4

commit v4 on v3

--- a/solution.py
+++ b/solution.py
@@ -174,7 +174,20 @@
         self.odd = place.z - 2 * (place.z // 2)
 
     def shared(self, i):
-        return self.near and i in (3, 5, 7)
+        return self.near and i == 3
+
+    def early(self, i):
+        return self.near and i == 8
+
+    def pass_on(self, i, k):
+        depth = self.place.depth
+        return remote(
+            self.slot(i, depth),
+            self.slot(i, depth + k),
+            self.xs.at[i, k],
+            self.xr.at[i, k],
+            self.place.far(depth - k, 0),
+        )
 
     def beside(self, i):
         g, a, b = self.chunks[i]
@@ -245,6 +258,10 @@
 
     def hand_on(self, i):
         z = self.place.z
+        if self.early(i):
+            self.across(i, 0).wait_recv()
+            for k in self.order():
+                self.pass_on(i, k).start()
         for k in self.order():
             self.along(i, k).wait_recv()
             if self.near and k == 2:
@@ -257,6 +274,8 @@
                 def _():
                     self.beyond(i, 3).start()
 
+            if self.early(i):
+                continue
             if self.shared(i) and k in (1, 3):
 
                 @pl.when(self.odd == (1 if k == 1 else 0))
@@ -270,7 +289,7 @@
 
     def arrived(self, i):
         for k in range(self.place.depth):
-            if k or not self.shared(i):
+            if k or not (self.shared(i) or self.early(i)):
                 self.across(i, k).wait_recv()
 
     def drain(self):
@@ -415,11 +434,12 @@
     relay_gate,
     relay_up,
     relay_down,
+    aside_up,
+    aside_down,
     all_dyb,
     all_normed,
     all_qkv,
     all_dresb,
-    x_ref,
     dyb_ref,
     grad_own,
     gain_ref,
@@ -466,7 +486,7 @@
 ):
     place = Place(wide, 4)
     depth = place.depth
-    size, width = x_ref.shape
+    size, width = x_in.shape
     block = width // wide
     inside = block % HD == 0
     ff = hidden.shape[1]
@@ -478,6 +498,7 @@
     home = [home_qkv, home_out, home_gate, home_up, home_down]
     come = [come_qkv, come_out, come_gate, come_up, come_down]
     relay = [relay_qkv, relay_out, relay_gate, relay_up, relay_down]
+    aside = [aside_up, aside_down]
     widths = [ref.shape[1] for ref in full]
     qkv_width, out_width = widths[0], widths[1]
     chunks = chunks_of(widths)
@@ -544,8 +565,14 @@
             loop(4, cast)
         fetch((stage.at[slot, :, pl.ds(0, widths[g])], full[g].at[pl.ds(0, block)]))
 
+    waiting = []
+
+    def flush():
+        while waiting:
+            waiting.pop(0)()
+
     landing = land(0, total)
-    x_copies = in_order(x_in, x_ref)
+    x_copies = in_order(x_in, tokens.at[pl.ds(0, size)])
     landing_out = land(1, resid)
     dy_copies = in_order(dy_in, dyb_ref)
 
@@ -567,12 +594,23 @@
                 made.start()
                 gain_copies.append(made)
     settle(0, total, landing)
-    landing = land(2, total)
     ag.issue(0)
     ag.issue(1)
+    landing = land(2, total)
     settle(1, resid, landing_out)
+    ag.issue(2)
     landing_up = land(3, resid)
-    ag.issue(2)
+    window = 4
+
+    def hand(i):
+        flush()
+        ag.hand_on(i)
+        ag.issue(i + window)
+
+    settle(2, total, landing)
+    ag.issue(3)
+    landing = land(4, total)
+    settle(3, resid, landing_up)
     slots[0] = gain_ref[...]
     for made in gain_copies:
         made.wait_recv()
@@ -586,12 +624,14 @@
 
     def first_norm(i):
         at = rows(i, quarter)
-        x = x_ref[at, :].astype(f32)
+        x = tokens[at, :].astype(f32)
         cross_out[at, :] = (x * row_scale(x) * gains[0:1, :]).astype(bf16)
 
     loop(4, first_norm)
     take_normed = Gather(side, cross_out, all_normed, size)
     normed_copy = keep(cross_out, all_normed.at[pl.ds(0, size)])
+    settle(4, total, landing)
+    hand(0)
     length = length_ref[0]
     for made in dy_copies:
         made.wait()
@@ -605,18 +645,12 @@
     loop(4, mask)
     take_dyb = Gather(side, dyb_ref, all_dyb, size)
     dyb_copy = keep(dyb_ref, all_dyb.at[pl.ds(0, size)])
-    settle(2, total, landing)
-    landing = land(4, total)
-    ag.hand_on(0)
-    settle(3, resid, landing_up)
-    ag.issue(3)
+    hand(1)
     take_normed.forward()
-    ag.hand_on(1)
-    ag.issue(4)
-    settle(4, total, landing)
-    ag.hand_on(2)
-    ag.issue(5)
     take_dyb.forward()
+    hand(2)
+    take_dyb.done()
+    dyb_copy.wait()
     take_normed.done()
     normed_copy.wait()
     ag.arrived(0)
@@ -662,7 +696,9 @@
 
             loop(groups, head)
 
-        loop(pairs, pair)
+        hand(3)
+        for p in range(pairs):
+            pair(p)
         qkv_copy.wait()
 
     pl.run_scoped(
@@ -672,56 +708,77 @@
         pltpu.VMEM((span, HD), bf16),
         pltpu.VMEM((span, HD), bf16),
     )
-    ag.hand_on(3)
-    ag.issue(6)
     ag.arrived(2)
     fetch((full_out, weights.at[:, pl.ds(0, out_width)]))
     step = 512
 
-    def scatter(tile):
-        def to_core(n):
-            half_out[:, rows(n, step)] = tile(2 * size, 2 * size, n).astype(bf16)
-
-        loop(width // step, to_core)
-        core = side.copy(half_out, half_in, 0, 1)
-
-        def to_self(n):
-            total[:, rows(n, step)] = tile(0, size, n)
-
-        loop(width // step, to_self)
-        core.wait_recv()
-
-        def to_other(n):
-            at = rows(n, step)
-            part = tile(size, size, n) + half_in[pl.ds(size, size), at].astype(f32)
-            cross_out[:, at] = part.astype(bf16)
-
-        loop(width // step, to_other)
-        other = side.copy(cross_out, cross_in, 1, 0)
-        total[...] += half_in[pl.ds(0, size), :].astype(f32)
-        return other
+    class Scatter:
+        def __init__(self, tile):
+            self.tile = tile
+
+        def half(self):
+            flush()
+
+            def one(n):
+                half_out[:, rows(n, step)] = self.tile(2 * size, 2 * size, n).astype(bf16)
+
+            loop(width // step, one)
+            self.core = side.copy(half_out, half_in, 0, 1)
+
+        def own(self):
+            flush()
+
+            def one(n):
+                total[:, rows(n, step)] = self.tile(0, size, n)
+
+            loop(width // step, one)
+
+        def rest(self):
+            flush()
+            self.core.wait_recv()
+            side.drain()
+
+            def one(n):
+                at = rows(n, step)
+                part = self.tile(size, size, n) + half_in[pl.ds(size, size), at].astype(f32)
+                cross_out[:, at] = part.astype(bf16)
+
+            loop(width // step, one)
+            self.other = side.copy(cross_out, cross_in, 1, 0)
+
+            def add(i):
+                at = rows(i, quarter)
+                total[at, :] += half_in[at, :].astype(f32)
+
+            loop(4, add)
+
+        def done(self):
+            flush()
+            self.other.wait_recv()
 
     def out_tile(start, count, n):
         return dot_nt(ctx[pl.ds(start, count), :], weights[rows(n, step), pl.ds(0, out_width)])
 
-    side.drain()
-    other = scatter(out_tile)
-    other.wait_recv()
+    summed_out = Scatter(out_tile)
+    summed_out.half()
+    summed_out.own()
+    hand(4)
+    hand(5)
+    summed_out.rest()
+    summed_out.done()
 
     def second_norm(i):
         at = rows(i, quarter)
-        value = x_ref[at, :].astype(f32) + total[at, :] + cross_in[at, :].astype(f32)
+        value = tokens[at, :].astype(f32) + total[at, :] + cross_in[at, :].astype(f32)
         resid[at, :] = value
         mixed[at, :] = (value * row_scale(value) * gains[1:2, :]).astype(bf16)
 
     loop(4, second_norm)
     take_mixed = Gather(side, mixed.at[pl.ds(0, size)], mixed, size)
-    ag.hand_on(4)
-    ag.issue(7)
+    hand(6)
     take_mixed.forward()
-    ag.hand_on(5)
-    ag.issue(8)
     take_mixed.done()
+    hand(7)
     half = ff // 2
     tile = 256
 
@@ -751,32 +808,28 @@
             place.far(k, 0),
         )
 
-    order = (1, 3, 2, 0) if ag.near else tuple(range(1, steps)) + (0,)
-    waiting = []
-    turns = [0]
-
-    def flush():
-        while waiting:
-            waiting.pop(0)()
-
-    def send_away(g, left, right):
+    beside, beyond = 1 + 2 * ag.odd, 3 - 2 * ag.odd
+
+    def lean_over(g):
+        return remote(
+            part_of(away[g], beside),
+            aside[g - 3],
+            rxs.at[g, beside],
+            rxr.at[g, depth],
+            place.far(beside, 0),
+        )
+
+    def relay_over(g):
+        return remote(
+            part_of(home[g], beyond),
+            relay[g],
+            rzs.at[g, beyond],
+            rzr.at[g, 0],
+            place.far(depth - beyond, 0),
+        )
+
+    def add_to_stage(g, slot, src, made):
         wide_g = widths[g]
-        for t in order:
-            flush()
-            slot = turns[0] % 2
-            turns[0] += 1
-            at = (steps + t) * piece
-            stage[slot, :, 0:wide_g] = dot_tn(left[:, at : at + piece], right()).astype(bf16)
-            staged(g, slot, part_of(away[g], t)).start()
-
-            def finish(t=t, slot=slot):
-                staged(g, slot, part_of(away[g], t)).wait()
-                cross(g, t).start()
-
-            waiting.append(finish)
-
-    def add_to_stage(g, slot, src, made):
-        wide_g = full[g].shape[1]
         made.wait_recv()
         more = pltpu.make_async_copy(src, arrived_tile.at[:, pl.ds(0, wide_g)], tile_sem)
         more.start()
@@ -785,56 +838,106 @@
             stage[slot, :, 0:wide_g].astype(f32) + arrived_tile[:, 0:wide_g].astype(f32)
         ).astype(bf16)
 
-    def relay_over(g, k):
-        return remote(
-            part_of(home[g], k),
-            relay[g],
-            rzs.at[g, k],
-            rzr.at[g, 0],
-            place.far(depth - 1 if k == 1 else 1, 0),
-        )
-
-    def send_home(g, left, right, which=None):
-        wide_g = full[g].shape[1]
-        for t in order if which is None else which:
-            flush()
-            slot = turns[0] % 2
-            turns[0] += 1
+    operands = {}
+    turns = [0]
+    gone = {g: 0 for g in range(5)}
+    come_home = {g: 0 for g in range(5)}
+
+    def known(t, value):
+        return isinstance(t, int) and t == value
+
+    def product(g, t):
+        left, right = operands[g]
+        return dot_tn(left[:, rows(t, piece)], right())
+
+    def send(g, t, lean=False):
+        wide_g = widths[g]
+        made = product(g, steps + t)
+        flush()
+        slot = turns[0] % 2
+        turns[0] += 1
+        stage[slot, :, 0:wide_g] = made.astype(bf16)
+        if lean and known(t, 0):
+            add_to_stage(g, slot, aside[g - 3], lean_over(g))
+        staged(g, slot, part_of(away[g], t)).start()
+
+        def finish():
+            staged(g, slot, part_of(away[g], t)).wait()
+            if lean and t is beside:
+                lean_over(g).start()
+            else:
+                cross(g, t).start()
+
+        waiting.append(finish)
+
+    def take(g, t, bare=False):
+        wide_g = widths[g]
+        flush()
+        slot = turns[0] % 2
+        turns[0] += 1
+        if bare:
+            stage[slot, :, 0:wide_g] = product(g, t).astype(bf16)
+        else:
             cross(g, t).wait_recv()
             get = pltpu.make_async_copy(
                 part_of(got[g], t), arrived_tile.at[:, pl.ds(0, wide_g)], tile_sem
             )
             get.start()
-            made = dot_tn(left[:, t * piece : (t + 1) * piece], right())
+            made = product(g, t)
             get.wait()
             made = made + arrived_tile[:, 0:wide_g].astype(f32)
             stage[slot, :, 0:wide_g] = made.astype(bf16)
-            if ag.near and t == 2:
-
-                @pl.when((place.z == 1) | (place.z == 2))
-                def _():
-                    add_to_stage(g, slot, relay[g], relay_over(g, 1))
-
-            staged(g, slot, part_of(home[g], t)).start()
-
-            def finish(t=t, slot=slot):
-                staged(g, slot, part_of(home[g], t)).wait()
-                for r in range(held):
-                    k = t * held + r
-                    if ag.near and k in (1, 3):
-                        at_end = place.z == (3 if k == 1 else 0)
-
-                        @pl.when(at_end)
-                        def _():
-                            relay_over(g, k).start()
-
-                        @pl.when(jnp.logical_not(at_end))
-                        def _():
-                            hand_over(g, k).start()
-                    elif k:
-                        hand_over(g, k).start()
-
-            waiting.append(finish)
+        if ag.near and known(t, 2):
+
+            @pl.when((place.z == 1) | (place.z == 2))
+            def _():
+                add_to_stage(g, slot, relay[g], relay_over(g))
+
+        staged(g, slot, part_of(home[g], t)).start()
+
+        def finish():
+            staged(g, slot, part_of(home[g], t)).wait()
+            if ag.near:
+                if t is beyond:
+                    at_end = (place.z == 0) | (place.z == 3)
+
+                    @pl.when(at_end)
+                    def _():
+                        relay_over(g).start()
+
+                    @pl.when(jnp.logical_not(at_end))
+                    def _():
+                        hand_over(g, t).start()
+                elif not known(t, 0):
+                    hand_over(g, t).start()
+                return
+            for r in range(held):
+                if t * held + r:
+                    hand_over(g, t * held + r).start()
+
+        waiting.append(finish)
+
+    def away_step(g):
+        i = gone[g]
+        gone[g] += 1
+        if not ag.near:
+            for t in range(steps) if i == 0 else ():
+                send(g, t)
+            return
+        lean = g in (3, 4)
+        send(g, ((beside, beyond, 2, 0) if lean else (beyond, beside, 2, 0))[i], lean)
+
+    def home_step(g, which):
+        come_home[g] += 1
+        if not ag.near:
+            for t in tuple(range(1, steps)) + (0,) if come_home[g] == 4 else ():
+                take(g, t)
+            return
+        lean = g in (3, 4)
+        order = (beside, beyond, 2, 0) if lean else (beyond, beside, 2, 0)
+        take(g, order[which], lean and which == 0)
+
+    tokens_copy = keep(all_dyb, tokens)
 
     def feed_forward(gate, up):
         def feed(part):
@@ -864,17 +967,16 @@
         ag.arrived(3)
         ag.arrived(4)
         feed(0)
-        take_dyb.done()
-        dyb_copy.wait()
-        tokens_copy = keep(all_dyb, tokens)
-        ag.hand_on(6)
-        ag.hand_on(7)
+        hand(8)
         ag.arrived(5)
         ag.arrived(6)
         feed(1)
-        ag.hand_on(8)
         tokens_copy.wait()
-        send_away(4, tokens, lambda: hidden[...])
+        operands[4] = tokens, lambda: hidden[...]
+        away_step(4)
+        home_step(4, 0)
+        away_step(4)
+        away_step(4)
         flush()
         ag.arrived(7)
         ag.arrived(8)
@@ -901,6 +1003,13 @@
 
     pl.run_scoped(feed_forward, pltpu.VMEM((span, ff), f32), pltpu.VMEM((span, ff), f32))
 
+    operands[2] = mixed, lambda: feed_grad[:, pl.ds(0, ff)]
+    operands[3] = mixed, lambda: feed_grad[:, pl.ds(ff, ff)]
+    away_step(3)
+    away_step(2)
+    away_step(3)
+    flush()
+
     def mixed_grad(both):
         fetch(
             (full_gate, both.at[:, pl.ds(0, ff)]),
@@ -910,17 +1019,22 @@
         def mixed_tile(start, count, n):
             return dot_nt(feed_grad[pl.ds(start, count), :], both[rows(n, step), :])
 
-        side.drain()
-        scattered.append(scatter(mixed_tile))
-
-    scattered = []
+        summed.append(Scatter(mixed_tile))
+        summed[0].half()
+        summed[0].own()
+        summed[0].rest()
+
+    summed = []
     pl.run_scoped(mixed_grad, pltpu.VMEM((width, 2 * ff), bf16))
-    other = scattered[0]
-    send_away(2, mixed, lambda: feed_grad[:, pl.ds(0, ff)])
-    flush()
-    down_home = functools.partial(send_home, 4, tokens, lambda: hidden[...])
-    down_home(order[:1])
-    other.wait_recv()
+    home_step(4, 1)
+    home_step(2, 0)
+    home_step(4, 2)
+    away_step(2)
+    away_step(4)
+    away_step(2)
+    home_step(3, 1)
+    away_step(2)
+    summed[0].done()
     sums[...] = jnp.zeros_like(sums)
     head_sums[...] = jnp.zeros_like(head_sums)
 
@@ -940,14 +1054,24 @@
     loop(4, second_back)
     take_dresb = Gather(side, cross_out, all_dresb, size)
     dresb_copy = keep(cross_out, all_dresb.at[pl.ds(0, size)])
-    send_away(3, mixed, lambda: feed_grad[:, pl.ds(ff, ff)])
+    take_dresb.core.wait_recv()
+    away_step(3)
+
+    def down_tile(start, count, n):
+        return dot_nt(hidden[pl.ds(start, count), :], weights[rows(n, step), :])
+
+    summed_down = Scatter(down_tile)
+    summed_down.half()
+    home_step(2, 1)
+    summed_down.own()
+    home_step(4, 3)
+    home_step(3, 0)
     flush()
-    down_home(order[1:2])
     take_dresb.forward()
-    down_home(order[2:])
-    flush()
-    take_dresb.done()
     dresb_copy.wait()
+    summed_down.rest()
+    pl.semaphore_signal(free_core, inc=1, device_id=place.side(0, 1), device_id_type=MESH)
+    take_dresb.last.wait_recv()
 
     def attention_back(qkv_grad, qkv, k_act, v_act, ctx_grad, k_grad, v_grad):
         fetch(
@@ -955,6 +1079,8 @@
             (all_qkv, qkv),
             (full_out, weights.at[:, pl.ds(0, out_width)]),
         )
+
+        operands[1] = tokens, lambda: ctx[...]
 
         def context_grad(m):
             ctx_grad[rows(m, size), :] = dot_nn(
@@ -1010,20 +1136,36 @@
                 column = pl.ds(pl.multiple_of((heads + pairs + p) * HD, HD), HD)
                 qkv_grad[at, column] = v_grad[to, :].astype(bf16)
 
-        loop(pairs, pair)
+        pair(0)
+        home_step(2, 2)
+        away_step(1)
+        flush()
+        summed_down.done()
+        side.drain()
+
+        def last_sum(i):
+            at = rows(i, quarter)
+            value = resid[at, :] + total[at, :] + cross_in[at, :].astype(f32)
+            cross_out[at, :] = value.astype(bf16)
+
+        loop(4, last_sum)
+        results.extend(in_order(o_out, cross_out, out=True))
+        pl.semaphore_signal(free_other, inc=1, device_id=place.side(1, 0), device_id_type=MESH)
+        for p in range(1, pairs):
+            pair(p)
+        for made in results:
+            made.wait()
+
+    results = []
 
     def finish_back(qkv_grad, normed, come_v, home_v, sum_v, sum_t):
         normed_copy = keep(all_normed, normed)
         qkv_copy = keep(full_qkv, weights.at[:, pl.ds(0, qkv_width)])
-        send_away(1, tokens, lambda: ctx[...])
+        operands[0] = normed, lambda: qkv_grad[...]
         normed_copy.wait()
-        send_away(0, normed, lambda: qkv_grad[...])
-        flush()
-        gate_home = functools.partial(send_home, 2, mixed, lambda: feed_grad[:, pl.ds(0, ff)])
-        up_home = functools.partial(send_home, 3, mixed, lambda: feed_grad[:, pl.ds(ff, ff)])
-        out_home = functools.partial(send_home, 1, tokens, lambda: ctx[...])
-        qkv_home = functools.partial(send_home, 0, normed, lambda: qkv_grad[...])
-        gate_home(order[:-1])
+        away_step(0)
+        away_step(0)
+        away_step(1)
         flush()
         qkv_copy.wait()
         written = []
@@ -1087,17 +1229,32 @@
                 qkv_grad[pl.ds(start, count), :], weights[rows(n, step), pl.ds(0, qkv_width)]
             )
 
-        side.drain()
-        other = scatter(normed_tile)
+        summed_normed = Scatter(normed_tile)
+        pl.semaphore_wait(free_core, 1)
+        summed_normed.half()
+        home_step(1, 0)
+        summed_normed.own()
+        home_step(3, 2)
+        pl.semaphore_wait(free_other, 1)
+        summed_normed.rest()
+        x_again = in_order(x_in, half_out.at[pl.ds(0, size)])
+        home_step(2, 3)
+        away_step(0)
+        away_step(1)
         finals(4)
-        gate_home(order[-1:])
-        up_home(order[:1])
-        flush()
-        other.wait_recv()
+        away_step(1)
+        home_step(0, 1)
+        finals(2)
+        home_step(1, 1)
+        away_step(3)
+        home_step(0, 0)
+        summed_normed.done()
+        for made in x_again:
+            made.wait()
 
         def first_back(i):
             at = rows(i, quarter)
-            value = x_ref[at, :].astype(f32)
+            value = half_out[at, :].astype(f32)
             scale = row_scale(value)
             unit = value * scale
             grad = total[at, :] + cross_in[at, :].astype(f32)
@@ -1105,17 +1262,30 @@
             grad_own[at, :] += norm_back(grad, unit, scale, gains[0:1, :])
 
         loop(4, first_back)
-        pl.semaphore_signal(free_core, inc=1, device_id=place.side(0, 1), device_id_type=MESH)
-        pl.semaphore_signal(free_other, inc=1, device_id=place.side(1, 0), device_id_type=MESH)
-
-        for flip, (dy, dc) in enumerate(((0, 1), (1, 0))):
-            norm_made = side.copy(sums, sums_in.at[flip], dy, dc)
-            head_made = side.copy(head_sums, head_sums_in.at[flip], dy, dc)
-            norm_made.wait_recv()
-            head_made.wait_recv()
+        grads = in_order(o_grad, grad_own, out=True)
+
+        def trade(flip, dy, dc):
+            return (
+                side.copy(sums, sums_in.at[flip], dy, dc),
+                side.copy(head_sums, head_sums_in.at[flip], dy, dc),
+            )
+
+        def add_trade(flip, made):
+            flush()
+            for one in made:
+                one.wait_recv()
             side.drain()
             sums[...] += sums_in[flip]
             head_sums[...] += head_sums_in[flip]
+
+        made = trade(0, 0, 1)
+        home_step(1, 2)
+        add_trade(0, made)
+        made = trade(1, 1, 0)
+        home_step(1, 3)
+        away_step(0)
+        home_step(0, 2)
+        add_trade(1, made)
         for made in gain_copies:
             made.wait_send()
         for b in range(wide):
@@ -1140,30 +1310,12 @@
                     )
                     made.start()
                     last.append(made)
-        up_home(order[1:-1])
-        fetch((full_down, weights))
-
-        def down_tile(start, count, n):
-            return dot_nt(hidden[pl.ds(start, count), :], weights[rows(n, step), :])
-
-        pl.semaphore_wait(free_core, 1)
-        pl.semaphore_wait(free_other, 1)
-        other = scatter(down_tile)
-        grads = in_order(o_grad, grad_own, out=True)
-        finals(2)
-        up_home(order[-1:])
-        flush()
-        other.wait_recv()
-        side.drain()
-        cross_out[...] = (resid[...] + total[...] + cross_in[...].astype(f32)).astype(bf16)
-        results = in_order(o_out, cross_out, out=True)
-        out_home(None)
-        qkv_home(order[:-1])
+        home_step(3, 3)
         finals(3)
         finals(1)
-        qkv_home(order[-1:])
+        home_step(0, 3)
         finals(0)
-        for made in grads + results + written:
+        for made in grads + written:
             made.wait()
         for made in last:
             made.wait_recv()
@@ -1238,6 +1390,7 @@
     outs += [shape((width, w), bf16) for w in widths]
     outs += [shape((width // 2, w), bf16) for w in widths] * 2
     outs += [shape((block, w), bf16) for w in widths]
+    outs += [shape((block, w), bf16) for w in widths[3:]]
     outs += [
         shape((span, width), bf16),
         shape((span, width), bf16),
@@ -1262,7 +1415,6 @@
         in_specs=[smem] + [vmem] * 4 + [anywhere] * 7,
         out_specs=[vmem] * 2 + [anywhere] * (len(outs) - 2),
         scratch_shapes=[
-            pltpu.VMEM((size, width), bf16),
             pltpu.VMEM((size, width), bf16),
             pltpu.VMEM((size, width), f32),
             pltpu.VMEM((8, lanes), f32),
@@ -1299,7 +1451,7 @@
             dma((2 * wide,)),
             dma((160,)),
             dma((5, depth)),
-            dma((5, depth)),
+            dma((5, depth + 1)),
             dma((5, depth)),
             dma((5, depth)),
             dma((2,)),

time: 626 us -> 575 us (0.919)
  Pallas kernels: 591 us -> 541 us
    pallas_call x1, Pallas kernels: 591 us -> 541 us  [layer_call(): pl.pallas_call(functools.partial(layer_kernel, wide, heads, pairs), out_s...]
where the time goes in v4:
time: 575 us; the launch traced here: 565 us
  Pallas kernels  541 us (94%)
  other arithmetic  18.3 us (3%)
    pallas_call x1, Pallas kernels, layer_call(): pl.pallas_call(functools.partial(layer_kernel, wide, heads, pairs), out_s...  541 us
    sub x7, other arithmetic, adamw(): weight - rate * (first_hat / (jnp.sqrt(second_hat) + adam_eps) + weight_d...  18.3 us

profile of v4, /device:TPU:1, one launch (start us, length us, event | category | flops | bytes accessed | tf_op | source)
XLA Modules:
  0.0 564.9 jit_solution(3562752810326088035)
XLA Ops:
  1.3 0.0 copy-start.19
  1.3 0.0 copy-start.22
  1.3 0.0 copy-start.23
  1.3 540.6 %shard_map.425 = (f32[8,256]{1,0:T(8,128)}, f32[8,128]{1,0:T(8,128)}, bf16[256,2048]{1,0:T(8,128)(2,1)}, f32[256,2048]{1,0:T(8,128)}, f32[256,512]{1,0:T(8,128)}...) custom-call(s32[1]{0:T(128)S(6)} %copy.51.length_ref, ...), custom_call_target="tpu_custom_call" | custom-call | tf_op jit(solution)/shard_map/pallas_call | solution.py:1412
  542.0 0.0 copy-done.19
  542.0 0.0 copy-done.22
  542.0 0.0 copy-done.23
  542.0 1.3 multiply_subtract_fusion.6
  543.3 8.4 %multiply_subtract_fusion = (f32[2,256,1536]{2,1,0:T(8,128)}, f32[2,256,1536]{2,1,0:T(8,128)}, f32[2,256,1536]{2,1,0:T(8,128)}) fusion(f32[2,256,1536]{2,1,0:T(8,128)} %w_gateup.1, f32[2,256,1536]{2,1,0:T(8,128)} %get-tuple-element.37, f32[2,256,1536]{2,1,0:T(8,128)} %param.39, f32[2,256,1536]{2,1,0:T(8,128)} %param.40), kind=kLoop, calls=%fused_computation.3 | loop fusion | flops 11010048 | bytes 22020096 | tf_op jit(solution)/shard_map/sub | solution.py:41
  551.7 0.0 copy-done
  551.8 0.9 copy-done.6
  552.6 0.5 copy-done.7
  553.1 3.0 multiply_subtract_fusion.1
  556.2 0.0 copy-start.3
  556.2 0.0 copy-start.13
  556.2 0.0 copy-start.14
  556.2 1.4 multiply_subtract_fusion.4
  557.7 0.2 copy-done.12
  557.9 0.3 copy-done.16
  558.2 1.4 multiply_subtract_fusion.3
  559.7 1.4 multiply_subtract_fusion.2
  561.1 1.3 multiply_subtract_fusion.5
  562.4 1.0 copy.52
  563.4 1.3 copy.53
  (34 shorter events, 0.1 us)
Async XLA Ops:
  1.3 540.7 %copy-start.19 = (f32[2,16]{1,0:T(2,128)S(1)}, f32[2,16]{1,0:T(2,128)}, u32[]{:S(2)}) copy-start(f32[2,16]{1,0:T(2,128)} %head_ref.1) | copy-start | bytes 388
  1.3 540.7 %copy-start.22 = (f32[2,16]{1,0:T(2,128)S(1)}, f32[2,16]{1,0:T(2,128)}, u32[]{:S(2)}) copy-start(f32[2,16]{1,0:T(2,128)} %param.48) | copy-start | bytes 388
  1.3 540.7 %copy-start.23 = (f32[2,16]{1,0:T(2,128)S(1)}, f32[2,16]{1,0:T(2,128)}, u32[]{:S(2)}) copy-start(f32[2,16]{1,0:T(2,128)} %param.49) | copy-start | bytes 388
  543.3 8.4 %copy-start = (f32[1536,256]{1,0:T(8,128)S(1)}, f32[1536,256]{1,0:T(8,128)}, u32[]{:S(2)}) copy-start(f32[1536,256]{1,0:T(8,128)} %w_down.1) | copy-start | bytes 4718596
  543.3 8.4 %copy-start.5 = (f32[1536,256]{1,0:T(8,128)S(1)}, f32[1536,256]{1,0:T(8,128)}, u32[]{:S(2)}) copy-start(f32[1536,256]{1,0:T(8,128)} %param.42) | copy-start | bytes 4718596
  543.3 9.3 %copy-start.6 = (f32[1536,256]{1,0:T(8,128)S(1)}, f32[1536,256]{1,0:T(8,128)}, u32[]{:S(2)}) copy-start(f32[1536,256]{1,0:T(8,128)} %param.43) | copy-start | bytes 4718596
  543.3 9.8 %copy-start.7 = (f32[1536,256]{1,0:T(8,128)S(1)}, f32[1536,256]{1,0:T(8,128)}, u32[]{:S(2)}) copy-start(f32[1536,256]{1,0:T(8,128)} %get-tuple-element.38) | copy-start | bytes 4718596
  553.1 3.1 copy-start.1
  553.1 3.1 copy-start.9
  553.1 3.1 copy-start.10
  553.1 3.1 copy-start.17
  556.1 1.5 copy-start.2
  556.1 1.5 copy-start.11
  556.2 1.8 copy-start.12
  556.2 2.1 copy-start.16
  556.2 3.5 copy-start.3
  556.2 3.5 copy-start.13
  556.2 3.4 copy-start.14
  556.2 3.4 copy-start.15
  558.2 2.9 copy-start.18
  558.2 2.9 copy-start.20
  558.2 2.9 copy-start.21
  558.2 4.2 copy-start.8
  559.7 3.7 copy-start.4

commit v5 on v4

--- a/solution.py
+++ b/solution.py
@@ -434,8 +434,7 @@
     relay_gate,
     relay_up,
     relay_down,
-    aside_up,
-    aside_down,
+    aside,
     all_dyb,
     all_normed,
     all_qkv,
@@ -481,6 +480,7 @@
     rzr,
     stage_sem,
     tile_sem,
+    come_sem,
     free_core,
     free_other,
 ):
@@ -498,7 +498,6 @@
     home = [home_qkv, home_out, home_gate, home_up, home_down]
     come = [come_qkv, come_out, come_gate, come_up, come_down]
     relay = [relay_qkv, relay_out, relay_gate, relay_up, relay_down]
-    aside = [aside_up, aside_down]
     widths = [ref.shape[1] for ref in full]
     qkv_width, out_width = widths[0], widths[1]
     chunks = chunks_of(widths)
@@ -600,7 +599,7 @@
     settle(1, resid, landing_out)
     ag.issue(2)
     landing_up = land(3, resid)
-    window = 4
+    window = 3
 
     def hand(i):
         flush()
@@ -608,7 +607,6 @@
         ag.issue(i + window)
 
     settle(2, total, landing)
-    ag.issue(3)
     landing = land(4, total)
     settle(3, resid, landing_up)
     slots[0] = gain_ref[...]
@@ -813,7 +811,7 @@
     def lean_over(g):
         return remote(
             part_of(away[g], beside),
-            aside[g - 3],
+            aside,
             rxs.at[g, beside],
             rxr.at[g, depth],
             place.far(beside, 0),
@@ -858,7 +856,7 @@
         turns[0] += 1
         stage[slot, :, 0:wide_g] = made.astype(bf16)
         if lean and known(t, 0):
-            add_to_stage(g, slot, aside[g - 3], lean_over(g))
+            add_to_stage(g, slot, aside, lean_over(g))
         staged(g, slot, part_of(away[g], t)).start()
 
         def finish():
@@ -870,20 +868,27 @@
 
         waiting.append(finish)
 
+    late = []
+    in_stage = []
+
     def take(g, t, bare=False):
         wide_g = widths[g]
-        flush()
         slot = turns[0] % 2
         turns[0] += 1
         if bare:
-            stage[slot, :, 0:wide_g] = product(g, t).astype(bf16)
+            made = product(g, t)
+            flush()
+            stage[slot, :, 0:wide_g] = made.astype(bf16)
         else:
+            if not late:
+                flush()
             cross(g, t).wait_recv()
             get = pltpu.make_async_copy(
                 part_of(got[g], t), arrived_tile.at[:, pl.ds(0, wide_g)], tile_sem
             )
             get.start()
             made = product(g, t)
+            flush()
             get.wait()
             made = made + arrived_tile[:, 0:wide_g].astype(f32)
             stage[slot, :, 0:wide_g] = made.astype(bf16)
@@ -893,6 +898,9 @@
             def _():
                 add_to_stage(g, slot, relay[g], relay_over(g))
 
+        if ag.near and g == 0 and known(t, 0):
+            in_stage.append(slot)
+            return
         staged(g, slot, part_of(home[g], t)).start()
 
         def finish():
@@ -924,7 +932,7 @@
             for t in range(steps) if i == 0 else ():
                 send(g, t)
             return
-        lean = g in (3, 4)
+        lean = g == 4
         send(g, ((beside, beyond, 2, 0) if lean else (beyond, beside, 2, 0))[i], lean)
 
     def home_step(g, which):
@@ -933,7 +941,7 @@
             for t in tuple(range(1, steps)) + (0,) if come_home[g] == 4 else ():
                 take(g, t)
             return
-        lean = g in (3, 4)
+        lean = g == 4
         order = (beside, beyond, 2, 0) if lean else (beyond, beside, 2, 0)
         take(g, order[which], lean and which == 0)
 
@@ -1072,6 +1080,8 @@
     summed_down.rest()
     pl.semaphore_signal(free_core, inc=1, device_id=place.side(0, 1), device_id_type=MESH)
     take_dresb.last.wait_recv()
+
+    late.append(True)
 
     def attention_back(qkv_grad, qkv, k_act, v_act, ctx_grad, k_grad, v_grad):
         fetch(
@@ -1173,34 +1183,45 @@
         def finals(g):
             flush()
             wide_g = widths[g]
-            mine = keep(home[g].at[pl.ds(0, block)], home_v.at[:, pl.ds(0, wide_g)])
-            for k in range(1, depth):
-                at = pl.ds((k - 1) * block, block)
-
-                def bring(g=g, k=k, at=at):
-                    hand_over(g, k).wait_recv()
-                    made = pltpu.make_async_copy(
-                        come[g].at[at], come_v.at[at, pl.ds(0, wide_g)], tile_sem
-                    )
-                    made.start()
-                    made.wait()
-
-                if ag.near and k in (1, 3):
-                    here = place.z != (0 if k == 1 else 3)
-                    pl.when(here)(bring)
-
-                    @pl.when(jnp.logical_not(here))
-                    def _(at=at):
-                        come_v[at, 0:wide_g] = jnp.zeros((block, wide_g), bf16)
-                else:
-                    bring()
-            mine.wait()
+            kept = in_stage if g == 0 else []
+            if not kept:
+                mine = keep(home[g].at[pl.ds(0, block)], home_v.at[:, pl.ds(0, wide_g)])
+
+            def slot_of(k):
+                return pl.ds((k - 1) * block, block)
+
+            def bring(k):
+                return pltpu.make_async_copy(
+                    come[g].at[slot_of(k)], come_v.at[slot_of(k), pl.ds(0, wide_g)], come_sem.at[k]
+                )
+
+            def begin(k):
+                hand_over(g, k).wait_recv()
+                bring(k).start()
+
+            def none(k):
+                come_v[slot_of(k), 0:wide_g] = jnp.zeros((block, wide_g), bf16)
+
+            for act, other in ((begin, none), (lambda k: bring(k).wait(), None)):
+                for k in (1, 3, 2) if ag.near else range(1, depth):
+                    if ag.near and k in (1, 3):
+                        here = place.z != (0 if k == 1 else 3)
+                        pl.when(here)(functools.partial(act, k))
+                        if other is not None:
+                            pl.when(jnp.logical_not(here))(functools.partial(other, k))
+                    else:
+                        act(k)
+            if not kept:
+                mine.wait()
             while written:
                 written.pop().wait()
 
             def add(i):
                 at = rows(i, block // 4)
-                value = home_v[at, 0:wide_g].astype(f32)
+                if kept:
+                    value = stage[kept[0], at, 0:wide_g].astype(f32)
+                else:
+                    value = home_v[at, 0:wide_g].astype(f32)
                 for k in range(1, depth):
                     more = pl.ds(
                         pl.multiple_of((k - 1) * block + i * (block // 4), block // 4), block // 4
@@ -1390,7 +1411,7 @@
     outs += [shape((width, w), bf16) for w in widths]
     outs += [shape((width // 2, w), bf16) for w in widths] * 2
     outs += [shape((block, w), bf16) for w in widths]
-    outs += [shape((block, w), bf16) for w in widths[3:]]
+    outs += [shape((block, ff), bf16)]
     outs += [
         shape((span, width), bf16),
         shape((span, width), bf16),
@@ -1456,6 +1477,7 @@
             dma((5, depth)),
             dma((2,)),
             dma,
+            dma((depth,)),
             pltpu.SemaphoreType.REGULAR,
             pltpu.SemaphoreType.REGULAR,
         ],

time: 575 us -> 559 us (0.972)
  Pallas kernels: 541 us -> 526 us
    pallas_call x1, Pallas kernels: 541 us -> 526 us  [layer_call(): pl.pallas_call(functools.partial(layer_kernel, wide, heads, pairs), out_s...]
where the time goes in v5:
time: 559 us; the launch traced here: 551 us
  Pallas kernels  526 us (94%)
  other arithmetic  18.3 us (3%)
    pallas_call x1, Pallas kernels, layer_call(): pl.pallas_call(functools.partial(layer_kernel, wide, heads, pairs), out_s...  526 us
    sub x7, other arithmetic, adamw(): weight - rate * (first_hat / (jnp.sqrt(second_hat) + adam_eps) + weight_d...  18.3 us

profile of v5, /device:TPU:1, one launch (start us, length us, event | category | flops | bytes accessed | tf_op | source)
XLA Modules:
  0.0 550.6 jit_solution(821785219283911336)
XLA Ops:
  1.3 0.0 copy-start.19
  1.3 0.0 copy-start.22
  1.3 0.0 copy-start.23
  1.3 526.3 %shard_map.425 = (f32[8,256]{1,0:T(8,128)}, f32[8,128]{1,0:T(8,128)}, bf16[256,2048]{1,0:T(8,128)(2,1)}, f32[256,2048]{1,0:T(8,128)}, f32[256,512]{1,0:T(8,128)}...) custom-call(s32[1]{0:T(128)S(6)} %copy.51.length_ref, ...), custom_call_target="tpu_custom_call" | custom-call | tf_op jit(solution)/shard_map/pallas_call | solution.py:1433
  527.7 0.0 copy-done.19
  527.7 1.3 multiply_subtract_fusion.6
  529.0 8.4 %multiply_subtract_fusion = (f32[2,256,1536]{2,1,0:T(8,128)}, f32[2,256,1536]{2,1,0:T(8,128)}, f32[2,256,1536]{2,1,0:T(8,128)}) fusion(f32[2,256,1536]{2,1,0:T(8,128)} %w_gateup.1, f32[2,256,1536]{2,1,0:T(8,128)} %get-tuple-element.37, f32[2,256,1536]{2,1,0:T(8,128)} %param.39, f32[2,256,1536]{2,1,0:T(8,128)} %param.40), kind=kLoop, calls=%fused_computation.3 | loop fusion | flops 11010048 | bytes 22020096 | tf_op jit(solution)/shard_map/sub | solution.py:41
  537.5 0.0 copy-done
  537.5 0.9 copy-done.6
  538.3 0.5 copy-done.7
  538.8 3.0 multiply_subtract_fusion.1
  541.9 0.0 copy-start.3
  541.9 0.0 copy-start.13
  541.9 0.0 copy-start.14
  541.9 1.4 multiply_subtract_fusion.4
  543.4 0.0 copy-done.11
  543.4 0.2 copy-done.12
  543.6 0.3 copy-done.16
  543.9 1.4 multiply_subtract_fusion.3
  545.4 0.0 copy-done.13
  545.4 1.4 multiply_subtract_fusion.2
  546.8 1.3 multiply_subtract_fusion.5
  548.1 1.0 copy.52
  549.1 1.3 copy.53
  (34 shorter events, 0.1 us)
Async XLA Ops:
  1.3 526.4 %copy-start.19 = (f32[2,16]{1,0:T(2,128)S(1)}, f32[2,16]{1,0:T(2,128)}, u32[]{:S(2)}) copy-start(f32[2,16]{1,0:T(2,128)} %head_ref.1) | copy-start | bytes 388
  1.3 526.4 %copy-start.22 = (f32[2,16]{1,0:T(2,128)S(1)}, f32[2,16]{1,0:T(2,128)}, u32[]{:S(2)}) copy-start(f32[2,16]{1,0:T(2,128)} %param.48) | copy-start | bytes 388
  1.3 526.4 %copy-start.23 = (f32[2,16]{1,0:T(2,128)S(1)}, f32[2,16]{1,0:T(2,128)}, u32[]{:S(2)}) copy-start(f32[2,16]{1,0:T(2,128)} %param.49) | copy-start | bytes 388
  529.0 8.4 %copy-start = (f32[1536,256]{1,0:T(8,128)S(1)}, f32[1536,256]{1,0:T(8,128)}, u32[]{:S(2)}) copy-start(f32[1536,256]{1,0:T(8,128)} %w_down.1) | copy-start | bytes 4718596
  529.0 8.4 %copy-start.5 = (f32[1536,256]{1,0:T(8,128)S(1)}, f32[1536,256]{1,0:T(8,128)}, u32[]{:S(2)}) copy-start(f32[1536,256]{1,0:T(8,128)} %param.42) | copy-start | bytes 4718596
  529.0 9.3 %copy-start.6 = (f32[1536,256]{1,0:T(8,128)S(1)}, f32[1536,256]{1,0:T(8,128)}, u32[]{:S(2)}) copy-start(f32[1536,256]{1,0:T(8,128)} %param.43) | copy-start | bytes 4718596
  529.0 9.8 %copy-start.7 = (f32[1536,256]{1,0:T(8,128)S(1)}, f32[1536,256]{1,0:T(8,128)}, u32[]{:S(2)}) copy-start(f32[1536,256]{1,0:T(8,128)} %get-tuple-element.38) | copy-start | bytes 4718596
  538.8 3.1 copy-start.1
  538.8 3.1 copy-start.9
  538.8 3.1 copy-start.10
  538.8 3.1 copy-start.17
  541.9 1.5 copy-start.2
  541.9 1.5 copy-start.11
  541.9 1.8 copy-start.12
  541.9 2.1 copy-start.16
  541.9 3.5 copy-start.3
  541.9 3.5 copy-start.13
  541.9 3.4 copy-start.14
  541.9 3.4 copy-start.15
  543.9 2.9 copy-start.18
  543.9 2.9 copy-start.20
  543.9 2.9 copy-start.21
  543.9 4.2 copy-start.8
  545.4 3.7 copy-start.4

commit v6 on v5

--- a/solution.py
+++ b/solution.py
@@ -307,14 +307,20 @@
                 self.across(i, k).wait_send()
 
 
-def greet(place):
+def peers_of(place):
     depth = place.depth
     peers = [place.far(k, dx) for dx in (0, 1) for k in range(depth) if k or dx]
-    peers += [place.side(1, 0), place.side(0, 1)]
+    return peers + [place.side(1, 0), place.side(0, 1)]
+
+
+def greet(place):
     barrier = pltpu.get_barrier_semaphore()
-    for peer in peers:
+    for peer in peers_of(place):
         pl.semaphore_signal(barrier, inc=1, device_id=peer, device_id_type=MESH)
-    pl.semaphore_wait(barrier, len(peers))
+
+
+def await_greetings(place):
+    pl.semaphore_wait(pltpu.get_barrier_semaphore(), len(peers_of(place)))
 
 
 def turn(values):
@@ -571,10 +577,10 @@
             waiting.pop(0)()
 
     landing = land(0, total)
+    greet(place)
+    landing_out = land(1, resid)
     x_copies = in_order(x_in, tokens.at[pl.ds(0, size)])
-    landing_out = land(1, resid)
     dy_copies = in_order(dy_in, dyb_ref)
-
     part = head_ref.shape[1]
     gain_ref[...] = jnp.zeros_like(gain_ref)
     gain_ref[0:2, 0:part] = head_ref[...]
@@ -582,7 +588,8 @@
     gain_ref[:, 0:HD] = pltpu.roll(spread, 2, 0)
     gain_ref[0:2, 0:block] = norm_ref[...]
     gain_ref[...] = gain_ref[...].astype(bf16).astype(f32)
-    greet(place)
+
+    await_greetings(place)
 
     gain_copies = []
     for dx in (0, 1):
@@ -982,9 +989,9 @@
         tokens_copy.wait()
         operands[4] = tokens, lambda: hidden[...]
         away_step(4)
-        home_step(4, 0)
         away_step(4)
         away_step(4)
+        home_step(4, 0)
         flush()
         ag.arrived(7)
         ag.arrived(8)

time: 559 us -> 558 us (level)
  no operation moved by 1% of the time
where the time goes in v6:
time: 558 us; the launch traced here: 549 us
  Pallas kernels  525 us (94%)
  other arithmetic  18.3 us (3%)
    pallas_call x1, Pallas kernels, layer_call(): pl.pallas_call(functools.partial(layer_kernel, wide, heads, pairs), out_s...  525 us
    sub x7, other arithmetic, adamw(): weight - rate * (first_hat / (jnp.sqrt(second_hat) + adam_eps) + weight_d...  18.3 us

profile of v6, /device:TPU:1, one launch (start us, length us, event | category | flops | bytes accessed | tf_op | source)
XLA Modules:
  0.0 549.0 jit_solution(13898300885124062177)
XLA Ops:
  1.3 0.0 copy-start.19
  1.3 0.0 copy-start.22
  1.3 0.0 copy-start.23
  1.3 524.7 %shard_map.425 = (f32[8,256]{1,0:T(8,128)}, f32[8,128]{1,0:T(8,128)}, bf16[256,2048]{1,0:T(8,128)(2,1)}, f32[256,2048]{1,0:T(8,128)}, f32[256,512]{1,0:T(8,128)}...) custom-call(s32[1]{0:T(128)S(6)} %copy.51.length_ref, ...), custom_call_target="tpu_custom_call" | custom-call | tf_op jit(solution)/shard_map/pallas_call | solution.py:1440
  526.1 1.3 multiply_subtract_fusion.6
  527.4 8.4 %multiply_subtract_fusion = (f32[2,256,1536]{2,1,0:T(8,128)}, f32[2,256,1536]{2,1,0:T(8,128)}, f32[2,256,1536]{2,1,0:T(8,128)}) fusion(f32[2,256,1536]{2,1,0:T(8,128)} %w_gateup.1, f32[2,256,1536]{2,1,0:T(8,128)} %get-tuple-element.37, f32[2,256,1536]{2,1,0:T(8,128)} %param.39, f32[2,256,1536]{2,1,0:T(8,128)} %param.40), kind=kLoop, calls=%fused_computation.3 | loop fusion | flops 11010048 | bytes 22020096 | tf_op jit(solution)/shard_map/sub | solution.py:41
  535.8 0.9 copy-done.6
  536.7 0.5 copy-done.7
  537.2 3.0 multiply_subtract_fusion.1
  540.3 0.0 copy-start.3
  540.3 0.0 copy-start.13
  540.3 0.0 copy-start.14
  540.3 0.0 copy-start.15
  540.3 1.4 multiply_subtract_fusion.4
  541.8 0.0 copy-done.2
  541.8 0.2 copy-done.12
  542.0 0.3 copy-done.16
  542.3 1.4 multiply_subtract_fusion.3
  543.8 1.4 multiply_subtract_fusion.2
  545.2 0.0 copy-done.20
  545.2 1.3 multiply_subtract_fusion.5
  546.5 1.0 copy.52
  547.5 0.0 copy-done.4
  547.5 1.3 copy.53
  (34 shorter events, 0.1 us)
Async XLA Ops:
  1.3 524.7 %copy-start.19 = (f32[2,16]{1,0:T(2,128)S(1)}, f32[2,16]{1,0:T(2,128)}, u32[]{:S(2)}) copy-start(f32[2,16]{1,0:T(2,128)} %head_ref.1) | copy-start | bytes 388
  1.3 524.7 %copy-start.22 = (f32[2,16]{1,0:T(2,128)S(1)}, f32[2,16]{1,0:T(2,128)}, u32[]{:S(2)}) copy-start(f32[2,16]{1,0:T(2,128)} %param.48) | copy-start | bytes 388
  1.3 524.7 %copy-start.23 = (f32[2,16]{1,0:T(2,128)S(1)}, f32[2,16]{1,0:T(2,128)}, u32[]{:S(2)}) copy-start(f32[2,16]{1,0:T(2,128)} %param.49) | copy-start | bytes 388
  527.4 8.4 %copy-start = (f32[1536,256]{1,0:T(8,128)S(1)}, f32[1536,256]{1,0:T(8,128)}, u32[]{:S(2)}) copy-start(f32[1536,256]{1,0:T(8,128)} %w_down.1) | copy-start | bytes 4718596
  527.4 8.4 %copy-start.5 = (f32[1536,256]{1,0:T(8,128)S(1)}, f32[1536,256]{1,0:T(8,128)}, u32[]{:S(2)}) copy-start(f32[1536,256]{1,0:T(8,128)} %param.42) | copy-start | bytes 4718596
  527.4 9.3 %copy-start.6 = (f32[1536,256]{1,0:T(8,128)S(1)}, f32[1536,256]{1,0:T(8,128)}, u32[]{:S(2)}) copy-start(f32[1536,256]{1,0:T(8,128)} %param.43) | copy-start | bytes 4718596
  527.4 9.8 %copy-start.7 = (f32[1536,256]{1,0:T(8,128)S(1)}, f32[1536,256]{1,0:T(8,128)}, u32[]{:S(2)}) copy-start(f32[1536,256]{1,0:T(8,128)} %get-tuple-element.38) | copy-start | bytes 4718596
  537.2 3.1 copy-start.1
  537.2 3.1 copy-start.9
  537.2 3.1 copy-start.10
  537.2 3.1 copy-start.17
  540.2 1.5 copy-start.2
  540.2 1.5 copy-start.11
  540.2 1.8 copy-start.12
  540.2 2.1 copy-start.16
  540.3 3.5 copy-start.3
  540.3 3.5 copy-start.13
  540.3 3.4 copy-start.14
  540.3 3.4 copy-start.15
  542.3 2.9 copy-start.18
  542.3 2.9 copy-start.20
  542.3 2.9 copy-start.21
  542.3 4.2 copy-start.8
  543.7 3.7 copy-start.4
